TPU v7x, 32 devices: a whole 2x2x4 slice. The times are simulated.
32 devices in a mesh: stream: 4 (over z), tm: 8 (over y, x, core).
Axes of the slice: x: 2, y: 2, z: 4, core: 2. Of those that a mesh axis runs over, the one named last changes fastest.
Arguments:
- frames: bfloat16 [4, 1024, 512], P('stream', 'tm'), may hold values from -6 to 6
- lengths: int32 [4, 5], P('stream'), may hold values from 1 to 896, as said below
- cotangent: bfloat16 [4, 1024, 512], P('stream', 'tm'), may hold values from -6 to 6
- ln_attn_gain: bfloat16 [512], replicated, may hold values from 0.25 to 1.75
- ln_attn_bias: bfloat16 [512], replicated, may hold values from -3 to 3
- ln_mlp_gain: bfloat16 [512], replicated, may hold values from 0.25 to 1.75
- ln_mlp_bias: bfloat16 [512], replicated, may hold values from -3 to 3
- qkv_weight: bfloat16 [512, 1536], replicated, may hold values from -0.25 to 0.25
- content_bias: bfloat16 [512], replicated, may hold values from -3 to 3
- position_bias: bfloat16 [512], replicated, may hold values from -3 to 3
- pos_weight: bfloat16 [512, 512], replicated, may hold values from -0.75 to 0.75
- out_weight: bfloat16 [512, 512], replicated, may hold values from -2 to 2
- up_weight: bfloat16 [512, 3072], replicated, may hold values from -0.25 to 0.25
- up_bias: bfloat16 [3072], replicated, may hold values from -3 to 3
- gate_norm_gain: bfloat16 [1536], replicated, may hold values from 0.25 to 1.75
- gate_norm_bias: bfloat16 [1536], replicated, may hold values from -3 to 3
- conv_kernel: bfloat16 [31, 1536], replicated, may hold values from -1 to 1
- conv_bias: bfloat16 [1536], replicated, may hold values from -3 to 3
- down_weight: bfloat16 [1536, 512], replicated, may hold values from -0.15625 to 0.15625
- down_bias: bfloat16 [512], replicated, may hold values from -2 to 2
- merge_weight: bfloat16 [1024, 512], replicated, may hold values from -0.1875 to 0.1875
- merge_bias: bfloat16 [512], replicated, may hold values from -3 to 3
Outputs:
- output: bfloat16 [4, 1024, 512], P('stream', 'tm')
- grad_frames: float32 [4, 1024, 512], P('stream', 'tm')
- grad_ln_attn_gain: float32 [512], P('stream')
- grad_ln_attn_bias: float32 [512], P('stream')
- grad_ln_mlp_gain: float32 [512], P('stream')
- grad_ln_mlp_bias: float32 [512], P('stream')
- grad_qkv_weight: float32 [512, 1536], P('stream')
- grad_content_bias: float32 [512], P('stream')
- grad_position_bias: float32 [512], P('stream')
- grad_pos_weight: float32 [512, 512], P('stream')
- grad_out_weight: float32 [512, 512], P('stream')
- grad_up_weight: float32 [512, 3072], P('stream')
- grad_up_bias: float32 [3072], P('stream')
- grad_gate_norm_gain: float32 [1536], P('stream')
- grad_gate_norm_bias: float32 [1536], P('stream')
- grad_conv_kernel: float32 [31, 1536], P(None, 'stream')
- grad_conv_bias: float32 [1536], P('stream')
- grad_down_weight: float32 [1536, 512], P('stream')
- grad_down_bias: float32 [512], P('stream')
- grad_merge_weight: float32 [1024, 512], P('stream')
- grad_merge_bias: float32 [512], P('stream')
Inputs may be any that keep to these rules, and one draw needn't show every extreme that they name: Each stream's utterances start at frame 0 and lie end to end in order; exactly one of them, at a position that differs between streams, is 896 frames long, the others 1 to 32 frames; their lengths sum to at most 1024, the frames after them are padding.
All inputs are finite; a program needn't handle non-finite values.
Results may differ from a plain program's by a relative error of at most 0.025.
Values may be sent and summed in bfloat16 or wider, within the bound.
No kernel may reach another device: no remote copies, remote signals or barrier semaphores. Data moves between devices by JAX's collectives and lax.ppermute only.
A program may use at most 192 MiB of HBM per device.

v0:
```python
import math

import jax
import jax.numpy as jnp
from jax import lax
from jax.experimental import pallas as pl
from jax.experimental.pallas import tpu as pltpu
from jax.sharding import PartitionSpec as P

D = 512
HEADS = 8
HEAD = 64
KERNEL = 31
ITEMS = 5
HALF = 1536


EPS = 1e-05
MASKED = -1e30


def extended(block, sides, width):
    for axis, dim in sides:
        count = lax.axis_size(axis)
        forward = [(i, i + 1) for i in range(count - 1)]
        backward = [(target, source) for source, target in forward]
        low = lax.ppermute(
            lax.slice_in_dim(block, block.shape[dim] - width, None, axis=dim), axis, forward
        )
        high = lax.ppermute(lax.slice_in_dim(block, 0, width, axis=dim), axis, backward)
        block = jnp.concatenate([low, block, high], axis=dim)
    return block


def norm_rows(inputs, scale_row, shift_row):
    row_mean = jnp.mean(inputs, axis=-1, keepdims=True)
    centred = inputs - row_mean
    spread = jnp.mean(centred * centred, axis=-1, keepdims=True)
    return centred * lax.rsqrt(spread + EPS) * scale_row + shift_row


def gelu_exact(inputs):
    return jax.nn.gelu(inputs, approximate=False)


def frame_info(lengths, offset, extent):
    item_ends = jnp.cumsum(lengths)
    first_table = jnp.concatenate([item_ends - lengths, item_ends[-1:]])
    frame_index = offset + jnp.arange(extent, dtype=jnp.int32)
    item_of = jnp.sum((frame_index[:, None] >= item_ends[None, :]).astype(jnp.int32), axis=1)
    labels = jnp.arange(ITEMS + 1, dtype=jnp.int32)
    first_frame = jnp.sum(
        jnp.where(item_of[:, None] == labels[None, :], first_table[None, :], 0), axis=1
    )
    return (frame_index, item_of, frame_index - first_frame)


def angles(place_in):
    frequency = jnp.exp(jnp.arange(D // 2, dtype=jnp.float32) * (-2.0 * math.log(10000.0) / D))
    phase_angle = place_in.astype(jnp.float32)[:, None] * frequency[None, :]
    return (jnp.sin(phase_angle), jnp.cos(phase_angle))


def rel_query(projected, sine_rows, cosine_rows):
    half_size = projected.shape[-1] // 2
    first_half = projected[..., :half_size]
    second_half = projected[..., half_size:]
    sine_wide = sine_rows[:, None, :]
    cosine_wide = cosine_rows[:, None, :]
    return jnp.concatenate(
        [
            first_half * sine_wide + second_half * cosine_wide,
            second_half * sine_wide - first_half * cosine_wide,
        ],
        axis=-1,
    )


def step_size(extent):
    return math.gcd(extent, 512)


def score_block(q_content, q_rel, query_item, query_frame, key_block, key_start, lengths):
    extent = key_block.shape[0]
    key_frame, key_item, key_place = frame_info(lengths, key_start, extent)
    sine_rows, cosine_rows = angles(key_place)
    k_rel = jnp.concatenate([cosine_rows, sine_rows], axis=1).astype(jnp.bfloat16)
    raw_scores = jnp.einsum(
        "qhe,khe->hqk",
        q_content,
        key_block.reshape(extent, HEADS, HEAD),
        preferred_element_type=jnp.float32,
    )
    raw_scores = raw_scores + jnp.einsum(
        "qhc,kc->hqk", q_rel, k_rel, preferred_element_type=jnp.float32
    )
    allowed = (query_item[:, None] == key_item[None, :]) & (
        (query_item[:, None] < ITEMS) | (query_frame[:, None] == key_frame[None, :])
    )
    return (raw_scores, allowed, k_rel)


def block_grads(
    q_content,
    q_rel,
    query_item,
    query_frame,
    grad_out,
    log_total,
    delta_rows,
    key_block,
    value_block,
    key_start,
    lengths,
):
    extent = key_block.shape[0]
    raw_scores, allowed, k_rel = score_block(
        q_content, q_rel, query_item, query_frame, key_block, key_start, lengths
    )
    prob_rows = jnp.where(allowed[None], jnp.exp(raw_scores * 0.125 - log_total[:, :, None]), 0.0)
    grad_prob = jnp.einsum(
        "qhe,khe->hqk",
        grad_out,
        value_block.reshape(extent, HEADS, HEAD),
        preferred_element_type=jnp.float32,
    )
    grad_raw = (prob_rows * (grad_prob - delta_rows[:, :, None]) * 0.125).astype(jnp.bfloat16)
    return (prob_rows.astype(jnp.bfloat16), grad_raw, k_rel)


def frame_device(
    frames,
    lengths,
    cotangent,
    ln_attn_gain,
    ln_attn_bias,
    ln_mlp_gain,
    ln_mlp_bias,
    qkv_weight,
    content_bias,
    position_bias,
    pos_weight,
    out_weight,
    up_weight,
    up_bias,
    gate_norm_gain,
    gate_norm_bias,
    conv_kernel,
    conv_bias,
    down_weight,
    down_bias,
    merge_weight,
    merge_bias,
):
    row_count = frames.shape[1]
    cycle_size = lax.axis_size("tm")
    offset = lax.axis_index("tm") * row_count
    stream_lengths = lengths[0]
    inputs = frames[0].astype(jnp.float32)
    frame_index, item_of, place_in = frame_info(stream_lengths, offset, row_count)
    sine_rows, cosine_rows = angles(place_in)
    attn_norm, attn_pull = jax.vjp(
        norm_rows, inputs, ln_attn_gain.astype(jnp.float32), ln_attn_bias.astype(jnp.float32)
    )
    mlp_norm, mlp_pull = jax.vjp(
        norm_rows, inputs, ln_mlp_gain.astype(jnp.float32), ln_mlp_bias.astype(jnp.float32)
    )
    attn_norm_low = attn_norm.astype(jnp.bfloat16)
    mlp_norm_low = mlp_norm.astype(jnp.bfloat16)
    qkv_rows = jnp.dot(attn_norm_low, qkv_weight, preferred_element_type=jnp.float32)
    query_rows = qkv_rows[:, :D]
    key_rows = qkv_rows[:, D : 2 * D].astype(jnp.bfloat16)
    value_rows = qkv_rows[:, 2 * D :].astype(jnp.bfloat16)
    q_content = (query_rows + content_bias.astype(jnp.float32)).astype(jnp.bfloat16)
    q_position = (query_rows + position_bias.astype(jnp.float32)).astype(jnp.bfloat16)
    content_heads = q_content.reshape(row_count, HEADS, HEAD)
    position_heads = q_position.reshape(row_count, HEADS, HEAD)
    pos_heads = pos_weight.reshape(D, HEADS, HEAD)
    projected = jnp.einsum(
        "the,che->thc", position_heads, pos_heads, preferred_element_type=jnp.float32
    )
    q_rel = rel_query(projected, sine_rows, cosine_rows).astype(jnp.bfloat16)
    start_state = (
        jnp.full((HEADS, row_count), MASKED, jnp.float32),
        jnp.zeros((HEADS, row_count), jnp.float32),
        jnp.zeros((HEADS, row_count, HEAD), jnp.float32),
    )
    fold_state = start_state
    key_piece = lax.all_gather(key_rows, "tm", axis=0, tiled=True)
    value_piece = lax.all_gather(value_rows, "tm", axis=0, tiled=True)
    extent = key_piece.shape[0]
    step_rows = step_size(extent)

    def forward_one_step(inner_state, step_index):
        row_top, row_total, row_acc = inner_state
        key_block = lax.dynamic_slice_in_dim(key_piece, step_index * step_rows, step_rows, 0)
        value_block = lax.dynamic_slice_in_dim(value_piece, step_index * step_rows, step_rows, 0)
        raw_scores, allowed, k_rel = score_block(
            content_heads,
            q_rel,
            item_of,
            frame_index,
            key_block,
            step_index * step_rows,
            stream_lengths,
        )
        scaled = jnp.where(allowed[None], raw_scores * 0.125, MASKED)
        new_top = jnp.maximum(row_top, jnp.max(scaled, axis=2))
        weight = jnp.where(allowed[None], jnp.exp(scaled - new_top[:, :, None]), 0.0)
        factor = jnp.exp(row_top - new_top)
        row_total = row_total * factor + jnp.sum(weight, axis=2)
        row_acc = row_acc * factor[:, :, None] + jnp.einsum(
            "hqk,khe->hqe",
            weight.astype(jnp.bfloat16),
            value_block.reshape(step_rows, HEADS, HEAD),
            preferred_element_type=jnp.float32,
        )
        return ((new_top, row_total, row_acc), None)

    fold_state, unused = lax.scan(
        forward_one_step, fold_state, jnp.arange(extent // step_rows, dtype=jnp.int32)
    )
    row_top, row_total, row_acc = fold_state
    attn_heads = row_acc / row_total[:, :, None]
    log_total = row_top + jnp.log(row_total)
    attn_low = jnp.transpose(attn_heads, (1, 0, 2)).reshape(row_count, D).astype(jnp.bfloat16)
    branch_attn = jnp.dot(attn_low, out_weight, preferred_element_type=jnp.float32).astype(
        jnp.bfloat16
    )
    hidden_pre = jnp.dot(
        mlp_norm_low, up_weight, preferred_element_type=jnp.float32
    ) + up_bias.astype(jnp.float32)
    hidden, gelu_pull = jax.vjp(gelu_exact, hidden_pre)
    gate_half = hidden[:, :HALF]
    conv_norm, conv_pull = jax.vjp(
        norm_rows,
        hidden[:, HALF:],
        gate_norm_gain.astype(jnp.float32),
        gate_norm_bias.astype(jnp.float32),
    )
    conv_in = conv_norm.astype(jnp.bfloat16)
    half_width = KERNEL // 2
    conv_wide = extended(conv_in, (("tm", 0),), half_width)
    wide_frame, wide_item, wide_place = frame_info(
        stream_lengths, offset - half_width, row_count + 2 * half_width
    )
    kernel_rows = conv_kernel.astype(jnp.float32)
    conv_out = conv_bias.astype(jnp.float32) + jnp.zeros_like(gate_half)
    for tap_index in range(KERNEL):
        same_item = (wide_item[tap_index : tap_index + row_count] == item_of)[:, None]
        conv_out = (
            conv_out
            + jnp.where(
                same_item, conv_wide[tap_index : tap_index + row_count].astype(jnp.float32), 0.0
            )
            * kernel_rows[tap_index]
        )
    gated_low = (gate_half * conv_out).astype(jnp.bfloat16)
    branch_mlp = (
        jnp.dot(gated_low, down_weight, preferred_element_type=jnp.float32)
        + down_bias.astype(jnp.float32)
    ).astype(jnp.bfloat16)
    joined = jnp.concatenate([branch_attn, branch_mlp], axis=1)
    result = (
        inputs
        + jnp.dot(joined, merge_weight, preferred_element_type=jnp.float32)
        + merge_bias.astype(jnp.float32)
    )
    out_rows = result.astype(jnp.bfloat16)[None]
    grad_low = cotangent[0]
    grad_rows = grad_low.astype(jnp.float32)
    grad_merge_bias = jnp.sum(grad_rows, axis=0)
    grad_merge_weight = jnp.einsum(
        "tc,td->cd", joined, grad_low, preferred_element_type=jnp.float32
    )
    grad_joined = jnp.einsum(
        "td,cd->tc", grad_low, merge_weight, preferred_element_type=jnp.float32
    )
    grad_attn_branch = grad_joined[:, :D].astype(jnp.bfloat16)
    grad_mlp_branch = grad_joined[:, D:].astype(jnp.bfloat16)
    grad_down_weight = jnp.einsum(
        "tc,td->cd", gated_low, grad_mlp_branch, preferred_element_type=jnp.float32
    )
    grad_down_bias = jnp.sum(grad_mlp_branch.astype(jnp.float32), axis=0)
    grad_gated = jnp.einsum(
        "td,cd->tc", grad_mlp_branch, down_weight, preferred_element_type=jnp.float32
    )
    grad_gate_half = grad_gated * conv_out
    grad_conv_out = (grad_gated * gate_half).astype(jnp.bfloat16)
    grad_conv_rows = grad_conv_out.astype(jnp.float32)
    grad_conv_bias = jnp.sum(grad_conv_rows, axis=0)
    grad_wide = extended(grad_conv_out, (("tm", 0),), half_width)
    kernel_list = []
    grad_conv_in = jnp.zeros_like(grad_conv_rows)
    for tap_index in range(KERNEL):
        same_item = (wide_item[tap_index : tap_index + row_count] == item_of)[:, None]
        kernel_list.append(
            jnp.sum(
                jnp.where(
                    same_item, conv_wide[tap_index : tap_index + row_count].astype(jnp.float32), 0.0
                )
                * grad_conv_rows,
                axis=0,
            )
        )
        back_start = 2 * half_width - tap_index
        back_item = (wide_item[back_start : back_start + row_count] == item_of)[:, None]
        grad_conv_in = (
            grad_conv_in
            + jnp.where(
                back_item, grad_wide[back_start : back_start + row_count].astype(jnp.float32), 0.0
            )
            * kernel_rows[tap_index]
        )
    grad_conv_kernel = jnp.stack(kernel_list)
    grad_second, grad_gate_norm_gain, grad_gate_norm_bias = conv_pull(grad_conv_in)
    (grad_pre_rows,) = gelu_pull(jnp.concatenate([grad_gate_half, grad_second], axis=1))
    grad_pre = grad_pre_rows.astype(jnp.bfloat16)
    grad_up_bias = jnp.sum(grad_pre.astype(jnp.float32), axis=0)
    grad_up_weight = jnp.einsum(
        "tc,tf->cf", mlp_norm_low, grad_pre, preferred_element_type=jnp.float32
    )
    grad_mlp_norm = jnp.einsum("tf,cf->tc", grad_pre, up_weight, preferred_element_type=jnp.float32)
    grad_out_weight = jnp.einsum(
        "tc,td->cd", attn_low, grad_attn_branch, preferred_element_type=jnp.float32
    )
    grad_attn_low = jnp.einsum(
        "td,cd->tc", grad_attn_branch, out_weight, preferred_element_type=jnp.float32
    ).astype(jnp.bfloat16)
    grad_out_heads = grad_attn_low.reshape(row_count, HEADS, HEAD)
    delta_rows = jnp.sum(
        jnp.transpose(grad_out_heads.astype(jnp.float32), (1, 0, 2)) * attn_heads, axis=2
    )
    total_frames = row_count * cycle_size
    back_start_state = (
        jnp.zeros((row_count, HEADS, HEAD), jnp.float32),
        jnp.zeros((row_count, HEADS, D), jnp.float32),
        jnp.zeros((total_frames, D), jnp.float32),
        jnp.zeros((total_frames, D), jnp.float32),
    )
    back_key_piece = lax.all_gather(key_rows, "tm", axis=0, tiled=True)
    back_value_piece = lax.all_gather(value_rows, "tm", axis=0, tiled=True)
    extent = back_key_piece.shape[0]
    back_step_rows = step_size(extent)

    def back_one_step(inner_state, step_index):
        grad_content, grad_rel = inner_state
        key_block = lax.dynamic_slice_in_dim(
            back_key_piece, step_index * back_step_rows, back_step_rows, 0
        )
        value_block = lax.dynamic_slice_in_dim(
            back_value_piece, step_index * back_step_rows, back_step_rows, 0
        )
        prob_low, grad_raw, k_rel = block_grads(
            content_heads,
            q_rel,
            item_of,
            frame_index,
            grad_out_heads,
            log_total,
            delta_rows,
            key_block,
            value_block,
            step_index * back_step_rows,
            stream_lengths,
        )
        grad_content = grad_content + jnp.einsum(
            "hqk,khe->qhe",
            grad_raw,
            key_block.reshape(back_step_rows, HEADS, HEAD),
            preferred_element_type=jnp.float32,
        )
        grad_rel = grad_rel + jnp.einsum(
            "hqk,kc->qhc", grad_raw, k_rel, preferred_element_type=jnp.float32
        )
        key_part = jnp.einsum(
            "hqk,qhe->khe", grad_raw, content_heads, preferred_element_type=jnp.float32
        ).reshape(back_step_rows, D)
        value_part = jnp.einsum(
            "hqk,qhe->khe", prob_low, grad_out_heads, preferred_element_type=jnp.float32
        ).reshape(back_step_rows, D)
        return ((grad_content, grad_rel), (key_part, value_part))

    inner_state, block_parts = lax.scan(
        back_one_step,
        (back_start_state[0], back_start_state[1]),
        jnp.arange(extent // back_step_rows, dtype=jnp.int32),
    )
    key_all = block_parts[0].reshape(extent, D)
    value_all = block_parts[1].reshape(extent, D)
    grad_content, grad_rel, key_all, value_all = (
        inner_state[0],
        inner_state[1],
        key_all,
        value_all,
    )
    grad_keys, grad_values = (
        lax.psum_scatter(key_all, "tm", scatter_dimension=0, tiled=True),
        lax.psum_scatter(value_all, "tm", scatter_dimension=0, tiled=True),
    )
    half_size = D // 2
    rel_first = grad_rel[..., :half_size]
    rel_second = grad_rel[..., half_size:]
    sine_wide = sine_rows[:, None, :]
    cosine_wide = cosine_rows[:, None, :]
    grad_projected = jnp.concatenate(
        [
            rel_first * sine_wide - rel_second * cosine_wide,
            rel_first * cosine_wide + rel_second * sine_wide,
        ],
        axis=-1,
    ).astype(jnp.bfloat16)
    grad_pos_weight = jnp.einsum(
        "thc,the->che", grad_projected, position_heads, preferred_element_type=jnp.float32
    ).reshape(D, D)
    grad_q_position = jnp.einsum(
        "thc,che->the", grad_projected, pos_heads, preferred_element_type=jnp.float32
    )
    grad_content_bias = jnp.sum(grad_content, axis=0).reshape(D)
    grad_position_bias = jnp.sum(grad_q_position, axis=0).reshape(D)
    grad_query = (grad_content + grad_q_position).reshape(row_count, D).astype(jnp.bfloat16)
    grad_qkv = jnp.concatenate(
        [grad_query, grad_keys.astype(jnp.bfloat16), grad_values.astype(jnp.bfloat16)], axis=1
    )
    grad_qkv_weight = jnp.einsum(
        "tc,tf->cf", attn_norm_low, grad_qkv, preferred_element_type=jnp.float32
    )
    grad_attn_norm = jnp.einsum(
        "tf,cf->tc", grad_qkv, qkv_weight, preferred_element_type=jnp.float32
    )
    grad_from_attn, grad_ln_attn_gain, grad_ln_attn_bias = attn_pull(grad_attn_norm)
    grad_from_mlp, grad_ln_mlp_gain, grad_ln_mlp_bias = mlp_pull(grad_mlp_norm)
    grad_inputs = grad_rows + grad_from_attn + grad_from_mlp
    weight_grads = (
        grad_ln_attn_gain,
        grad_ln_attn_bias,
        grad_ln_mlp_gain,
        grad_ln_mlp_bias,
        grad_qkv_weight,
        grad_content_bias,
        grad_position_bias,
        grad_pos_weight,
        grad_out_weight,
        grad_up_weight,
        grad_up_bias,
        grad_gate_norm_gain,
        grad_gate_norm_bias,
        grad_conv_kernel,
        grad_conv_bias,
        grad_down_weight,
        grad_down_bias,
        grad_merge_weight,
        grad_merge_bias,
    )
    summed = lax.psum(
        (
            weight_grads[0],
            weight_grads[1],
            weight_grads[2],
            weight_grads[3],
            weight_grads[4],
            weight_grads[5],
            weight_grads[6],
            weight_grads[7],
            weight_grads[8],
            weight_grads[9],
            weight_grads[10],
            weight_grads[11],
            weight_grads[12],
            weight_grads[13],
            weight_grads[14],
            weight_grads[15],
            weight_grads[16],
            weight_grads[17],
            weight_grads[18],
        ),
        "tm",
    )
    shares = (
        lax.psum_scatter(
            summed[0].astype(jnp.bfloat16), "stream", scatter_dimension=0, tiled=True
        ).astype(jnp.float32),
        lax.psum_scatter(
            summed[1].astype(jnp.bfloat16), "stream", scatter_dimension=0, tiled=True
        ).astype(jnp.float32),
        lax.psum_scatter(
            summed[2].astype(jnp.bfloat16), "stream", scatter_dimension=0, tiled=True
        ).astype(jnp.float32),
        lax.psum_scatter(
            summed[3].astype(jnp.bfloat16), "stream", scatter_dimension=0, tiled=True
        ).astype(jnp.float32),
        lax.psum_scatter(
            summed[4].astype(jnp.bfloat16), "stream", scatter_dimension=0, tiled=True
        ).astype(jnp.float32),
        lax.psum_scatter(
            summed[5].astype(jnp.bfloat16), "stream", scatter_dimension=0, tiled=True
        ).astype(jnp.float32),
        lax.psum_scatter(
            summed[6].astype(jnp.bfloat16), "stream", scatter_dimension=0, tiled=True
        ).astype(jnp.float32),
        lax.psum_scatter(
            summed[7].astype(jnp.bfloat16), "stream", scatter_dimension=0, tiled=True
        ).astype(jnp.float32),
        lax.psum_scatter(
            summed[8].astype(jnp.bfloat16), "stream", scatter_dimension=0, tiled=True
        ).astype(jnp.float32),
        lax.psum_scatter(
            summed[9].astype(jnp.bfloat16), "stream", scatter_dimension=0, tiled=True
        ).astype(jnp.float32),
        lax.psum_scatter(
            summed[10].astype(jnp.bfloat16), "stream", scatter_dimension=0, tiled=True
        ).astype(jnp.float32),
        lax.psum_scatter(
            summed[11].astype(jnp.bfloat16), "stream", scatter_dimension=0, tiled=True
        ).astype(jnp.float32),
        lax.psum_scatter(
            summed[12].astype(jnp.bfloat16), "stream", scatter_dimension=0, tiled=True
        ).astype(jnp.float32),
        lax.psum_scatter(
            summed[13].astype(jnp.bfloat16), "stream", scatter_dimension=1, tiled=True
        ).astype(jnp.float32),
        lax.psum_scatter(
            summed[14].astype(jnp.bfloat16), "stream", scatter_dimension=0, tiled=True
        ).astype(jnp.float32),
        lax.psum_scatter(
            summed[15].astype(jnp.bfloat16), "stream", scatter_dimension=0, tiled=True
        ).astype(jnp.float32),
        lax.psum_scatter(
            summed[16].astype(jnp.bfloat16), "stream", scatter_dimension=0, tiled=True
        ).astype(jnp.float32),
        lax.psum_scatter(
            summed[17].astype(jnp.bfloat16), "stream", scatter_dimension=0, tiled=True
        ).astype(jnp.float32),
        lax.psum_scatter(
            summed[18].astype(jnp.bfloat16), "stream", scatter_dimension=0, tiled=True
        ).astype(jnp.float32),
    )
    return (out_rows, grad_inputs[None]) + tuple(shares)


LANES = 128
LOW = LANES // 2
BLOCK = 128
TALL = 256
WINDOW = 64
MARGIN = 16
BOUNDS = 16
MEGA = 1024 * 1024
F32 = jnp.float32
BF16 = jnp.bfloat16


def dot_nn(left, right):
    return jnp.dot(left, right, preferred_element_type=F32)


def dot_nt(left, right):
    return lax.dot_general(left, right, (((1,), (1,)), ((), ())), preferred_element_type=F32)


def dot_tn(left, right):
    return lax.dot_general(left, right, (((0,), (0,)), ((), ())), preferred_element_type=F32)


def rows_of(index, size, base=0):
    return pl.ds(pl.multiple_of(index * size, size) + base, size)


def line_of(ref):
    return ref[...].astype(F32).reshape(1, ref.shape[0])


def fold_rows(values):
    return jnp.sum(values.reshape(values.shape[0] // 8, 8, values.shape[1]), axis=0)


def one_row(values):
    return jnp.sum(values, axis=0, keepdims=True)


def turn(values):
    return pltpu.roll(values, LOW, 1)


def low_lanes(rows):
    return lax.broadcasted_iota(jnp.int32, (rows, LANES), 1) < LOW


def centre_rows(inputs):
    mean = jnp.mean(inputs, axis=-1, keepdims=True)
    centred = inputs - mean
    spread = jnp.mean(centred * centred, axis=-1, keepdims=True)
    return centred * lax.rsqrt(spread + EPS)


def gelu_parts(values):
    phi = 0.5 + 0.5 * lax.erf(values * math.sqrt(0.5))
    bell = jnp.exp(values * values * -0.5)
    return values * phi, phi + values * bell * (1.0 / math.sqrt(2.0 * math.pi))


class Part:
    def __init__(self, shape=None, pairs=None, refs=1, late=False):
        self.shape, self.pairs, self.refs, self.late = shape, pairs, refs, late

    def buffer(self, operand):
        return self.shape or operand.shape

    def copies(self, refs, buffer):
        return self.pairs(refs, buffer) if self.pairs else [(refs[0], buffer)]


def blocks_part(half, late=False):
    def pairs(refs, buffer):
        place = lax.axis_index("tm")
        return [
            (
                ref.at[:, pl.ds(half * D, D)],
                buffer.at[rows_of(lax.bitwise_xor(jnp.int32(apart), place), BLOCK)],
            )
            for apart, ref in enumerate(refs)
        ]

    return Part((HEADS * BLOCK, D), pairs, HEADS, late)


def rows_part(first, size, late=False):
    return Part((size, D), lambda refs, buffer: [(refs[0].at[pl.ds(first, size)], buffer)], late=late)


class Fetch:
    def __init__(self, pairs, buffer, sems, first):
        self.buffer, self.begun = buffer, False
        self.pending = [
            pltpu.make_async_copy(source, target, sems.at[first + index])
            for index, (source, target) in enumerate(pairs)
        ]

    def begin(self):
        if not self.begun:
            for copy in self.pending:
                copy.start()
        self.begun = True

    def __call__(self):
        self.begin()
        for copy in self.pending:
            copy.wait()
        self.pending = []
        return self.buffer


def begin(*fetches):
    for fetch in fetches:
        fetch.begin()


class Send:
    def __init__(self, buffer, target, sems):
        self.buffer, self.target, self.sems, self.copies = buffer, target, sems, []

    def go(self, *index):
        source, target = (self.buffer.at[index], self.target.at[index]) if index else (self.buffer, self.target)
        copy = pltpu.make_async_copy(source, target, self.sems[len(self.copies)])
        copy.start()
        self.copies.append(copy)

    def finish(self):
        if not self.copies:
            self.go()


SPACES = {"v": pltpu.VMEM, "s": pltpu.SMEM, "k": pl.ANY}


def kernel_call(body, out_shapes, plan, scratch=(), megas=58, bounds=False, aliases=None):
    def call(*operands):
        in_specs, buffers, at = [], [], 0
        for item in plan:
            if item == "f":
                in_specs.append(pl.BlockSpec(memory_space=pl.ANY))
                buffers.append(pltpu.VMEM(operands[at].shape, operands[at].dtype))
                at += 1
            elif isinstance(item, Part):
                in_specs += [pl.BlockSpec(memory_space=pl.ANY)] * item.refs
                buffers.append(pltpu.VMEM(item.buffer(operands[at]), operands[at].dtype))
                at += item.refs
            else:
                in_specs.append(pl.BlockSpec(memory_space=SPACES[item]))
                at += 1
        sent = [out for out in out_shapes if len(out) > 2]
        buffers += [pltpu.VMEM(out[3] if len(out) > 3 else out[0], out[1]) for out in sent]
        sem_count = 96
        extra = [pltpu.SMEM((BOUNDS,), jnp.int32)] if bounds else []

        def outer(*refs):
            inputs, rest = refs[: len(in_specs)], refs[len(in_specs) :]
            outputs, rest = rest[: len(out_shapes)], rest[len(out_shapes) :]
            held, rest = list(rest[: len(buffers)]), rest[len(buffers) :]
            sems, rest = rest[0], rest[1:]
            given, at, used = [], 0, 0
            for item in plan:
                if item == "f":
                    given.append(Fetch([(inputs[at], held[0])], held.pop(0), sems, used))
                    given[-1].begin()
                    used += 1
                    at += 1
                elif isinstance(item, Part):
                    buffer = held.pop(0)
                    pairs = item.copies(inputs[at : at + item.refs], buffer)
                    given.append(Fetch(pairs, buffer, sems, used))
                    if not item.late:
                        given[-1].begin()
                    used += len(pairs)
                    at += item.refs
                else:
                    given.append(inputs[at])
                    at += 1
            results = []
            for out, ref in zip(out_shapes, outputs):
                if len(out) > 2:
                    target = out[4](ref) if len(out) > 3 else ref
                    results.append(Send(held.pop(0), target, [sems.at[used + index] for index in range(4)]))
                    used += 4
                else:
                    results.append(ref)
            assert used <= sem_count
            given = [item() if kind == "f" else item for kind, item in zip(plan, given)]
            body(*given, *results, *rest)
            for item in given:
                if isinstance(item, Fetch):
                    item()
            sends = [item for item in results if isinstance(item, Send)]
            for item in sends:
                item.finish()
            for item in sends:
                for copy in item.copies:
                    copy.wait()

        return pl.pallas_call(
            outer,
            out_shape=[jax.ShapeDtypeStruct(out[0], out[1]) for out in out_shapes],
            in_specs=in_specs,
            out_specs=[pl.BlockSpec(memory_space=pl.ANY if len(out) > 2 else pltpu.VMEM) for out in out_shapes],
            scratch_shapes=buffers
            + [pltpu.SemaphoreType.DMA((sem_count,))]
            + [pltpu.VMEM(shape, kind) for shape, kind in scratch]
            + extra,
            input_output_aliases=aliases or {},
            compiler_params=pltpu.CompilerParams(vmem_limit_bytes=megas * MEGA),
            cost_estimate=pl.CostEstimate(flops=0, bytes_accessed=0, transcendentals=0),
        )(*operands)

    return call


def fill_bounds(lengths_ref, bounds_s, total):
    bounds_s[0] = jnp.int32(0)
    end = jnp.int32(0)
    for item in range(ITEMS):
        end = end + lengths_ref[0, item]
        bounds_s[item + 1] = end
    for item in range(ITEMS + 1, BOUNDS):
        bounds_s[item] = jnp.int32(total)


def select_kernel(
    up_ref,
    up_bias_ref,
    gain_ref,
    bias_ref,
    conv_bias_ref,
    taps_ref,
    qkv_ref,
    pos_ref,
    content_ref,
    position_ref,
    up_out,
    table_out,
    qkv_out,
    pos_out,
    bias_out,
):
    place = lax.axis_index("tm")
    quarters = lax.axis_size("stream")
    share = HALF // (quarters * lax.axis_size("tm"))
    lane = lax.broadcasted_iota(jnp.int32, (1, 2 * LANES), 1)
    channel = jnp.where(lane < LANES + LOW, lane, lane - LOW)
    group = jnp.zeros_like(channel)
    for quarter in range(1, quarters):
        group = group + (channel >= quarter * share).astype(jnp.int32)
    source = group * (HALF // quarters) + share * place + channel - group * share
    chosen = (lax.broadcasted_iota(jnp.int32, (HALF, 2 * LANES), 0) == source).astype(F32).astype(BF16)
    gate = dot_nn(up_ref[:, :HALF], chosen)
    conv = dot_nn(up_ref[:, HALF:], chosen)
    up_out[:, :LANES] = gate[:, :LANES].astype(BF16)
    up_out[:, LANES : 2 * LANES] = jnp.where(low_lanes(D), gate[:, LANES:], conv[:, LANES:]).astype(BF16)
    up_out[:, 2 * LANES :] = conv[:, :LANES].astype(BF16)
    up_bias = line_of(up_bias_ref)
    lines = jnp.concatenate(
        [
            up_bias[:, :HALF],
            up_bias[:, HALF:],
            line_of(gain_ref),
            line_of(bias_ref),
            line_of(conv_bias_ref),
            jnp.zeros((3, HALF), F32),
        ],
        axis=0,
    )
    lines = dot_nn(lines.astype(BF16), chosen)
    taps = dot_nn(taps_ref[...], chosen)
    for part in range(2):
        lanes = slice(part * LANES, (part + 1) * LANES)
        table_out[part, :8] = lines[:, lanes]
        table_out[part, 8 : 8 + KERNEL] = taps[:, lanes]
        table_out[part, 8 + KERNEL :] = jnp.zeros((1, LANES), F32)

    odd = lax.rem(place, 2) == 1

    def head_lanes(ref, base):
        at = pl.ds(pl.multiple_of(lax.div(place, 2) * LANES + base, LANES), LANES)
        values = ref[:, at].astype(F32)
        values = jnp.where(odd, turn(values), values)
        return jnp.where(low_lanes(values.shape[0]), values, 0.0)

    for part in range(3):
        qkv_out[:, part * LANES : (part + 1) * LANES] = head_lanes(qkv_ref, part * D).astype(BF16)
    pos_out[...] = head_lanes(pos_ref, 0).astype(BF16)
    bias_out[...] = jnp.zeros((8, LANES), F32)
    for line, ref in enumerate((content_ref, position_ref)):
        values = line_of(ref)
        picked = values[:, :LANES]
        for tile in range(1, D // LANES):
            picked = jnp.where(
                lax.div(place, 2) == tile, values[:, tile * LANES : (tile + 1) * LANES], picked
            )
        picked = jnp.where(odd, turn(picked), picked)
        bias_out[line : line + 1] = jnp.where(low_lanes(1), picked, 0.0)


def angle_rows(coarse_ref, fine_ref, block, rows):
    half = D // 2
    base = coarse_ref[pl.ds(block, 1)]
    base_sine, base_cosine = base[:, :half], base[:, half:]
    sine, cosine = fine_ref[rows, :half], fine_ref[rows, half:]
    return base_sine * cosine + base_cosine * sine, base_cosine * cosine - base_sine * sine


def item_codes(bounds_s, index):
    code = jnp.zeros_like(index)
    for item in range(1, ITEMS + 1):
        code = code + (index >= bounds_s[item]).astype(jnp.int32)
    return jnp.where(code < ITEMS, code, ITEMS + index)


def attend_kernel(
    lengths_ref,
    x_ref,
    attn_gain_ref,
    attn_bias_ref,
    mlp_gain_ref,
    mlp_bias_ref,
    qkv_ref,
    pos_ref,
    bias_ref,
    coarse_ref,
    fine_ref,
    up_ref,
    up_bias_ref,
    n_attn_out,
    n_mlp_out,
    hat_out,
    q_position_out,
    query_out,
    key_out,
    value_out,
    prob_out,
    attn_out,
    stats_out,
    bounds_s,
):
    frames = n_attn_out.buffer.shape[0]
    half = D // 2
    fill_bounds(lengths_ref, bounds_s, frames)
    attn_gain, attn_bias = line_of(attn_gain_ref), line_of(attn_bias_ref)
    mlp_gain, mlp_bias = line_of(mlp_gain_ref), line_of(mlp_bias_ref)
    content, position = bias_ref[0:1], bias_ref[1:2]
    x_ref = x_ref()
    begin(up_ref)

    @pl.loop(0, frames // TALL, unroll=4)
    def _(block):
        rows = rows_of(block, TALL)
        for part in range(TALL // 32):
            at = pl.ds(pl.multiple_of(block * TALL + part * 32, 32), 32)
            hat = centre_rows(x_ref[at].astype(F32))
            hat_out.buffer[at] = hat.astype(BF16)
            n_attn_out.buffer[at] = (hat * attn_gain + attn_bias).astype(BF16)
            n_mlp_out.buffer[at] = (hat * mlp_gain + mlp_bias).astype(BF16)
        parts = dot_nn(n_attn_out.buffer[rows], qkv_ref[...])
        query = parts[:, :LANES]
        query_out.buffer[rows, :LANES] = ((query + content).astype(BF16).astype(F32) * 0.125).astype(BF16)
        q_position = (query + position).astype(BF16)
        q_position_out.buffer[rows] = q_position
        key_out.buffer[rows, :LANES] = parts[:, LANES : 2 * LANES].astype(BF16)
        value_out.buffer[rows] = parts[:, 2 * LANES :].astype(BF16)
        projected = dot_nt(q_position, pos_ref[...])
        for part in range(TALL // 32):
            at = pl.ds(pl.multiple_of(block * TALL + part * 32, 32), 32)
            inner = part * 32 % BLOCK
            sine, cosine = angle_rows(
                coarse_ref, fine_ref, block * (TALL // BLOCK) + part * 32 // BLOCK, slice(inner, inner + 32)
            )
            first = projected[part * 32 : part * 32 + 32, :half]
            second = projected[part * 32 : part * 32 + 32, half:]
            query_out.buffer[at, LANES : LANES + half] = ((first * sine + second * cosine) * 0.125).astype(BF16)
            query_out.buffer[at, LANES + half :] = ((second * sine - first * cosine) * 0.125).astype(BF16)
            key_out.buffer[at, LANES : LANES + half] = cosine.astype(BF16)
            key_out.buffer[at, LANES + half :] = sine.astype(BF16)

    for out in (n_attn_out, n_mlp_out, hat_out, q_position_out, query_out, key_out, value_out):
        out.go()
    up_ref = up_ref()
    up_bias = line_of(up_bias_ref)[:, HALF:]
    lane = lax.broadcasted_iota(jnp.int32, (16, LANES), 1)

    @pl.loop(0, frames // TALL, unroll=2)
    def _(block):
        values = dot_nn(n_mlp_out.buffer[rows_of(block, TALL)], up_ref[...])
        for part in range(TALL // 16):
            pre = values[part * 16 : part * 16 + 16] + up_bias
            hidden = pre * (0.5 + 0.5 * lax.erf(pre * math.sqrt(0.5)))
            mean = jnp.mean(hidden, axis=-1, keepdims=True)
            centred = hidden - mean
            rate = lax.rsqrt(jnp.mean(centred * centred, axis=-1, keepdims=True) + EPS)
            at = pl.ds(pl.multiple_of(block * TALL + part * 16, 16), 16)
            stats_out.buffer[at] = jnp.where(lane == 0, mean, rate)

    stats_out.go()
    key_code = item_codes(bounds_s, lax.broadcasted_iota(jnp.int32, (1, frames), 1))

    low = low_lanes(32)
    for block in range(frames // TALL):
        rows = pl.ds(block * TALL, TALL)
        raw = dot_nt(query_out.buffer[rows], key_out.buffer[...])
        shares = []
        for part in range(TALL // 32):
            start = block * TALL + part * 32
            index = start + lax.broadcasted_iota(jnp.int32, (32, 1), 0)
            scaled = jnp.where(
                item_codes(bounds_s, index) == key_code, raw[part * 32 : part * 32 + 32], MASKED
            )
            weight = jnp.exp(scaled - jnp.max(scaled, axis=1, keepdims=True))
            prob_out.buffer[pl.ds(start, 32)] = weight.astype(BF16)
            shares.append(1.0 / jnp.sum(weight, axis=1, keepdims=True))
        prob_out.go(rows)
        attn = dot_nn(prob_out.buffer[rows], value_out.buffer[...])
        for part in range(TALL // 32):
            share = shares[part]
            attn_out.buffer[pl.ds(block * TALL + part * 32, 32)] = jnp.where(
                low, attn[part * 32 : part * 32 + 32] * share, share
            )


def fill_margins(wide_s, frames):
    edge = jnp.zeros((MARGIN, LANES), F32)
    wide_s[0, :MARGIN] = edge
    wide_s[0, MARGIN + frames : 2 * MARGIN + frames] = edge
    base = frames + 3 * MARGIN
    after = base + frames // 2
    low = low_lanes(MARGIN)
    wide_s[0, base - MARGIN : base] = jnp.where(low, 0.0, turn(wide_s[0, after - MARGIN : after]))
    wide_s[0, after : after + MARGIN] = jnp.where(low, turn(wide_s[0, base : base + MARGIN]), 0.0)
    wide_s[0, after + MARGIN :] = jnp.zeros((wide_s.shape[1] - after - MARGIN, LANES), F32)

    @pl.loop(0, (after + MARGIN) // WINDOW, unroll=5)
    def _(step):
        window = wide_s[0, pl.ds(pl.multiple_of(step * WINDOW, WINDOW), WINDOW + 8)]
        for shift in range(1, 8):
            wide_s[shift, pl.ds(pl.multiple_of(step * WINDOW, WINDOW), WINDOW)] = window[shift : shift + WINDOW]


def item_span(bounds_s, frame):
    begin, end = bounds_s[0], bounds_s[BOUNDS - 1]
    for item in range(1, ITEMS + 1):
        edge = bounds_s[item]
        begin = jnp.where(frame >= edge, edge, begin)
    for item in range(ITEMS, 0, -1):
        edge = bounds_s[item]
        end = jnp.where(frame < edge, edge, end)
    return begin, end


def is_whole(bounds_s, start):
    begin, end = item_span(bounds_s, start)
    reach = KERNEL // 2
    low = (begin == 0) | (begin <= start - reach)
    high = (end == bounds_s[BOUNDS - 1]) | (end >= start + WINDOW + reach)
    return low & high & (end >= start + WINDOW)


def tap_limits(bounds_s, start):
    frame = start + lax.broadcasted_iota(jnp.int32, (WINDOW, LANES), 0)
    begin, end = item_span(bounds_s, frame)
    return begin - frame, end - frame


def grouped(values):
    return values.reshape(WINDOW // 8, 8, LANES)


def triple_places(step, frames):
    half = frames // 2
    return (
        pl.multiple_of(step * WINDOW, 2 * MARGIN),
        pl.multiple_of(step * WINDOW + half, 2 * MARGIN),
        pl.multiple_of(step * WINDOW + frames + 2 * MARGIN, 2 * MARGIN),
    )


def over_windows(bounds_s, frames, body):
    half = frames // 2

    @pl.loop(0, half // WINDOW)
    def _(step):
        start = step * WINDOW
        whole = is_whole(bounds_s, start) & is_whole(bounds_s, start + half)

        @pl.when(whole)
        def _():
            body(step, None)

        @pl.when(jnp.logical_not(whole))
        def _():
            first, second = tap_limits(bounds_s, start), tap_limits(bounds_s, start + half)
            low = low_lanes(WINDOW)
            rest = [jnp.where(low, one, other) for one, other in zip(first, second)]
            body(step, (first, second, rest))


def tap_mask(tap, limits):
    shift = tap - KERNEL // 2
    return None if limits is None else (limits[0] <= shift) & (limits[1] > shift)


def tap_view(wide_s, base, tap, mask):
    at = pl.ds(pl.multiple_of(base + (tap + 1) // 8 * 8, 8), WINDOW)
    view = wide_s[(tap + 1) % 8, at]
    return grouped(view if mask is None else jnp.where(mask, view, 0.0))


def mlp_first_kernel(
    lengths_ref,
    n_ref,
    up_ref,
    table_ref,
    stats_ref,
    cot_ref,
    merge_ref,
    down_ref,
    attn_ref,
    mixed_out,
    gate_pre_out,
    grad_out,
    rate_out,
    hat_out,
    early_out,
    vectors_out,
    lines_out,
    hat_s,
    slope_s,
    gate_s,
    hidden_s,
    gate_slope_s,
    conv_s,
    grad_s,
    out_s,
    back_s,
    branch_s,
    mix_s,
    taps_s,
    turn_s,
    tap_sum_s,
    columns_s,
    bounds_s,
):
    frames = mix_s.shape[0]
    half = frames // 2
    blocks = frames // BLOCK
    quarters, early_rows, _ = early_out.buffer.shape
    share = early_rows // 8
    channels = quarters * share
    fill_bounds(lengths_ref, bounds_s, frames)
    for part in range(2):
        for tap in range(KERNEL):
            line = jnp.broadcast_to(table_ref[part, 8 + tap : 9 + tap], (8, LANES))
            taps_s[part, tap] = line
            turn_s[part, KERNEL - 1 - tap] = line
    tap_sum_s[...] = jnp.zeros(tap_sum_s.shape, F32)
    main, rest = table_ref[0, :8], table_ref[1, :8]
    mixed_bias = jnp.where(low_lanes(1), rest[0:1], rest[1:2])
    low = low_lanes(64)
    gate_pre_ref = gate_pre_out.buffer
    n_ref = n_ref()
    stats_ref = stats_ref()
    begin(cot_ref, merge_ref, down_ref, attn_ref)

    def stat_rows(rows):
        stats = stats_ref[rows]
        return stats[:, 0:1], stats[:, 1:2]

    def chunk(start, base=0):
        return pl.ds(pl.multiple_of(start, 64) + base, 64)

    def conv_part(hidden, mean, rate, lines, rows, to_rows):
        hat = (hidden - mean) * rate
        hat_s[rows] = hat
        hat_out.buffer[rows] = hat.astype(BF16)
        conv_s[0, to_rows] = (hat * lines[2:3] + lines[3:4]).astype(BF16).astype(F32)

    @pl.loop(0, half // TALL, unroll=2)
    def _(block):
        pre = [dot_nn(n_ref[rows_of(block, TALL, base)], up_ref[...]) for base in (0, half)]
        for part in range(TALL // 64):
            inner = slice(part * 64, part * 64 + 64)
            start = block * TALL + part * 64
            mixed = []
            for values, base in zip(pre, (0, half)):
                rows = chunk(start, base)
                gate, gate_slope = gelu_parts(values[inner, :LANES] + main[0:1])
                hidden_s[rows] = gate
                gate_slope_s[rows] = gate_slope
                hidden, slope = gelu_parts(values[inner, 2 * LANES :] + main[1:2])
                mean, rate = stat_rows(rows)
                slope_s[rows] = slope * rate
                conv_part(hidden, mean, rate, main, rows, chunk(start, base + MARGIN))
                mixed.append((*gelu_parts(values[inner, LANES : 2 * LANES] + mixed_bias), mean, rate))
            (low_hidden, low_slope, low_mean, low_rate), (high_hidden, high_slope, high_mean, high_rate) = mixed
            rows = chunk(start, frames)
            hidden_s[rows] = jnp.where(low, low_hidden, turn(high_hidden))
            gate_slope_s[rows] = jnp.where(low, low_slope, turn(high_slope))
            rate = jnp.where(low, low_rate, high_rate)
            slope_s[rows] = jnp.where(low, turn(low_slope), high_slope) * rate
            conv_part(
                jnp.where(low, turn(low_hidden), high_hidden),
                jnp.where(low, low_mean, high_mean),
                rate,
                rest,
                rows,
                chunk(start, frames + 3 * MARGIN),
            )

    hat_out.go()
    fill_margins(conv_s, frames)
    outs = (0, half, frames)

    def convolve(step, limits):
        for index, base in enumerate(triple_places(step, frames)):
            own = None if limits is None else limits[index]
            total = jnp.zeros((WINDOW // 8, 8, LANES), F32)
            for tap in range(KERNEL):
                view = tap_view(conv_s, base, tap, tap_mask(tap, own))
                total = total + view * taps_s[index // 2, tap][None]
            lines = rest if index == 2 else main
            out_s[rows_of(step, WINDOW, outs[index])] = total.reshape(WINDOW, LANES) + lines[4:5]

    over_windows(bounds_s, frames, convolve)
    cot_ref = cot_ref()
    merge_ref = merge_ref()
    down_ref = down_ref()
    attn_ref = attn_ref()
    down_ref[channels:] = jnp.zeros((2 * LANES - channels, D), BF16)
    zero = jnp.zeros((8, LANES), F32)

    def branch_part(grad_gated, rows, to_rows, sums):
        up_sum, conv_sum = sums
        gate, conv = hidden_s[rows], out_s[rows]
        gate_pre = (grad_gated * conv * gate_slope_s[rows]).astype(BF16)
        gate_pre_ref[rows] = gate_pre
        grad_conv = (grad_gated * gate).astype(BF16).astype(F32)
        grad_s[0, to_rows] = grad_conv
        gate_pre = gate_pre.astype(F32)
        return gate * conv, gate_pre, (up_sum + fold_rows(gate_pre), conv_sum + fold_rows(grad_conv))

    def branch_step(block, sums):
        main_sums, rest_sums = sums
        grads = []
        for base in (0, half):
            rows = rows_of(block, TALL, base)
            branch = dot_nt(cot_ref[rows], merge_ref[...]).astype(BF16)
            branch_s[rows] = branch
            grads.append(dot_nt(branch, down_ref[...]))
        for part in range(TALL // 64):
            inner = slice(part * 64, part * 64 + 64)
            start = block * TALL + part * 64
            for values, base in zip(grads, (0, half)):
                rows = chunk(start, base)
                gated, gate_pre, main_sums = branch_part(
                    values[inner, :LANES], rows, chunk(start, base + MARGIN), main_sums
                )
                mix_s[rows, :LANES] = gated.astype(BF16)
                gate_s[rows, :LANES] = gate_pre.astype(BF16)
            grad = jnp.where(low, grads[0][inner, LANES:], turn(grads[1][inner, LANES:]))
            gated, gate_pre, rest_sums = branch_part(
                grad, chunk(start, frames), chunk(start, frames + 3 * MARGIN), rest_sums
            )
            low_rows, high_rows = chunk(start), chunk(start, half)
            gate_s[low_rows, LANES:] = gate_pre.astype(BF16)
            gate_s[high_rows, LANES:] = turn(gate_pre).astype(BF16)
            mix_s[low_rows, LANES:] = jnp.where(low, gated, turn(attn_ref[low_rows])).astype(BF16)
            mix_s[high_rows, LANES:] = jnp.where(low, turn(gated), turn(attn_ref[high_rows])).astype(BF16)
        return main_sums, rest_sums

    (main_up, main_conv), (rest_up, rest_conv) = lax.fori_loop(
        0, half // TALL, branch_step, ((zero, zero), (zero, zero)), unroll=2
    )
    gate_pre_out.go()
    fill_margins(grad_s, frames)
    ones = jnp.ones((16, frames), BF16)
    lines_out[0:1] = dot_nn(ones, branch_s[...])[0:1]
    lines_out[1:2] = dot_nn(ones, cot_ref[...])[0:1]
    lines_out[2:8] = jnp.zeros((6, D), F32)
    grad_down = dot_tn(mix_s[...], branch_s[...])
    grad_gate = dot_tn(gate_s[...], n_ref[...])
    for quarter in range(quarters):
        for tile in range(4):
            early_out.buffer[quarter, tile * share : (tile + 1) * share] = grad_down[
                quarter * share : (quarter + 1) * share, tile * LANES : (tile + 1) * LANES
            ].astype(BF16)
        early_out.buffer[quarter, 4 * share :] = grad_gate[
            :channels, quarter * LANES : (quarter + 1) * LANES
        ].astype(BF16)
    early_out.go()
    for block in range(blocks):
        mixed_out.buffer[block, :BLOCK] = mix_s[block * BLOCK : (block + 1) * BLOCK]
    mixed_out.go(slice(None), pl.ds(0, BLOCK))

    def differentiate(step, limits):
        for index, base in enumerate(triple_places(step, frames)):
            own = None if limits is None else limits[index]
            total = jnp.zeros((WINDOW // 8, 8, LANES), F32)
            centre = grouped(grad_s[0, pl.ds(base + MARGIN, WINDOW)])
            for tap in range(KERNEL):
                mask = tap_mask(tap, own)
                total = total + tap_view(grad_s, base, tap, mask) * turn_s[index // 2, tap][None]
                tap_sum_s[index // 2, tap] += jnp.sum(tap_view(conv_s, base, tap, mask) * centre, axis=0)
            back_s[rows_of(step, WINDOW, outs[index])] = total.reshape(WINDOW, LANES)

    over_windows(bounds_s, frames, differentiate)
    lane = lax.broadcasted_iota(jnp.int32, (64, LANES), 1)

    def norm_part(rows, lines, sums):
        gain_sum, bias_sum = sums
        back, hat, slope = back_s[rows], hat_s[rows], slope_s[rows]
        grad = back * lines[2:3]
        grad_out.buffer[rows] = (grad * slope).astype(BF16)
        rate_out.buffer[rows] = slope.astype(BF16)
        along = back * hat
        return grad, along * lines[2:3], (gain_sum + fold_rows(along), bias_sum + fold_rows(back))

    def norm_step(block, sums):
        main_sums, rest_sums = sums
        for part in range(TALL // 64):
            start = block * TALL + part * 64
            pairs = []
            for base in (0, half):
                plain, along, main_sums = norm_part(chunk(start, base), main, main_sums)
                pairs.append([plain, along])
            plain, along, rest_sums = norm_part(chunk(start, frames), rest, rest_sums)
            for item, values in enumerate((plain, along)):
                pairs[0][item] = pairs[0][item] + jnp.where(low, values, 0.0)
                pairs[1][item] = pairs[1][item] + jnp.where(low, 0.0, values)
            for (plain, along), base in zip(pairs, (0, half)):
                columns_s[chunk(start, base)] = jnp.where(
                    lane == 0,
                    jnp.sum(plain, axis=-1, keepdims=True),
                    jnp.where(lane == 1, jnp.sum(along, axis=-1, keepdims=True), 0.0),
                )
        return main_sums, rest_sums

    (main_gain, main_bias), (rest_gain, rest_bias) = lax.fori_loop(
        0, half // TALL, norm_step, ((zero, zero), (zero, zero)), unroll=2
    )
    grad_out.go()
    rate_out.go()
    totals = jnp.concatenate(
        [jnp.transpose(columns_s[block * BLOCK : (block + 1) * BLOCK])[:2] for block in range(blocks)], axis=0
    )
    high = totals.astype(BF16)
    low_part = (totals - high.astype(F32)).astype(BF16)
    for block in range(blocks):
        mixed_out.buffer[block, BLOCK:, :LANES] = high
        mixed_out.buffer[block, BLOCK:, LANES:] = low_part
    mixed_out.go(slice(None), pl.ds(BLOCK, 2 * blocks))

    def vectors(part, lines):
        taps = jnp.sum(tap_sum_s[part], axis=1)[:KERNEL]
        stacked = jnp.concatenate([taps] + [one_row(line) for line in lines], axis=0)
        if part:
            stacked = stacked + turn(stacked)
        return jnp.transpose(
            jnp.concatenate([stacked, jnp.zeros((LANES - stacked.shape[0], LANES), F32)], axis=0)
        )

    vectors_out[:LANES] = vectors(0, (main_conv, main_gain, main_bias, main_up))
    vectors_out[LANES:] = vectors(1, (rest_conv, rest_gain, rest_bias, rest_up))[: channels - LANES]


def attend_back_kernel(
    cot_ref,
    merge_ref,
    head_ref,
    attn_ref,
    value_ref,
    prob_ref,
    key_ref,
    coarse_ref,
    fine_ref,
    pos_ref,
    query_ref,
    n_ref,
    q_position_ref,
    qkv_ref,
    hat_ref,
    gain_ref,
    early_ref,
    branch_out,
    total_out,
    pack_0,
    pack_1,
    pack_2,
    pack_3,
    lines_out,
    grad_s,
    raw_s,
    projected_s,
    parts_s,
    grads_s,
):
    place = lax.axis_index("tm")
    frames = raw_s.shape[0]
    blocks = frames // BLOCK
    half = D // 2
    zero = jnp.zeros((8, LANES), F32)
    cot_ref, merge_ref, head_ref, attn_ref = cot_ref(), merge_ref(), head_ref(), attn_ref()
    head_ref[HEAD:] = jnp.zeros((LANES - HEAD, D), BF16)
    begin(value_ref, prob_ref, key_ref, pos_ref)

    @pl.loop(0, frames // TALL, unroll=4)
    def _(block):
        rows = rows_of(block, TALL)
        branch = dot_nt(cot_ref[rows], merge_ref[...]).astype(BF16)
        branch_out.buffer[rows] = branch
        grad_s[rows] = (dot_nt(branch, head_ref[...]) * attn_ref[rows, HEAD : HEAD + 1]).astype(BF16)

    branch_out.go()
    value_ref, prob_ref = value_ref(), prob_ref()
    key_ref, pos_ref = key_ref(), pos_ref()
    begin(query_ref, n_ref, q_position_ref, qkv_ref, hat_ref, early_ref)

    def score_step(block, sums):
        content_sum, position_sum = sums
        rows = rows_of(block, TALL)
        grad = grad_s[rows]
        score = dot_nt(grad, value_ref[...])
        for part in range(TALL // 32):
            at = pl.ds(pl.multiple_of(block * TALL + part * 32, 32), 32)
            inner = slice(part * 32, part * 32 + 32)
            delta = jnp.sum(grad[inner].astype(F32) * attn_ref[at], axis=1, keepdims=True)
            raw_s[at] = (prob_ref[at].astype(F32) * (score[inner] - delta)).astype(BF16)
        query = dot_nn(raw_s[rows], key_ref[...]) * 0.125
        for part in range(TALL // 32):
            at = pl.ds(pl.multiple_of(block * TALL + part * 32, 32), 32)
            inner = part * 32 % BLOCK
            sine, cosine = angle_rows(
                coarse_ref, fine_ref, block * (TALL // BLOCK) + part * 32 // BLOCK, slice(inner, inner + 32)
            )
            inner = slice(part * 32, part * 32 + 32)
            first, second = query[inner, LANES : LANES + half], query[inner, LANES + half :]
            projected_s[at, :half] = (first * sine - second * cosine).astype(BF16)
            projected_s[at, half:] = (first * cosine + second * sine).astype(BF16)
        position = dot_nn(projected_s[rows], pos_ref[...])
        content = query[:, :LANES]
        parts_s[rows, :LANES] = (content + position).astype(BF16)
        return content_sum + fold_rows(content), position_sum + fold_rows(position)

    content_sum, position_sum = lax.fori_loop(0, frames // TALL, score_step, (zero, zero), unroll=4)
    query_ref, n_ref, q_position_ref = query_ref(), n_ref(), q_position_ref()
    qkv_ref, hat_ref = qkv_ref(), hat_ref()
    grad_key = dot_tn(query_ref[...], raw_s[...])
    grad_value = dot_tn(grad_s[...], prob_ref[...])
    for block in range(blocks):
        at = slice(block * BLOCK, (block + 1) * BLOCK)
        parts_s[at, LANES : 2 * LANES] = jnp.transpose(grad_key[:, at]).astype(BF16)
        parts_s[at, 2 * LANES :] = jnp.transpose(grad_value[:, at]).astype(BF16)
    grads_s[:HEAD] = dot_tn(parts_s[:, :LANES], n_ref[...])[:HEAD]
    grads_s[HEAD : 2 * HEAD] = dot_nn(grad_key.astype(BF16), n_ref[...])[:HEAD]
    grads_s[2 * HEAD : 3 * HEAD] = dot_nn(grad_value.astype(BF16), n_ref[...])[:HEAD]
    grads_s[3 * HEAD :] = dot_tn(q_position_ref[...], projected_s[...])[:HEAD]
    stream = lax.axis_index("stream")
    early_ref = early_ref()
    for apart, pack_out in enumerate((pack_0, pack_1, pack_2, pack_3)):
        quarter = lax.bitwise_xor(stream, jnp.int32(apart))
        lanes = pl.ds(pl.multiple_of(quarter * LANES, LANES), LANES)
        pack_out.buffer[: 4 * HEAD] = grads_s[:, lanes].astype(BF16)
        pack_out.buffer[4 * HEAD :] = early_ref[quarter]
        pack_out.go()
    gain = line_of(gain_ref)
    wide_zero = jnp.zeros((8, D), F32)

    def norm_step(block, sums):
        gain_sum, bias_sum = sums
        grad = dot_nt(parts_s[rows_of(block, TALL)], qkv_ref[...])
        for part in range(TALL // 32):
            at = pl.ds(pl.multiple_of(block * TALL + part * 32, 32), 32)
            own = grad[part * 32 : part * 32 + 32]
            total_out.buffer[at] = (own * gain).astype(BF16)
            gain_sum = gain_sum + fold_rows(own * hat_ref[at].astype(F32))
            bias_sum = bias_sum + fold_rows(own)
        return gain_sum, bias_sum

    gain_sum, bias_sum = lax.fori_loop(0, frames // TALL, norm_step, (wide_zero, wide_zero), unroll=4)
    lane = lax.broadcasted_iota(jnp.int32, (1, LANES), 1)

    def own_lanes(sums):
        line = one_row(sums)
        line = line + turn(line)
        tiles = [
            jnp.where(lax.div(tile * LANES + lane, HEAD) == place, line, 0.0) for tile in range(D // LANES)
        ]
        return jnp.concatenate(tiles, axis=1)

    lines_out[...] = jnp.concatenate(
        [
            one_row(gain_sum),
            one_row(bias_sum),
            own_lanes(content_sum),
            own_lanes(position_sum),
            jnp.zeros((4, D), F32),
        ],
        axis=0,
    )


def mlp_second_kernel(
    mixed_ref,
    gate_pre_ref,
    grad_ref,
    rate_ref,
    hat_ref,
    up_ref,
    norm_hat_ref,
    gain_ref,
    other_ref,
    n_ref,
    vectors_ref,
    first_lines_ref,
    head_lines_ref,
    same_out,
    apart_out,
    pack_out,
    pre_s,
    columns_s,
    grad_up_s,
    lines_s,
    up_columns_s,
):
    pack_ref = pack_out.buffer
    place = lax.axis_index("tm")
    frames = pre_s.shape[0]
    half = frames // 2
    blocks = frames // BLOCK
    quarters = pack_ref.shape[0]
    channels = vectors_ref.shape[0]
    share = channels // quarters
    totals = jnp.zeros((2 * blocks, LANES), F32)
    mixed_ref = mixed_ref()
    for source in range(mixed_ref.shape[0]):
        both = mixed_ref[source].astype(F32)
        totals = totals + (both[:, :LANES] + both[:, LANES:])
    totals = totals * (1.0 / HALF)
    columns = jnp.transpose(jnp.concatenate([totals, jnp.zeros((LANES - 2 * blocks, LANES), F32)], axis=0))
    lane = lax.broadcasted_iota(jnp.int32, (BLOCK, LANES), 1)
    for block in range(blocks):
        columns_s[block * BLOCK : (block + 1) * BLOCK] = jnp.where(
            lane == 0, columns[:, 2 * block : 2 * block + 1], columns[:, 2 * block + 1 : 2 * block + 2]
        )
    gate_pre_ref, grad_ref, rate_ref, hat_ref = gate_pre_ref(), grad_ref(), rate_ref(), hat_ref()
    begin(n_ref, up_ref, norm_hat_ref, other_ref)
    low = low_lanes(64)
    gain = line_of(gain_ref)

    def chunk(start, base=0):
        return pl.ds(pl.multiple_of(start, 64) + base, 64)

    def pre_part(rows, table, up_sum):
        plain, along = table
        hat, rate = hat_ref[rows].astype(F32), rate_ref[rows].astype(F32)
        pre = (grad_ref[rows].astype(F32) - rate * (plain + hat * along)).astype(BF16).astype(F32)
        return pre, up_sum + fold_rows(pre)

    def pre_step(block, sums):
        main_up, rest_up = sums
        for part in range(TALL // 64):
            start = block * TALL + part * 64
            tables = []
            for base in (0, half):
                rows = chunk(start, base)
                values = columns_s[rows]
                table = [values[:, item : item + 1] for item in range(2)]
                tables.append(table)
                pre, main_up = pre_part(rows, table, main_up)
                pre_s[rows, :LANES] = gate_pre_ref[rows]
                pre_s[rows, 2 * LANES :] = pre.astype(BF16)
            rows = chunk(start, frames)
            table = [jnp.where(low, one, other) for one, other in zip(*tables)]
            pre, rest_up = pre_part(rows, table, rest_up)
            gate_pre = gate_pre_ref[rows].astype(F32)
            pre_s[chunk(start), LANES : 2 * LANES] = jnp.where(low, gate_pre, turn(pre)).astype(BF16)
            pre_s[chunk(start, half), LANES : 2 * LANES] = jnp.where(low, turn(gate_pre), pre).astype(BF16)
        return main_up, rest_up

    zero = jnp.zeros((8, LANES), F32)
    main_up, rest_up = lax.fori_loop(0, half // TALL, pre_step, (zero, zero), unroll=2)
    n_ref, up_ref, norm_hat_ref, other_ref = n_ref(), up_ref(), norm_hat_ref(), other_ref()
    grad_up_s[...] = dot_tn(pre_s[:, LANES:], n_ref[...])
    wide_zero = jnp.zeros((8, D), F32)

    def norm_step(block, sums):
        gain_sum, bias_sum = sums
        rows = rows_of(block, BLOCK)
        grad = dot_nt(pre_s[rows], up_ref[...])
        total = (grad * gain + other_ref[rows].astype(F32)).astype(BF16)
        apart = lax.bitwise_xor(block, place)

        @pl.when(lax.rem(apart, 2) == 0)
        def _():
            same_out.buffer[lax.div(apart, 2)] = total

        @pl.when(lax.rem(apart, 2) == 1)
        def _():
            apart_out.buffer[lax.div(apart, 2)] = total

        return gain_sum + fold_rows(grad * norm_hat_ref[rows].astype(F32)), bias_sum + fold_rows(grad)

    gain_sum, bias_sum = lax.fori_loop(0, blocks, norm_step, (wide_zero, wide_zero), unroll=4)
    apart_out.go()
    same_out.go()
    rest_line = one_row(rest_up)
    up_columns_s[:LANES] = jnp.transpose(jnp.broadcast_to(one_row(main_up), (LANES, LANES)))
    up_columns_s[LANES:] = jnp.transpose(jnp.broadcast_to(rest_line + turn(rest_line), (LANES, LANES)))[:LOW]
    first_device = (place == 0).astype(F32)
    lines_s[...] = jnp.concatenate(
        [
            head_lines_ref[0:2],
            one_row(gain_sum),
            one_row(bias_sum),
            head_lines_ref[2:4],
            first_lines_ref[0:2] * first_device,
            jnp.zeros((8, D), F32),
        ],
        axis=0,
    )
    gate_at = KERNEL + 3
    lane = lax.broadcasted_iota(jnp.int32, (share, LANES), 1)
    for quarter in range(quarters):
        lanes = slice(quarter * LANES, (quarter + 1) * LANES)
        pack_ref[quarter, :LANES] = grad_up_s[LANES:, lanes].astype(BF16)
        pack_ref[quarter, LANES:channels] = grad_up_s[LOW:LANES, lanes].astype(BF16)
        table = vectors_ref[quarter * share : (quarter + 1) * share]
        for other in range(2):
            at = slice((2 * (quarter % 2) + other) * share, (2 * (quarter % 2) + other + 1) * share)
            column = vectors_ref[at, gate_at : gate_at + 1] if quarter < quarters // 2 else up_columns_s[at, 0:1]
            table = jnp.where(lane == gate_at + other, column, table)
        pack_ref[quarter, channels : channels + share] = table.astype(BF16)
        pack_ref[quarter, channels + share : channels + share + 16] = lines_s[:, lanes].astype(BF16)


def merge_kernel(joined_ref, branch_ref, cot_ref, up_ref, pack_out):
    pack_ref = pack_out.buffer
    cot_ref = cot_ref()
    quarters, first, _ = up_ref.shape
    sources, _, rows = joined_ref.shape
    merge_rows = 2 * D // sources
    head_rows = D // sources
    grad_merge = jnp.zeros((merge_rows, D), F32)
    grad_head = jnp.zeros((head_rows, D), F32)
    for source in range(sources):
        at = slice(source * rows, (source + 1) * rows)
        joined = joined_ref[source]
        grad_merge = grad_merge + dot_nn(joined[:merge_rows], cot_ref[at])
        grad_head = grad_head + dot_nn(joined[merge_rows : merge_rows + head_rows], branch_ref[at])
    pack_ref[:, :first] = up_ref[...]
    for quarter in range(quarters):
        base = first
        for grad in (grad_merge, grad_head):
            share = grad.shape[0] // quarters
            for tile in range(4):
                pack_ref[quarter, base : base + share] = grad[
                    quarter * share : (quarter + 1) * share, tile * LANES : (tile + 1) * LANES
                ].astype(BF16)
                base += share


def output_kernel(
    x_ref, mixed_ref, head_ref, down_ref, down_bias_ref, merge_ref, merge_bias_ref, out_ref, joined_out
):
    sources = mixed_ref.shape[0]
    rows = x_ref.shape[0]
    channels = HALF // sources
    share = channels // 4
    attn_parts = []
    branch_attn = jnp.zeros((rows, D), F32)
    branch_mlp = jnp.zeros((rows, D), F32)
    for source in range(sources):
        attn = turn(mixed_ref[source, :rows, LANES:].astype(F32))[:, :HEAD].astype(BF16)
        attn_parts.append(attn)
        branch_attn = branch_attn + dot_nn(attn, head_ref[source * HEAD : (source + 1) * HEAD])
        down = jnp.concatenate(
            [down_ref[(part * sources + source) * share : (part * sources + source + 1) * share] for part in range(4)],
            axis=0,
        )
        branch_mlp = branch_mlp + dot_nn(mixed_ref[source, :rows, :channels], down)
    joined = jnp.concatenate(
        [branch_attn.astype(BF16), (branch_mlp + line_of(down_bias_ref)).astype(BF16)], axis=1
    )
    result = x_ref[...].astype(F32) + dot_nn(joined, merge_ref[...]) + line_of(merge_bias_ref)
    out_ref[...] = result.astype(BF16)
    turned = jnp.transpose(joined.astype(F32))
    heads = jnp.transpose(jnp.concatenate(attn_parts, axis=1).astype(F32))
    merge_share = turned.shape[0] // (4 * sources)
    head_share = heads.shape[0] // (4 * sources)
    used = 4 * (merge_share + head_share)
    for target in range(sources):
        for part in range(4):
            at = (part * sources + target) * merge_share
            joined_out[target, part * merge_share : (part + 1) * merge_share] = turned[
                at : at + merge_share
            ].astype(BF16)
            at = (part * sources + target) * head_share
            to = 4 * merge_share + part * head_share
            joined_out[target, to : to + head_share] = heads[at : at + head_share].astype(BF16)
        joined_out[target, used:] = jnp.zeros((joined_out.shape[1] - used, rows), BF16)


def pair_kernel(same_ref, other_ref, *out_refs):
    for slot, out_ref in enumerate(out_refs):
        out_ref[...] = (same_ref[slot].astype(F32) + other_ref[slot].astype(F32)).astype(BF16)


def frames_kernel(x_ref, cot_ref, *refs):
    total_refs, out_ref = refs[:-1], refs[-1]
    for part in range(x_ref.shape[0] // 32):
        rows = slice(part * 32, part * 32 + 32)
        inputs = x_ref[rows].astype(F32)
        mean = jnp.mean(inputs, axis=-1, keepdims=True)
        centred = inputs - mean
        rate = lax.rsqrt(jnp.mean(centred * centred, axis=-1, keepdims=True) + EPS)
        hat = centred * rate
        grad = total_refs[0][rows].astype(F32)
        for total_ref in total_refs[1:]:
            grad = grad + total_ref[rows].astype(F32)
        plain = jnp.mean(grad, axis=-1, keepdims=True)
        along = jnp.mean(grad * hat, axis=-1, keepdims=True)
        out_ref[rows] = cot_ref[rows].astype(F32) + rate * (grad - plain - hat * along)


def add_kernel(*refs):
    out_ref = refs[-1]
    first = 0
    for at in range(0, len(refs) - 1, 4):
        total = refs[at][...].astype(F32)
        for ref in refs[at + 1 : at + 4]:
            total = total + ref[...].astype(F32)
        out_ref[first : first + total.shape[0]] = total.astype(BF16)
        first += total.shape[0]


def gather_parts(near_ref, far_ref, all_s):
    place = lax.axis_index("tm")
    for apart in range(all_s.shape[0]):
        part_ref = far_ref if apart % 2 else near_ref
        all_s[lax.bitwise_xor(jnp.int32(apart), place)] = part_ref[apart // 2]


def lines_from(all_s, base, size):
    return jnp.concatenate([all_s[source, base : base + size] for source in range(all_s.shape[0])], axis=0).astype(F32)


def add_streams_kernel(parts_ref, out_ref):
    total = parts_ref[0].astype(F32)
    for source in range(1, parts_ref.shape[0]):
        total = total + parts_ref[source].astype(F32)
    out_ref[...] = total.astype(BF16)


def early_kernel(near_ref, far_ref, qkv_out, pos_out, down_out, up_out, all_s):
    gather_parts(near_ref, far_ref, all_s)
    sources = all_s.shape[0]
    share = HALF // (4 * sources)
    for kind in range(4):
        lines = jnp.transpose(lines_from(all_s, kind * HEAD, HEAD))
        if kind < 3:
            qkv_out[:, kind * D : (kind + 1) * D] = lines
        else:
            pos_out[...] = lines
    base = 4 * HEAD
    for source in range(sources):
        for tile in range(4):
            down_out[source * share : (source + 1) * share, tile * LANES : (tile + 1) * LANES] = all_s[
                source, base + tile * share : base + (tile + 1) * share
            ].astype(F32)
    wide = sources * share
    for group in range(4):
        up_out.buffer[:, group * wide : (group + 1) * wide] = jnp.transpose(
            lines_from(all_s, base + 4 * share + group * share, share)
        )


def late_kernel(*refs):
    _, near_ref, far_ref = refs[:3]
    (
        attn_gain_out,
        attn_bias_out,
        mlp_gain_out,
        mlp_bias_out,
        content_out,
        position_out,
        outw_out,
        up_out,
        up_bias_out,
        gain_out,
        bias_out,
        taps_out,
        conv_bias_out,
        down_bias_out,
        merge_out,
        merge_bias_out,
        all_s,
    ) = refs[3:]
    gather_parts(near_ref, far_ref, all_s)
    sources = all_s.shape[0]
    channels = HALF // sources
    share = channels // 4
    base = 0
    for group in range(4):
        at = group * sources * share
        up_out.buffer[:, at : at + sources * share] = jnp.transpose(lines_from(all_s, base + group * share, share))
    up_out.go()
    table = jnp.transpose(lines_from(all_s, base + channels, share))
    taps_out[...] = table[:KERNEL]
    conv_bias_out[...] = table[KERNEL]
    gain_out[...] = table[KERNEL + 1]
    bias_out[...] = table[KERNEL + 2]
    wide = sources * share
    up_bias_out[:wide] = table[KERNEL + 3]
    up_bias_out[wide:] = table[KERNEL + 4]
    base = base + channels + share
    lines = all_s[0, base : base + 16].astype(F32)
    for source in range(1, sources):
        lines = lines + all_s[source, base : base + 16].astype(F32)
    outs = (attn_gain_out, attn_bias_out, mlp_gain_out, mlp_bias_out, content_out, position_out, down_bias_out, merge_bias_out)
    for line, out in enumerate(outs):
        out[...] = lines[line]
    base = base + 16
    merge_share = 2 * D // (4 * sources)
    head_share = D // (4 * sources)
    for source in range(sources):
        for tile in range(4):
            lanes = slice(tile * LANES, (tile + 1) * LANES)
            at = base + tile * merge_share
            merge_out[source * merge_share : (source + 1) * merge_share, lanes] = all_s[
                source, at : at + merge_share
            ].astype(F32)
            at = base + 4 * merge_share + tile * head_share
            outw_out[source * head_share : (source + 1) * head_share, lanes] = all_s[
                source, at : at + head_share
            ].astype(F32)


def moved(block, axis, bits):
    count = lax.axis_size(axis)
    return lax.ppermute(block, axis, [(index, index ^ bits) for index in range(count)])


def over_streams(packs):
    return [packs[0]] + [moved(packs[bits], "stream", bits) for bits in range(1, lax.axis_size("stream"))]


def near_blocks(block):
    return [block] + [moved(block, "tm", bits) for bits in range(2, lax.axis_size("tm"), 2)]


def far_blocks(near):
    far = [moved(part, "tm", 1) for part in near]
    return [part for pair in zip(near, far) for part in pair]


def far_stack(near):
    stack = jnp.stack(near)
    return stack, moved(stack, "tm", 1)


def head_device(
    frames,
    lengths,
    cotangent,
    ln_attn_gain,
    ln_attn_bias,
    ln_mlp_gain,
    ln_mlp_bias,
    qkv_weight,
    content_bias,
    position_bias,
    pos_weight,
    out_weight,
    up_weight,
    up_bias,
    gate_norm_gain,
    gate_norm_bias,
    conv_kernel,
    conv_bias,
    down_weight,
    down_bias,
    merge_weight,
    merge_bias,
):
    count = lax.axis_size("tm")
    quarters = lax.axis_size("stream")
    own = frames.shape[1]
    total = own * count
    folded = total + total // 2
    padded = folded + 4 * MARGIN
    share = HALF // (quarters * count)
    channels = HALF // count
    quarter = D // quarters
    own_frames = frames[0]
    own_cotangent = cotangent[0]

    whole, late = Part(), Part(late=True)
    near = near_blocks(jnp.concatenate([own_frames, own_cotangent], axis=1))
    up_own, table, qkv_own, pos_own, bias_own = kernel_call(
        select_kernel,
        [
            ((D, 3 * LANES), BF16),
            ((2, 8 + KERNEL + 1, LANES), F32),
            ((D, 3 * LANES), BF16),
            ((D, LANES), BF16),
            ((8, LANES), F32),
        ],
        10 * "v",
    )(
        up_weight,
        up_bias,
        gate_norm_gain,
        gate_norm_bias,
        conv_bias,
        conv_kernel,
        qkv_weight,
        pos_weight,
        content_bias,
        position_bias,
    )
    near, up_own = lax.optimization_barrier((near, up_own))
    blocks = far_blocks(near)
    frequency = jnp.exp(jnp.arange(D // 2, dtype=F32) * (-2.0 * math.log(10000.0) / D))
    coarse = jnp.arange(0, total, BLOCK, dtype=F32)[:, None] * frequency[None]
    fine = jnp.arange(BLOCK, dtype=F32)[:, None] * frequency[None]
    coarse_table = jnp.concatenate([jnp.sin(coarse), jnp.cos(coarse)], axis=1)
    fine_table = jnp.concatenate([jnp.sin(fine), jnp.cos(fine)], axis=1)

    n_attn, n_mlp, hat, q_position, query, key, value, prob, attn, stats = kernel_call(
        attend_kernel,
        [
            ((total, D), BF16, 1),
            ((total, D), BF16, 1),
            ((total, D), BF16, 1),
            ((total, LANES), BF16, 1),
            ((total, LANES + D), BF16, 1),
            ((total, LANES + D), BF16, 1),
            ((total, LANES), BF16, 1),
            ((total, total), BF16, 1),
            ((total, LANES), F32, 1),
            ((total, LANES), F32, 1),
        ],
        [
            "s",
            blocks_part(0),
            *"vvvvvvvvv",
            Part((D, HALF), lambda refs, buffer: [(refs[0].at[:, pl.ds(HALF, HALF)], buffer)], late=True),
            "v",
        ],
        bounds=True,
    )(
        lengths,
        *blocks,
        ln_attn_gain,
        ln_attn_bias,
        ln_mlp_gain,
        ln_mlp_bias,
        qkv_own,
        pos_own,
        bias_own,
        coarse_table,
        fine_table,
        up_weight,
        up_bias,
    )

    def own_down(refs, buffer):
        place = lax.axis_index("tm")
        stride = HALF // quarters
        return [
            (
                refs[0].at[pl.ds(pl.multiple_of(part * stride + share * place, 16), share)],
                buffer.at[pl.ds(part * share, share)],
            )
            for part in range(quarters)
        ]

    mixed, gate_pre, grad_y, slope, gate_hat, early_pack, vectors, first_lines = kernel_call(
        mlp_first_kernel,
        [
            ((count, own + 16, 2 * LANES), BF16, 1),
            ((folded, LANES), BF16, 1),
            ((folded, LANES), BF16, 1),
            ((folded, LANES), BF16, 1),
            ((folded, LANES), BF16, 1),
            ((quarters, 8 * share, LANES), BF16, 1),
            ((channels, LANES), F32),
            ((8, D), F32),
        ],
        [
            "s",
            whole,
            "v",
            "v",
            whole,
            blocks_part(1, late=True),
            rows_part(D, D, late=True),
            Part((2 * LANES, D), own_down, late=True),
            Part(late=True),
        ],
        [
            ((folded, LANES), F32),
            ((folded, LANES), F32),
            ((total, 2 * LANES), BF16),
            ((folded, LANES), F32),
            ((folded, LANES), F32),
            ((8, padded + WINDOW, LANES), F32),
            ((8, padded + WINDOW, LANES), F32),
            ((folded, LANES), F32),
            ((folded, LANES), F32),
            ((total, D), BF16),
            ((total, 2 * LANES), BF16),
            ((2, 32, 8, LANES), F32),
            ((2, 32, 8, LANES), F32),
            ((2, 32, 8, LANES), F32),
            ((total, LANES), F32),
        ],
        bounds=True,
    )(lengths, n_mlp, up_own, table, stats, *blocks, merge_weight, down_weight, attn)
    mixed_own = lax.all_to_all(mixed, "tm", 0, 0, tiled=True)

    def own_head(refs, buffer):
        at = pl.ds(pl.multiple_of(lax.axis_index("tm") * HEAD, HEAD), HEAD)
        return [(refs[0].at[at], buffer.at[pl.ds(0, HEAD)])]

    branch, from_attn, *head_packs, head_lines = kernel_call(
        attend_back_kernel,
        [
            ((total, D), BF16, 1),
            ((total, D), BF16, 1),
            *([((4 * HEAD + 8 * share, LANES), BF16, 1)] * quarters),
            ((8, D), F32),
        ],
        [
            blocks_part(1),
            rows_part(0, D),
            Part((LANES, D), own_head),
            whole,
            late,
            late,
            late,
            "v",
            "v",
            late,
            Part((total, LANES), lambda refs, buffer: [(refs[0].at[:, pl.ds(0, LANES)], buffer)], late=True),
            late,
            late,
            late,
            late,
            "v",
            late,
        ],
        [
            ((total, LANES), BF16),
            ((total, total), BF16),
            ((total, D), BF16),
            ((total, 3 * LANES), BF16),
            ((4 * HEAD, D), F32),
        ],
    )(
        *blocks,
        merge_weight,
        out_weight,
        attn,
        value,
        prob,
        key,
        coarse_table,
        fine_table,
        pos_own,
        query,
        n_attn,
        q_position,
        qkv_own,
        hat,
        ln_attn_gain,
        early_pack,
    )
    head_parts = over_streams(head_packs)
    mixed_own, _ = lax.optimization_barrier((mixed_own, head_lines))
    out_rows, joined = kernel_call(
        output_kernel,
        [((own, D), BF16), ((count, 256, own), BF16)],
        "vvvvvvv",
        megas=24,
    )(own_frames, mixed_own, out_weight, down_weight, down_bias, merge_weight, merge_bias)
    joined_all = lax.all_to_all(joined, "tm", 0, 0, tiled=True)
    gate_pre, _ = lax.optimization_barrier((gate_pre, joined))
    up_rows = 5 * share + 16
    late_rows = up_rows + 3 * D // count
    same, apart, up_pack = kernel_call(
        mlp_second_kernel,
        [((count // 2, own, D), BF16, 1)] * 2 + [((quarters, up_rows, LANES), BF16, 1)],
        [
            Part(
                (count, 2 * total // BLOCK, 2 * LANES),
                lambda refs, buffer: [(refs[0].at[:, pl.ds(own, 2 * total // BLOCK)], buffer)],
            ),
            *([whole] * 4),
            late,
            late,
            "v",
            late,
            late,
            *"vvv",
        ],
        [
            ((total, 3 * LANES), BF16),
            ((total, LANES), F32),
            ((2 * LANES, D), F32),
            ((16, D), F32),
            ((channels, LANES), F32),
        ],
    )(
        mixed_own,
        gate_pre,
        grad_y,
        slope,
        gate_hat,
        up_own,
        hat,
        ln_mlp_gain,
        from_attn,
        n_mlp,
        vectors,
        first_lines,
        head_lines,
    )
    (late_pack,) = kernel_call(
        merge_kernel, [((quarters, late_rows, LANES), BF16, 1)], ["f", "f", blocks_part(1), "f"]
    )(joined_all, branch, *blocks, up_pack)
    late_pack, head_parts = lax.optimization_barrier((late_pack, head_parts))
    late_moved = lax.all_to_all(late_pack, "stream", 0, 0, tiled=True)
    sibling = moved(apart, "tm", 1)
    (early_part,) = kernel_call(add_kernel, [((4 * HEAD + 8 * share, LANES), BF16)], quarters * "v", megas=24)(
        *head_parts
    )
    early_near = near_blocks(early_part)
    pairs = kernel_call(pair_kernel, [((own, D), BF16)] * (count // 2), "vv", megas=24)(same, sibling)
    sums = [pairs[0]] + [moved(pairs[slot], "tm", 2 * slot) for slot in range(1, count // 2)]
    late_moved, early_near, sums = lax.optimization_barrier((late_moved, early_near, sums))
    (late_part,) = kernel_call(add_streams_kernel, [((late_rows, LANES), BF16)], "v", megas=24)(late_moved)
    late_near = near_blocks(late_part)
    early_all = far_stack(early_near)
    (grad_frames,) = kernel_call(frames_kernel, [((own, D), F32)], (2 + count // 2) * "v", megas=24)(
        own_frames, own_cotangent, *sums
    )
    grad_qkv, grad_pos, grad_down, half_up = kernel_call(
        early_kernel,
        [
            ((quarter, 3 * D), F32),
            ((quarter, D), F32),
            ((HALF // quarters, D), F32),
            ((quarter, 2 * HALF), F32, 1, (quarter, HALF), lambda ref: ref.at[:, pl.ds(0, HALF)]),
        ],
        "vv",
        [((count, 4 * HEAD + 8 * share, LANES), BF16)],
        megas=24,
    )(*early_all)
    late_near, grad_frames, grad_pos = lax.optimization_barrier((late_near, grad_frames, grad_pos))
    late_parts = far_stack(late_near)
    late = kernel_call(
        late_kernel,
        [((quarter,), F32)] * 6
        + [
            ((quarter, D), F32),
            ((quarter, 2 * HALF), F32, 1, (quarter, HALF), lambda ref: ref.at[:, pl.ds(HALF, HALF)]),
            ((2 * HALF // quarters,), F32),
            ((HALF // quarters,), F32),
            ((HALF // quarters,), F32),
            ((KERNEL, HALF // quarters), F32),
            ((HALF // quarters,), F32),
            ((quarter,), F32),
            ((2 * D // quarters, D), F32),
            ((quarter,), F32),
        ],
        "kvv",
        [((count,) + late_part.shape, BF16)],
        megas=24,
        aliases={0: 7},
    )(half_up, *late_parts)
    return (
        out_rows[None],
        grad_frames[None],
        *late[:4],
        grad_qkv,
        *late[4:6],
        grad_pos,
        *late[6:13],
        grad_down,
        *late[13:],
    )


def per_device(*operands):
    fits = (
        lax.axis_size("tm") == HEADS
        and lax.axis_size("stream") * LANES == D
        and operands[0].shape[1] == BLOCK
    )
    return head_device(*operands) if fits else frame_device(*operands)


def solution(mesh):
    return jax.shard_map(
        per_device,
        mesh=mesh,
        in_specs=(
            P("stream", "tm", None),
            P("stream", None),
            P("stream", "tm", None),
            P(),
            P(),
            P(),
            P(),
            P(),
            P(),
            P(),
            P(),
            P(),
            P(),
            P(),
            P(),
            P(),
            P(),
            P(),
            P(),
            P(),
            P(),
            P(),
        ),
        out_specs=(
            P("stream", "tm", None),
            P("stream", "tm", None),
            P("stream"),
            P("stream"),
            P("stream"),
            P("stream"),
            P("stream", None),
            P("stream"),
            P("stream"),
            P("stream", None),
            P("stream", None),
            P("stream", None),
            P("stream"),
            P("stream"),
            P("stream"),
            P(None, "stream"),
            P("stream"),
            P("stream", None),
            P("stream"),
            P("stream", None),
            P("stream"),
        ),
        check_vma=False,
    )
```

profile of v0, /device:TPU:0, one launch (start us, length us, event | category | flops | bytes accessed | tf_op | source)
XLA Modules:
  0.0 133.4 jit_solution(12201538175806066655)
XLA Ops:
  1.7 4.0 %collective-permute-start.2 = (bf16[128,1024]{1,0:T(8,128)(2,1)S(1)}, bf16[128,1024]{1,0:T(8,128)(2,1)S(1)}, u32[]{:S(2)}, u32[]{:S(2)}) collective-permute-start(bf16[128,1024]{1,0:T(8,128)(2,1)S(1)} %pad_maximum_fusion.2.refs_1_.refs_5_.refs_0_.refs_2_), channel_id=1, source_target_pairs={{0,6},{1,7},{2,4},{3,5},{4,2},{5,3},{6,0},{7,1},{8,14},{9,15},{10,... | collective-permute-start | bytes 786440 | tf_op jit(solution)/shard_map/ppermute | solution.py:1784
  6.3 5.5 %shard_map.373 = (bf16[512,384]{1,0:T(8,128)(2,1)}, f32[2,40,128]{2,1,0:T(8,128)}, bf16[512,384]{1,0:T(8,128)(2,1)}, bf16[512,128]{1,0:T(8,128)(2,1)}, f32[8,128]{1,0:T(8,128)}) custom-call(bf16[512,3072]{1,0:T(8,128)(2,1)} %refs_18_.1, bf16[3072]{0:T(1024)(128)(2,1)} %refs_19_.1, bf16[1536]{0:T(1024)(128)(2,1)} %refs_2_.2, bf16[1536]{0:T(1024)(128)(2,1)} %refs_3_.2, ...), custom_call_target="tpu_custom_call" | custom-call | tf_op jit(solution)/shard_map/pallas_call | solution.py:740
  12.8 4.7 %collective-permute-done.1.refs_5_.refs_9_.refs_4_.refs_6_ = bf16[128,1024]{1,0:T(8,128)(2,1)S(1)} collective-permute-done((bf16[128,1024]{1,0:T(8,128)(2,1)S(1)}, bf16[128,1024]{1,0:T(8,128)(2,1)S(1)}, u32[]{:S(2)}, u32[]{:S(2)}) %collective-permute-start.1) | collective-permute-done | bytes 262176 | tf_op jit(solution)/shard_map/ppermute | solution.py:1784
  21.3 12.8 %shard_map.374 = (bf16[1024,512]{1,0:T(8,128)(2,1)}, bf16[1024,512]{1,0:T(8,128)(2,1)}, bf16[1024,512]{1,0:T(8,128)(2,1)}, bf16[1024,128]{1,0:T(8,128)(2,1)}, bf...) custom-call(s32[1,5]{1,0:T(1,128)} %refs_0_.5, ...), custom_call_target="tpu_custom_call" | custom-call | tf_op jit(solution)/shard_map/pallas_call | solution.py:740
  34.2 18.6 %shard_map.375 = (bf16[8,144,256]{2,1,0:T(8,128)(2,1)}, bf16[1536,128]{1,0:T(8,128)(2,1)}, bf16[1536,128]{1,0:T(8,128)(2,1)}, bf16[1536,128]{1,0:T(8,128)(2,1)},...) custom-call(s32[1,5]{1,0:T(1,128)} %refs_0_.5, ...), custom_call_target="tpu_custom_call" | custom-call | tf_op jit(solution)/shard_map/pallas_call | solution.py:740
  52.8 3.8 %all-to-all-start = ((bf16[8,144,256]{2,1,0:T(8,128)(2,1)}), bf16[8,144,256]{2,1,0:T(8,128)(2,1)S(1)}, u32[]{:S(2)}, u32[]{:S(2)}) async-start(bf16[8,144,256]{2,1,0:T(8,128)(2,1)} %get-tuple-element.120), calls=%async_computation | async-start | bytes 1179648 | tf_op jit(solution)/shard_map/all_to_all | solution.py:1964
  56.6 12.6 %shard_map.376 = (bf16[1024,512]{1,0:T(8,128)(2,1)}, bf16[1024,512]{1,0:T(8,128)(2,1)}, bf16[640,128]{1,0:T(8,128)(2,1)}, bf16[640,128]{1,0:T(8,128)(2,1)}, bf16...) custom-call(bf16[128,1024]{1,0:T(8,128)(2,1)} %copy-done.11, bf16[128,1024]{1,0:T(8,128)(2,1)} %copy-done.15, ...), custom_call_target="tpu_custom_call" | custom-call | tf_op jit(solution)/shard_map/pallas_call | solution.py:740
  70.5 2.5 %shard_map.377 = (bf16[128,512]{1,0:T(8,128)(2,1)}, bf16[8,256,128]{2,1,0:T(8,128)(2,1)S(1)}) custom-call(bf16[128,512]{1,0:T(8,128)(2,1)S(1)} %bitcast.13, bf16[8,144,256]{2,1,0:T(8,128)(2,1)S(1)} %all-to-all-done.refs_1_.refs_0_, bf16[512,512]{1,0:T(8,128)(2,1)S(1)} %copy-done.3, bf16[1536,512]{1,0:T(8,128)(2,1)S(1)} %copy-done.1, ...), custom_call_target="tpu_custom_call" | custom-call | tf_op jit(solution)/shard_map/pallas_call | solution.py:740
  73.8 3.9 %all-to-all-start.1 = ((bf16[8,256,128]{2,1,0:T(8,128)(2,1)}), bf16[8,256,128]{2,1,0:T(8,128)(2,1)S(1)}, u32[]{:S(2)}, u32[]{:S(2)}) async-start(bf16[8,256,128]{2,1,0:T(8,128)(2,1)} %copy-done.6), calls=%async_computation.1 | async-start | bytes 1048576 | tf_op jit(solution)/shard_map/all_to_all | solution.py:2031
  77.7 2.4 %collective-permute-start.8 = (bf16[640,128]{1,0:T(8,128)(2,1)}, bf16[640,128]{1,0:T(8,128)(2,1)S(1)}, u32[]{:S(2)}, u32[]{:S(2)}) collective-permute-start(bf16[640,128]{1,0:T(8,128)(2,1)} %get-tuple-element.145), channel_id=1, source_target_pairs={{0,16},{8,24},{16,0},{24,8},{1,17},{9,25},{17,1},{25,9},{2,18},{10... | collective-permute-start | bytes 491528 | tf_op jit(solution)/shard_map/ppermute | solution.py:1784
  80.1 2.0 %collective-permute-start.9 = (bf16[640,128]{1,0:T(8,128)(2,1)S(1)}, bf16[640,128]{1,0:T(8,128)(2,1)S(1)}, u32[]{:S(2)}, u32[]{:S(2)}) collective-permute-start(bf16[640,128]{1,0:T(8,128)(2,1)S(1)} %copy-done.21), channel_id=1, source_target_pairs={{0,24},{8,16},{16,8},{24,0},{1,25},{9,17},{17,9},{25,1},{2,26},{10... | collective-permute-start | bytes 491528 | tf_op jit(solution)/shard_map/ppermute | solution.py:1784
  82.1 9.1 %shard_map.378 = (bf16[4,128,512]{2,1,0:T(8,128)(2,1)}, bf16[4,128,512]{2,1,0:T(8,128)(2,1)}, bf16[4,256,128]{2,1,0:T(8,128)(2,1)}) custom-call(bf16[8,144,256]{2,1,0:T(8,128)(2,1)} %copy-done.2, bf16[1536,128]{1,0:T(8,128)(2,1)} %get-tuple-element.135.refs_1_, bf16[1536,128]{1,0:T(8,128)(2,1)} %get-tuple-element.136.refs_2_, ...), custom_call_target="tpu_custom_call" | custom-call | tf_op jit(solution)/shard_map/pallas_call | solution.py:740
  92.0 4.0 %shard_map.379 = bf16[4,448,128]{2,1,0:T(8,128)(2,1)} custom-call(bf16[8,256,128]{2,1,0:T(8,128)(2,1)} %copy-done.19, bf16[1024,512]{1,0:T(8,128)(2,1)} %get-tuple-element.133.refs_1_, bf16[128,1024]{1,0:T(8,128)(2,1)} %copy-done.11, bf16[128,1024]{1,0:T(8,128)(2,1)} %copy-done.15, bf16[128,1024]{1,0:T(8,128)(2,1)} %copy-done.14, ...), custom_call_target="tpu_custom_call" | custom-call | tf_op jit(solution)/shard_map/pallas_call | solution.py:740
  96.0 3.9 %all-to-all-start.2 = ((bf16[4,448,128]{2,1,0:T(8,128)(2,1)}), bf16[4,448,128]{2,1,0:T(8,128)(2,1)S(1)}, u32[]{:S(2)}, u32[]{:S(2)}) async-start(bf16[4,448,128]{2,1,0:T(8,128)(2,1)} %shard_map.379), calls=%async_computation.2 | async-start | bytes 917504 | tf_op jit(solution)/shard_map/all_to_all | solution.py:2077
  101.0 3.0 %collective-permute-start.12 = (bf16[640,128]{1,0:T(8,128)(2,1)S(1)}, bf16[640,128]{1,0:T(8,128)(2,1)S(1)}, u32[]{:S(2)}, u32[]{:S(2)}) collective-permute-start(bf16[640,128]{1,0:T(8,128)(2,1)S(1)} %shard_map.380), channel_id=1, source_target_pairs={{0,6},{1,7},{2,4},{3,5},{4,2},{5,3},{6,0},{7,1},{8,14},{9,15},{10,... | collective-permute-start | bytes 491528 | tf_op jit(solution)/shard_map/ppermute | solution.py:1784
  105.6 2.0 %collective-permute-start.14 = (bf16[128,512]{1,0:T(8,128)(2,1)S(1)}, bf16[128,512]{1,0:T(8,128)(2,1)S(1)}, u32[]{:S(2)}, u32[]{:S(2)}) collective-permute-start(bf16[128,512]{1,0:T(8,128)(2,1)S(1)} %get-tuple-element.155), channel_id=1, source_target_pairs={{0,2},{1,3},{2,0},{3,1},{4,6},{5,7},{6,4},{7,5},{8,10},{9,11},{10,... | collective-permute-start | bytes 393224 | tf_op jit(solution)/shard_map/ppermute | solution.py:1784
  109.1 2.8 %collective-permute-start.16 = (bf16[128,512]{1,0:T(8,128)(2,1)S(1)}, bf16[128,512]{1,0:T(8,128)(2,1)S(1)}, u32[]{:S(2)}, u32[]{:S(2)}) collective-permute-start(bf16[128,512]{1,0:T(8,128)(2,1)S(1)} %get-tuple-element.157), channel_id=1, source_target_pairs={{0,6},{1,7},{2,4},{3,5},{4,2},{5,3},{6,0},{7,1},{8,14},{9,15},{10,... | collective-permute-start | bytes 393224 | tf_op jit(solution)/shard_map/ppermute | solution.py:1784
  113.0 2.8 %collective-permute-done.14.refs_3_ = bf16[128,512]{1,0:T(8,128)(2,1)S(1)} collective-permute-done((bf16[128,512]{1,0:T(8,128)(2,1)S(1)}, bf16[128,512]{1,0:T(8,128)(2,1)S(1)}, u32[]{:S(2)}, u32[]{:S(2)}) %collective-permute-start.14) | collective-permute-done | bytes 131104 | tf_op jit(solution)/shard_map/ppermute | solution.py:1784
  115.8 2.1 %collective-permute-done.16.refs_5_ = bf16[128,512]{1,0:T(8,128)(2,1)S(1)} collective-permute-done((bf16[128,512]{1,0:T(8,128)(2,1)S(1)}, bf16[128,512]{1,0:T(8,128)(2,1)S(1)}, u32[]{:S(2)}, u32[]{:S(2)}) %collective-permute-start.16) | collective-permute-done | bytes 131104 | tf_op jit(solution)/shard_map/ppermute | solution.py:1784
  119.1 2.7 %collective-permute-start.19 = (bf16[448,128]{1,0:T(8,128)(2,1)S(1)}, bf16[448,128]{1,0:T(8,128)(2,1)S(1)}, u32[]{:S(2)}, u32[]{:S(2)}) collective-permute-start(bf16[448,128]{1,0:T(8,128)(2,1)S(1)} %shard_map.382), channel_id=1, source_target_pairs={{0,6},{1,7},{2,4},{3,5},{4,2},{5,3},{6,0},{7,1},{8,14},{9,15},{10,... | collective-permute-start | bytes 344072 | tf_op jit(solution)/shard_map/ppermute | solution.py:1784
  122.6 1.9 %shard_map.383 = f32[128,512]{1,0:T(8,128)} custom-call(bf16[128,512]{1,0:T(8,128)(2,1)S(1)} %bitcast.14, bf16[128,512]{1,0:T(8,128)(2,1)S(1)} %bitcast.17, bf16[128,512]{1,0:T(8,128)(2,1)S(1)} %get-tuple-element.159.refs_2_, bf16[128,512]{1,0:T(8,128)(2,1)S(1)} %collective-permute-done.14.refs_3_, bf16[128,512]{1,0:T(8,128)(2,1)S(1)} %collective-permute-done.15.refs_4_, ...), custom_call_target="tpu_custom_call" | custom-call | tf_op jit(solution)/shard_map/pallas_call | solution.py:740
  124.5 3.4 %shard_map.384 = (f32[128,1536]{1,0:T(8,128)}, f32[128,512]{1,0:T(8,128)}, f32[384,512]{1,0:T(8,128)}, f32[128,3072]{1,0:T(8,128)}) custom-call(bf16[4,640,128]{2,1,0:T(8,128)(2,1)S(1)} %pad_maximum_fusion.refs_0_, bf16[4,640,128]{2,1,0:T(8,128)(2,1)S(1)} %collective-permute-done.20.refs_1_), custom_call_target="tpu_custom_call" | custom-call | tf_op jit(solution)/shard_map/pallas_call | solution.py:740
  128.5 1.8 %collective-permute-done.21.refs_2_ = bf16[4,448,128]{2,1,0:T(8,128)(2,1)S(1)} collective-permute-done((bf16[4,448,128]{2,1,0:T(8,128)(2,1)S(1)}, bf16[4,448,128]{2,1,0:T(8,128)(2,1)S(1)}, u32[]{:S(2)}, u32[]{:S(2)}) %collective-permute-start.21) | collective-permute-done | bytes 458784 | tf_op jit(solution)/shard_map/ppermute | solution.py:1784
  130.3 2.9 %shard_map.385 = (f32[128]{0:T(128)}, f32[128]{0:T(128)}, f32[128]{0:T(128)}, f32[128]{0:T(128)}, f32[128]{0:T(128)}, /*index=5*/f32[128]{0:T(128)}, f32[128,512...) custom-call(f32[128,3072]{1,0:T(8,128)} %get-tuple-element.169.refs_, ...), custom_call_target="tpu_custom_call", output_to_operand_aliasing={{7}: (0, {})} | custom-call | tf_op jit(solution)/shard_map/pallas_call | solution.py:740
  (92 shorter events, 17.0 us)
Async XLA Ops:
  1.7 11.1 %collective-permute-start.2 = (bf16[128,1024]{1,0:T(8,128)(2,1)S(1)}, bf16[128,1024]{1,0:T(8,128)(2,1)S(1)}, u32[]{:S(2)}, u32[]{:S(2)}) collective-permute-start(bf16[128,1024]{1,0:T(8,128)(2,1)S(1)} %pad_maximum_fusion.2.refs_1_.refs_5_.refs_0_.refs_2_), channel_id=1, source_target_pairs={{0,6},{1,7},{2,4},{3,5},{4,2},{5,3},{6,0},{7,1},{8,14},{9,15},{10,... | collective-permute-start | bytes 786440 | tf_op jit(solution)/shard_map/ppermute | solution.py:1784
  5.6 11.9 %collective-permute-start.1 = (bf16[128,1024]{1,0:T(8,128)(2,1)S(1)}, bf16[128,1024]{1,0:T(8,128)(2,1)S(1)}, u32[]{:S(2)}, u32[]{:S(2)}) collective-permute-start(bf16[128,1024]{1,0:T(8,128)(2,1)S(1)} %pad_maximum_fusion.2.refs_1_.refs_5_.refs_0_.refs_2_), channel_id=1, source_target_pairs={{0,4},{1,5},{2,6},{3,7},{4,0},{5,1},{6,2},{7,3},{8,12},{9,13},{10,... | collective-permute-start | bytes 786440 | tf_op jit(solution)/shard_map/ppermute | solution.py:1784
  6.1 11.7 %collective-permute-start = (bf16[128,1024]{1,0:T(8,128)(2,1)S(1)}, bf16[128,1024]{1,0:T(8,128)(2,1)S(1)}, u32[]{:S(2)}, u32[]{:S(2)}) collective-permute-start(bf16[128,1024]{1,0:T(8,128)(2,1)S(1)} %pad_maximum_fusion.2.refs_1_.refs_5_.refs_0_.refs_2_), channel_id=1, source_target_pairs={{0,2},{1,3},{2,0},{3,1},{4,6},{5,7},{6,4},{7,5},{8,10},{9,11},{10,... | collective-permute-start | bytes 786440 | tf_op jit(solution)/shard_map/ppermute | solution.py:1784
  17.8 2.5 %collective-permute-start.3 = (bf16[128,1024]{1,0:T(8,128)(2,1)S(1)}, bf16[128,1024]{1,0:T(8,128)(2,1)S(1)}, u32[]{:S(2)}, u32[]{:S(2)}) collective-permute-start(bf16[128,1024]{1,0:T(8,128)(2,1)S(1)} %pad_maximum_fusion.2.refs_1_.refs_5_.refs_0_.refs_2_), channel_id=1, source_target_pairs={{0,1},{1,0},{2,3},{3,2},{4,5},{5,4},{6,7},{7,6},{8,9},{9,8},{10,11... | collective-permute-start | bytes 786440 | tf_op jit(solution)/shard_map/ppermute | solution.py:1784
  17.9 2.5 %collective-permute-start.4 = (bf16[128,1024]{1,0:T(8,128)(2,1)S(1)}, bf16[128,1024]{1,0:T(8,128)(2,1)S(1)}, u32[]{:S(2)}, u32[]{:S(2)}) collective-permute-start(bf16[128,1024]{1,0:T(8,128)(2,1)S(1)} %collective-permute-done.refs_3_.refs_7_.refs_2_.refs_4_), channel_id=1, source_target_pairs={{0,1},{1,0},{2,3},{3,2},{4,5},{5,4},{6,7},{7,6},{8,9},{9,8},{10,11... | collective-permute-start | bytes 786440 | tf_op jit(solution)/shard_map/ppermute | solution.py:1784
  18.4 2.0 %collective-permute-start.5 = (bf16[128,1024]{1,0:T(8,128)(2,1)S(1)}, bf16[128,1024]{1,0:T(8,128)(2,1)S(1)}, u32[]{:S(2)}, u32[]{:S(2)}) collective-permute-start(bf16[128,1024]{1,0:T(8,128)(2,1)S(1)} %collective-permute-done.1.refs_5_.refs_9_.refs_4_.refs_6_), channel_id=1, source_target_pairs={{0,1},{1,0},{2,3},{3,2},{4,5},{5,4},{6,7},{7,6},{8,9},{9,8},{10,11... | collective-permute-start | bytes 786440 | tf_op jit(solution)/shard_map/ppermute | solution.py:1784
  18.4 2.1 %collective-permute-start.6 = (bf16[128,1024]{1,0:T(8,128)(2,1)S(1)}, bf16[128,1024]{1,0:T(8,128)(2,1)S(1)}, u32[]{:S(2)}, u32[]{:S(2)}) collective-permute-start(bf16[128,1024]{1,0:T(8,128)(2,1)S(1)} %collective-permute-done.2.refs_7_.refs_11_.refs_6_.refs_8_), channel_id=1, source_target_pairs={{0,1},{1,0},{2,3},{3,2},{4,5},{5,4},{6,7},{7,6},{8,9},{9,8},{10,11... | collective-permute-start | bytes 786440 | tf_op jit(solution)/shard_map/ppermute | solution.py:1784
  52.8 16.4 %all-to-all-start = ((bf16[8,144,256]{2,1,0:T(8,128)(2,1)}), bf16[8,144,256]{2,1,0:T(8,128)(2,1)S(1)}, u32[]{:S(2)}, u32[]{:S(2)}) async-start(bf16[8,144,256]{2,1,0:T(8,128)(2,1)} %get-tuple-element.120), calls=%async_computation | async-start | bytes 1179648 | tf_op jit(solution)/shard_map/all_to_all | solution.py:1964
  73.8 17.3 %all-to-all-start.1 = ((bf16[8,256,128]{2,1,0:T(8,128)(2,1)}), bf16[8,256,128]{2,1,0:T(8,128)(2,1)S(1)}, u32[]{:S(2)}, u32[]{:S(2)}) async-start(bf16[8,256,128]{2,1,0:T(8,128)(2,1)} %copy-done.6), calls=%async_computation.1 | async-start | bytes 1048576 | tf_op jit(solution)/shard_map/all_to_all | solution.py:2031
  77.7 18.3 %collective-permute-start.7 = (bf16[640,128]{1,0:T(8,128)(2,1)}, bf16[640,128]{1,0:T(8,128)(2,1)S(1)}, u32[]{:S(2)}, u32[]{:S(2)}) collective-permute-start(bf16[640,128]{1,0:T(8,128)(2,1)} %get-tuple-element.144), channel_id=1, source_target_pairs={{0,8},{8,0},{16,24},{24,16},{1,9},{9,1},{17,25},{25,17},{2,10},{10... | collective-permute-start | bytes 491528 | tf_op jit(solution)/shard_map/ppermute | solution.py:1784
  77.7 18.3 %collective-permute-start.8 = (bf16[640,128]{1,0:T(8,128)(2,1)}, bf16[640,128]{1,0:T(8,128)(2,1)S(1)}, u32[]{:S(2)}, u32[]{:S(2)}) collective-permute-start(bf16[640,128]{1,0:T(8,128)(2,1)} %get-tuple-element.145), channel_id=1, source_target_pairs={{0,16},{8,24},{16,0},{24,8},{1,17},{9,25},{17,1},{25,9},{2,18},{10... | collective-permute-start | bytes 491528 | tf_op jit(solution)/shard_map/ppermute | solution.py:1784
  80.1 15.9 %collective-permute-start.9 = (bf16[640,128]{1,0:T(8,128)(2,1)S(1)}, bf16[640,128]{1,0:T(8,128)(2,1)S(1)}, u32[]{:S(2)}, u32[]{:S(2)}) collective-permute-start(bf16[640,128]{1,0:T(8,128)(2,1)S(1)} %copy-done.21), channel_id=1, source_target_pairs={{0,24},{8,16},{16,8},{24,0},{1,25},{9,17},{17,9},{25,1},{2,26},{10... | collective-permute-start | bytes 491528 | tf_op jit(solution)/shard_map/ppermute | solution.py:1784
  96.0 21.9 %all-to-all-start.2 = ((bf16[4,448,128]{2,1,0:T(8,128)(2,1)}), bf16[4,448,128]{2,1,0:T(8,128)(2,1)S(1)}, u32[]{:S(2)}, u32[]{:S(2)}) async-start(bf16[4,448,128]{2,1,0:T(8,128)(2,1)} %shard_map.379), calls=%async_computation.2 | async-start | bytes 917504 | tf_op jit(solution)/shard_map/all_to_all | solution.py:2077
  99.9 4.7 %collective-permute-start.13 = (bf16[4,128,512]{2,1,0:T(8,128)(2,1)S(1)}, bf16[4,128,512]{2,1,0:T(8,128)(2,1)S(1)}, u32[]{:S(2)}, u32[]{:S(2)}) collective-permute-start(bf16[4,128,512]{2,1,0:T(8,128)(2,1)S(1)} %copy-done.20), channel_id=1, source_target_pairs={{0,1},{1,0},{2,3},{3,2},{4,5},{5,4},{6,7},{7,6},{8,9},{9,8},{10,11... | collective-permute-start | bytes 1572872 | tf_op jit(solution)/shard_map/ppermute | solution.py:1784
  101.0 8.1 %collective-permute-start.12 = (bf16[640,128]{1,0:T(8,128)(2,1)S(1)}, bf16[640,128]{1,0:T(8,128)(2,1)S(1)}, u32[]{:S(2)}, u32[]{:S(2)}) collective-permute-start(bf16[640,128]{1,0:T(8,128)(2,1)S(1)} %shard_map.380), channel_id=1, source_target_pairs={{0,6},{1,7},{2,4},{3,5},{4,2},{5,3},{6,0},{7,1},{8,14},{9,15},{10,... | collective-permute-start | bytes 491528 | tf_op jit(solution)/shard_map/ppermute | solution.py:1784
  103.9 8.4 %collective-permute-start.11 = (bf16[640,128]{1,0:T(8,128)(2,1)S(1)}, bf16[640,128]{1,0:T(8,128)(2,1)S(1)}, u32[]{:S(2)}, u32[]{:S(2)}) collective-permute-start(bf16[640,128]{1,0:T(8,128)(2,1)S(1)} %shard_map.380), channel_id=1, source_target_pairs={{0,4},{1,5},{2,6},{3,7},{4,0},{5,1},{6,2},{7,3},{8,12},{9,13},{10,... | collective-permute-start | bytes 491528 | tf_op jit(solution)/shard_map/ppermute | solution.py:1784
  104.5 8.5 %collective-permute-start.10 = (bf16[640,128]{1,0:T(8,128)(2,1)S(1)}, bf16[640,128]{1,0:T(8,128)(2,1)S(1)}, u32[]{:S(2)}, u32[]{:S(2)}) collective-permute-start(bf16[640,128]{1,0:T(8,128)(2,1)S(1)} %shard_map.380), channel_id=1, source_target_pairs={{0,2},{1,3},{2,0},{3,1},{4,6},{5,7},{6,4},{7,5},{8,10},{9,11},{10,... | collective-permute-start | bytes 491528 | tf_op jit(solution)/shard_map/ppermute | solution.py:1784
  105.6 10.3 %collective-permute-start.14 = (bf16[128,512]{1,0:T(8,128)(2,1)S(1)}, bf16[128,512]{1,0:T(8,128)(2,1)S(1)}, u32[]{:S(2)}, u32[]{:S(2)}) collective-permute-start(bf16[128,512]{1,0:T(8,128)(2,1)S(1)} %get-tuple-element.155), channel_id=1, source_target_pairs={{0,2},{1,3},{2,0},{3,1},{4,6},{5,7},{6,4},{7,5},{8,10},{9,11},{10,... | collective-permute-start | bytes 393224 | tf_op jit(solution)/shard_map/ppermute | solution.py:1784
  107.6 8.2 %collective-permute-start.15 = (bf16[128,512]{1,0:T(8,128)(2,1)S(1)}, bf16[128,512]{1,0:T(8,128)(2,1)S(1)}, u32[]{:S(2)}, u32[]{:S(2)}) collective-permute-start(bf16[128,512]{1,0:T(8,128)(2,1)S(1)} %get-tuple-element.156), channel_id=1, source_target_pairs={{0,4},{1,5},{2,6},{3,7},{4,0},{5,1},{6,2},{7,3},{8,12},{9,13},{10,... | collective-permute-start | bytes 393224 | tf_op jit(solution)/shard_map/ppermute | solution.py:1784
  109.1 8.9 %collective-permute-start.16 = (bf16[128,512]{1,0:T(8,128)(2,1)S(1)}, bf16[128,512]{1,0:T(8,128)(2,1)S(1)}, u32[]{:S(2)}, u32[]{:S(2)}) collective-permute-start(bf16[128,512]{1,0:T(8,128)(2,1)S(1)} %get-tuple-element.157), channel_id=1, source_target_pairs={{0,6},{1,7},{2,4},{3,5},{4,2},{5,3},{6,0},{7,1},{8,14},{9,15},{10,... | collective-permute-start | bytes 393224 | tf_op jit(solution)/shard_map/ppermute | solution.py:1784
  118.1 6.4 %collective-permute-start.20 = (bf16[4,640,128]{2,1,0:T(8,128)(2,1)S(1)}, bf16[4,640,128]{2,1,0:T(8,128)(2,1)S(1)}, u32[]{:S(2)}, u32[]{:S(2)}) collective-permute-start(bf16[4,640,128]{2,1,0:T(8,128)(2,1)S(1)} %pad_maximum_fusion.refs_0_), channel_id=1, source_target_pairs={{0,1},{1,0},{2,3},{3,2},{4,5},{5,4},{6,7},{7,6},{8,9},{9,8},{10,11... | collective-permute-start | bytes 1966088 | tf_op jit(solution)/shard_map/ppermute | solution.py:1784
  119.1 8.8 %collective-permute-start.19 = (bf16[448,128]{1,0:T(8,128)(2,1)S(1)}, bf16[448,128]{1,0:T(8,128)(2,1)S(1)}, u32[]{:S(2)}, u32[]{:S(2)}) collective-permute-start(bf16[448,128]{1,0:T(8,128)(2,1)S(1)} %shard_map.382), channel_id=1, source_target_pairs={{0,6},{1,7},{2,4},{3,5},{4,2},{5,3},{6,0},{7,1},{8,14},{9,15},{10,... | collective-permute-start | bytes 344072 | tf_op jit(solution)/shard_map/ppermute | solution.py:1784
  121.8 6.3 %collective-permute-start.18 = (bf16[448,128]{1,0:T(8,128)(2,1)S(1)}, bf16[448,128]{1,0:T(8,128)(2,1)S(1)}, u32[]{:S(2)}, u32[]{:S(2)}) collective-permute-start(bf16[448,128]{1,0:T(8,128)(2,1)S(1)} %shard_map.382), channel_id=1, source_target_pairs={{0,4},{1,5},{2,6},{3,7},{4,0},{5,1},{6,2},{7,3},{8,12},{9,13},{10,... | collective-permute-start | bytes 344072 | tf_op jit(solution)/shard_map/ppermute | solution.py:1784
  122.3 6.0 %collective-permute-start.17 = (bf16[448,128]{1,0:T(8,128)(2,1)S(1)}, bf16[448,128]{1,0:T(8,128)(2,1)S(1)}, u32[]{:S(2)}, u32[]{:S(2)}) collective-permute-start(bf16[448,128]{1,0:T(8,128)(2,1)S(1)} %shard_map.382), channel_id=1, source_target_pairs={{0,2},{1,3},{2,0},{3,1},{4,6},{5,7},{6,4},{7,5},{8,10},{9,11},{10,... | collective-permute-start | bytes 344072 | tf_op jit(solution)/shard_map/ppermute | solution.py:1784
  (23 other events, 160.4 us)
where the time goes:
time: 134 us; the launch traced here: 133 us
  Pallas kernels  76.1 us (57%)
  starting transfers between devices  35.2 us (26%)
  waiting for transfers between devices  14.1 us (11%)
  local copies, waits for them, and re-layouts  3.65 us (3%)
  other arithmetic  3.07 us (2%)
    pallas_call x13, Pallas kernels, call(): pl.pallas_call(outer, out_shape=[jax.ShapeDtypeStruct(out[0], out[1]) for...  76.1 us
    ppermute x22, starting transfers between devices, moved(): lax.ppermute(block, axis, [(index, index ^ bits) for index in range(count)])  23.7 us
    ppermute x22, waiting for transfers between devices, moved(): lax.ppermute(block, axis, [(index, index ^ bits) for index in range(count)])  14.1 us
    all_to_all x1, starting transfers between devices, head_device(): joined_all = lax.all_to_all(joined, 'tm', 0, 0, tiled=True)  3.89 us
    all_to_all x1, starting transfers between devices, head_device(): late_moved = lax.all_to_all(late_pack, 'stream', 0, 0, tiled=True)  3.87 us
    all_to_all x1, starting transfers between devices, head_device(): mixed_own = lax.all_to_all(mixed, 'tm', 0, 0, tiled=True)  3.77 us
    unnamed x44, local copies, waits for them, and re-layouts  3.65 us
  transfers between devices with their start and end apart: 25, of which 11 were waited for; matrix products, arithmetic and copies ran while one was open for 1% of the time, Pallas kernels for 29%

commit v1 on v0

--- a/solution.py
+++ b/solution.py
@@ -965,20 +965,13 @@
 
 def fill_margins(wide_s, frames):
     edge = jnp.zeros((MARGIN, LANES), F32)
-    wide_s[0, :MARGIN] = edge
-    wide_s[0, MARGIN + frames : 2 * MARGIN + frames] = edge
+    wide_s[:MARGIN] = edge
+    wide_s[MARGIN + frames : 2 * MARGIN + frames] = edge
     base = frames + 3 * MARGIN
     after = base + frames // 2
     low = low_lanes(MARGIN)
-    wide_s[0, base - MARGIN : base] = jnp.where(low, 0.0, turn(wide_s[0, after - MARGIN : after]))
-    wide_s[0, after : after + MARGIN] = jnp.where(low, turn(wide_s[0, base : base + MARGIN]), 0.0)
-    wide_s[0, after + MARGIN :] = jnp.zeros((wide_s.shape[1] - after - MARGIN, LANES), F32)
-
-    @pl.loop(0, (after + MARGIN) // WINDOW, unroll=5)
-    def _(step):
-        window = wide_s[0, pl.ds(pl.multiple_of(step * WINDOW, WINDOW), WINDOW + 8)]
-        for shift in range(1, 8):
-            wide_s[shift, pl.ds(pl.multiple_of(step * WINDOW, WINDOW), WINDOW)] = window[shift : shift + WINDOW]
+    wide_s[base - MARGIN : base] = jnp.where(low, 0.0, turn(wide_s[after - MARGIN : after]))
+    wide_s[after : after + MARGIN] = jnp.where(low, turn(wide_s[base : base + MARGIN]), 0.0)
 
 
 def item_span(bounds_s, frame):
@@ -1044,9 +1037,8 @@
     return None if limits is None else (limits[0] <= shift) & (limits[1] > shift)
 
 
-def tap_view(wide_s, base, tap, mask):
-    at = pl.ds(pl.multiple_of(base + (tap + 1) // 8 * 8, 8), WINDOW)
-    view = wide_s[(tap + 1) % 8, at]
+def tap_view(window_ref, tap, mask):
+    view = window_ref[tap + 1 : tap + 1 + WINDOW]
     return grouped(view if mask is None else jnp.where(mask, view, 0.0))
 
 
@@ -1083,8 +1075,11 @@
     turn_s,
     tap_sum_s,
     columns_s,
+    forward_s,
+    backward_s,
     bounds_s,
 ):
+    place = lax.axis_index("tm")
     frames = mix_s.shape[0]
     half = frames // 2
     blocks = frames // BLOCK
@@ -1117,7 +1112,7 @@
         hat = (hidden - mean) * rate
         hat_s[rows] = hat
         hat_out.buffer[rows] = hat.astype(BF16)
-        conv_s[0, to_rows] = (hat * lines[2:3] + lines[3:4]).astype(BF16).astype(F32)
+        conv_s[to_rows] = (hat * lines[2:3] + lines[3:4]).astype(BF16).astype(F32)
 
     @pl.loop(0, half // TALL, unroll=2)
     def _(block):
@@ -1153,15 +1148,18 @@
 
     hat_out.go()
     fill_margins(conv_s, frames)
+    tall = WINDOW + 2 * MARGIN
     outs = (0, half, frames)
 
     def convolve(step, limits):
         for index, base in enumerate(triple_places(step, frames)):
+            forward_s[index] = conv_s[pl.ds(base, tall)]
+        for index in range(3):
             own = None if limits is None else limits[index]
             total = jnp.zeros((WINDOW // 8, 8, LANES), F32)
             for tap in range(KERNEL):
-                view = tap_view(conv_s, base, tap, tap_mask(tap, own))
-                total = total + view * taps_s[index // 2, tap][None]
+                mask = tap_mask(tap, own)
+                total = total + tap_view(forward_s.at[index], tap, mask) * taps_s[index // 2, tap][None]
             lines = rest if index == 2 else main
             out_s[rows_of(step, WINDOW, outs[index])] = total.reshape(WINDOW, LANES) + lines[4:5]
 
@@ -1179,7 +1177,7 @@
         gate_pre = (grad_gated * conv * gate_slope_s[rows]).astype(BF16)
         gate_pre_ref[rows] = gate_pre
         grad_conv = (grad_gated * gate).astype(BF16).astype(F32)
-        grad_s[0, to_rows] = grad_conv
+        grad_s[to_rows] = grad_conv
         gate_pre = gate_pre.astype(F32)
         return gate * conv, gate_pre, (up_sum + fold_rows(gate_pre), conv_sum + fold_rows(grad_conv))
 
@@ -1217,9 +1215,9 @@
     )
     gate_pre_out.go()
     fill_margins(grad_s, frames)
-    ones = jnp.ones((16, frames), BF16)
-    lines_out[0:1] = dot_nn(ones, branch_s[...])[0:1]
-    lines_out[1:2] = dot_nn(ones, cot_ref[...])[0:1]
+    own = rows_of(place, BLOCK)
+    lines_out[0:1] = one_row(fold_rows(branch_s[own].astype(F32)))
+    lines_out[1:2] = one_row(fold_rows(cot_ref[own].astype(F32)))
     lines_out[2:8] = jnp.zeros((6, D), F32)
     grad_down = dot_tn(mix_s[...], branch_s[...])
     grad_gate = dot_tn(gate_s[...], n_ref[...])
@@ -1238,13 +1236,16 @@
 
     def differentiate(step, limits):
         for index, base in enumerate(triple_places(step, frames)):
+            forward_s[index] = conv_s[pl.ds(base, tall)]
+            backward_s[index] = grad_s[pl.ds(base, tall)]
+        for index in range(3):
             own = None if limits is None else limits[index]
             total = jnp.zeros((WINDOW // 8, 8, LANES), F32)
-            centre = grouped(grad_s[0, pl.ds(base + MARGIN, WINDOW)])
+            centre = grouped(backward_s[index, MARGIN : MARGIN + WINDOW])
             for tap in range(KERNEL):
                 mask = tap_mask(tap, own)
-                total = total + tap_view(grad_s, base, tap, mask) * turn_s[index // 2, tap][None]
-                tap_sum_s[index // 2, tap] += jnp.sum(tap_view(conv_s, base, tap, mask) * centre, axis=0)
+                total = total + tap_view(backward_s.at[index], tap, mask) * turn_s[index // 2, tap][None]
+                tap_sum_s[index // 2, tap] += jnp.sum(tap_view(forward_s.at[index], tap, mask) * centre, axis=0)
             back_s[rows_of(step, WINDOW, outs[index])] = total.reshape(WINDOW, LANES)
 
     over_windows(bounds_s, frames, differentiate)
@@ -1453,27 +1454,18 @@
     norm_hat_ref,
     gain_ref,
     other_ref,
-    n_ref,
-    vectors_ref,
-    first_lines_ref,
-    head_lines_ref,
+    pre_out,
     same_out,
     apart_out,
-    pack_out,
-    pre_s,
+    lines_out,
+    up_out,
     columns_s,
-    grad_up_s,
-    lines_s,
-    up_columns_s,
 ):
-    pack_ref = pack_out.buffer
     place = lax.axis_index("tm")
+    pre_s = pre_out.buffer
     frames = pre_s.shape[0]
     half = frames // 2
     blocks = frames // BLOCK
-    quarters = pack_ref.shape[0]
-    channels = vectors_ref.shape[0]
-    share = channels // quarters
     totals = jnp.zeros((2 * blocks, LANES), F32)
     mixed_ref = mixed_ref()
     for source in range(mixed_ref.shape[0]):
@@ -1487,7 +1479,7 @@
             lane == 0, columns[:, 2 * block : 2 * block + 1], columns[:, 2 * block + 1 : 2 * block + 2]
         )
     gate_pre_ref, grad_ref, rate_ref, hat_ref = gate_pre_ref(), grad_ref(), rate_ref(), hat_ref()
-    begin(n_ref, up_ref, norm_hat_ref, other_ref)
+    begin(up_ref, norm_hat_ref, other_ref)
     low = low_lanes(64)
     gain = line_of(gain_ref)
 
@@ -1523,64 +1515,86 @@
 
     zero = jnp.zeros((8, LANES), F32)
     main_up, rest_up = lax.fori_loop(0, half // TALL, pre_step, (zero, zero), unroll=2)
-    n_ref, up_ref, norm_hat_ref, other_ref = n_ref(), up_ref(), norm_hat_ref(), other_ref()
-    grad_up_s[...] = dot_tn(pre_s[:, LANES:], n_ref[...])
+    pre_out.go()
+    up_ref, norm_hat_ref, other_ref = up_ref(), norm_hat_ref(), other_ref()
     wide_zero = jnp.zeros((8, D), F32)
 
-    def norm_step(block, sums):
+    def norm_step(step, sums):
         gain_sum, bias_sum = sums
-        rows = rows_of(block, BLOCK)
-        grad = dot_nt(pre_s[rows], up_ref[...])
-        total = (grad * gain + other_ref[rows].astype(F32)).astype(BF16)
-        apart = lax.bitwise_xor(block, place)
-
-        @pl.when(lax.rem(apart, 2) == 0)
-        def _():
-            same_out.buffer[lax.div(apart, 2)] = total
-
-        @pl.when(lax.rem(apart, 2) == 1)
-        def _():
-            apart_out.buffer[lax.div(apart, 2)] = total
-
-        return gain_sum + fold_rows(grad * norm_hat_ref[rows].astype(F32)), bias_sum + fold_rows(grad)
-
-    gain_sum, bias_sum = lax.fori_loop(0, blocks, norm_step, (wide_zero, wide_zero), unroll=4)
+        grads = dot_nt(pre_s[rows_of(step, TALL)], up_ref[...])
+        for part in range(TALL // BLOCK):
+            block = step * (TALL // BLOCK) + part
+            rows = rows_of(block, BLOCK)
+            grad = grads[part * BLOCK : (part + 1) * BLOCK]
+            total = (grad * gain + other_ref[rows].astype(F32)).astype(BF16)
+            apart = lax.bitwise_xor(block, place)
+
+            @pl.when(lax.rem(apart, 2) == 0)
+            def _(apart=apart, total=total):
+                same_out.buffer[lax.div(apart, 2)] = total
+
+            @pl.when(lax.rem(apart, 2) == 1)
+            def _(apart=apart, total=total):
+                apart_out.buffer[lax.div(apart, 2)] = total
+
+            gain_sum = gain_sum + fold_rows(grad * norm_hat_ref[rows].astype(F32))
+            bias_sum = bias_sum + fold_rows(grad)
+        return gain_sum, bias_sum
+
+    gain_sum, bias_sum = lax.fori_loop(0, frames // TALL, norm_step, (wide_zero, wide_zero), unroll=2)
     apart_out.go()
     same_out.go()
+    lines_out[...] = jnp.concatenate([one_row(gain_sum), one_row(bias_sum), jnp.zeros((6, D), F32)], axis=0)
     rest_line = one_row(rest_up)
-    up_columns_s[:LANES] = jnp.transpose(jnp.broadcast_to(one_row(main_up), (LANES, LANES)))
-    up_columns_s[LANES:] = jnp.transpose(jnp.broadcast_to(rest_line + turn(rest_line), (LANES, LANES)))[:LOW]
-    first_device = (place == 0).astype(F32)
-    lines_s[...] = jnp.concatenate(
+    up_out[:LANES] = jnp.transpose(jnp.broadcast_to(one_row(main_up), (LANES, LANES)))
+    up_out[LANES:] = jnp.transpose(jnp.broadcast_to(rest_line + turn(rest_line), (LANES, LANES)))[:LOW]
+
+
+def late_pack_kernel(
+    pre_ref,
+    n_ref,
+    joined_ref,
+    branch_ref,
+    cot_ref,
+    vectors_ref,
+    up_columns_ref,
+    first_lines_ref,
+    head_lines_ref,
+    own_lines_ref,
+    pack_out,
+):
+    pack_ref = pack_out.buffer
+    quarters = pack_ref.shape[0]
+    channels = vectors_ref.shape[0]
+    share = channels // quarters
+    gate_at = KERNEL + 3
+    lane = lax.broadcasted_iota(jnp.int32, (share, LANES), 1)
+    lines = jnp.concatenate(
         [
             head_lines_ref[0:2],
-            one_row(gain_sum),
-            one_row(bias_sum),
+            own_lines_ref[0:2],
             head_lines_ref[2:4],
-            first_lines_ref[0:2] * first_device,
+            first_lines_ref[0:2],
             jnp.zeros((8, D), F32),
         ],
         axis=0,
     )
-    gate_at = KERNEL + 3
-    lane = lax.broadcasted_iota(jnp.int32, (share, LANES), 1)
     for quarter in range(quarters):
-        lanes = slice(quarter * LANES, (quarter + 1) * LANES)
-        pack_ref[quarter, :LANES] = grad_up_s[LANES:, lanes].astype(BF16)
-        pack_ref[quarter, LANES:channels] = grad_up_s[LOW:LANES, lanes].astype(BF16)
         table = vectors_ref[quarter * share : (quarter + 1) * share]
         for other in range(2):
             at = slice((2 * (quarter % 2) + other) * share, (2 * (quarter % 2) + other + 1) * share)
-            column = vectors_ref[at, gate_at : gate_at + 1] if quarter < quarters // 2 else up_columns_s[at, 0:1]
+            column = vectors_ref[at, gate_at : gate_at + 1] if quarter < quarters // 2 else up_columns_ref[at, 0:1]
             table = jnp.where(lane == gate_at + other, column, table)
         pack_ref[quarter, channels : channels + share] = table.astype(BF16)
-        pack_ref[quarter, channels + share : channels + share + 16] = lines_s[:, lanes].astype(BF16)
-
-
-def merge_kernel(joined_ref, branch_ref, cot_ref, up_ref, pack_out):
-    pack_ref = pack_out.buffer
-    cot_ref = cot_ref()
-    quarters, first, _ = up_ref.shape
+        pack_ref[quarter, channels + share : channels + share + 16] = lines[
+            :, quarter * LANES : (quarter + 1) * LANES
+        ].astype(BF16)
+    grad_up = dot_tn(pre_ref()[...], n_ref()[...])
+    for quarter in range(quarters):
+        lanes = slice(quarter * LANES, (quarter + 1) * LANES)
+        pack_ref[quarter, :LANES] = grad_up[LANES:, lanes].astype(BF16)
+        pack_ref[quarter, LANES:channels] = grad_up[LOW:LANES, lanes].astype(BF16)
+    joined_ref, cot_ref, branch_ref = joined_ref(), cot_ref(), branch_ref()
     sources, _, rows = joined_ref.shape
     merge_rows = 2 * D // sources
     head_rows = D // sources
@@ -1591,16 +1605,15 @@
         joined = joined_ref[source]
         grad_merge = grad_merge + dot_nn(joined[:merge_rows], cot_ref[at])
         grad_head = grad_head + dot_nn(joined[merge_rows : merge_rows + head_rows], branch_ref[at])
-    pack_ref[:, :first] = up_ref[...]
     for quarter in range(quarters):
-        base = first
+        base = channels + share + 16
         for grad in (grad_merge, grad_head):
-            share = grad.shape[0] // quarters
+            part = grad.shape[0] // quarters
             for tile in range(4):
-                pack_ref[quarter, base : base + share] = grad[
-                    quarter * share : (quarter + 1) * share, tile * LANES : (tile + 1) * LANES
+                pack_ref[quarter, base : base + part] = grad[
+                    quarter * part : (quarter + 1) * part, tile * LANES : (tile + 1) * LANES
                 ].astype(BF16)
-                base += share
+                base += part
 
 
 def output_kernel(
@@ -1948,8 +1961,8 @@
             ((total, 2 * LANES), BF16),
             ((folded, LANES), F32),
             ((folded, LANES), F32),
-            ((8, padded + WINDOW, LANES), F32),
-            ((8, padded + WINDOW, LANES), F32),
+            ((padded, LANES), F32),
+            ((padded, LANES), F32),
             ((folded, LANES), F32),
             ((folded, LANES), F32),
             ((total, D), BF16),
@@ -1958,6 +1971,8 @@
             ((2, 32, 8, LANES), F32),
             ((2, 32, 8, LANES), F32),
             ((total, LANES), F32),
+            ((3, WINDOW + 2 * MARGIN, LANES), F32),
+            ((3, WINDOW + 2 * MARGIN, LANES), F32),
         ],
         bounds=True,
     )(lengths, n_mlp, up_own, table, stats, *blocks, merge_weight, down_weight, attn)
@@ -2030,11 +2045,16 @@
     )(own_frames, mixed_own, out_weight, down_weight, down_bias, merge_weight, merge_bias)
     joined_all = lax.all_to_all(joined, "tm", 0, 0, tiled=True)
     gate_pre, _ = lax.optimization_barrier((gate_pre, joined))
-    up_rows = 5 * share + 16
-    late_rows = up_rows + 3 * D // count
-    same, apart, up_pack = kernel_call(
+    late_rows = 5 * share + 16 + 3 * D // count
+    pre, same, apart, own_lines, up_columns = kernel_call(
         mlp_second_kernel,
-        [((count // 2, own, D), BF16, 1)] * 2 + [((quarters, up_rows, LANES), BF16, 1)],
+        [
+            ((total, 3 * LANES), BF16, 1),
+            ((count // 2, own, D), BF16, 1),
+            ((count // 2, own, D), BF16, 1),
+            ((8, D), F32),
+            ((channels, LANES), F32),
+        ],
         [
             Part(
                 (count, 2 * total // BLOCK, 2 * LANES),
@@ -2045,37 +2065,28 @@
             late,
             "v",
             late,
-            late,
-            *"vvv",
         ],
+        [((total, LANES), F32)],
+    )(mixed_own, gate_pre, grad_y, slope, gate_hat, up_own, hat, ln_mlp_gain, from_attn)
+    sibling = moved(apart, "tm", 1)
+    pre, joined_all = lax.optimization_barrier((pre, joined_all))
+    (late_pack,) = kernel_call(
+        late_pack_kernel,
+        [((quarters, late_rows, LANES), BF16, 1)],
         [
-            ((total, 3 * LANES), BF16),
-            ((total, LANES), F32),
-            ((2 * LANES, D), F32),
-            ((16, D), F32),
-            ((channels, LANES), F32),
+            Part(
+                (total, 2 * LANES),
+                lambda refs, buffer: [(refs[0].at[:, pl.ds(LANES, 2 * LANES)], buffer)],
+            ),
+            whole,
+            whole,
+            whole,
+            blocks_part(1),
+            *"vvvvv",
         ],
-    )(
-        mixed_own,
-        gate_pre,
-        grad_y,
-        slope,
-        gate_hat,
-        up_own,
-        hat,
-        ln_mlp_gain,
-        from_attn,
-        n_mlp,
-        vectors,
-        first_lines,
-        head_lines,
-    )
-    (late_pack,) = kernel_call(
-        merge_kernel, [((quarters, late_rows, LANES), BF16, 1)], ["f", "f", blocks_part(1), "f"]
-    )(joined_all, branch, *blocks, up_pack)
+    )(pre, n_mlp, joined_all, branch, *blocks, vectors, up_columns, first_lines, head_lines, own_lines)
     late_pack, head_parts = lax.optimization_barrier((late_pack, head_parts))
     late_moved = lax.all_to_all(late_pack, "stream", 0, 0, tiled=True)
-    sibling = moved(apart, "tm", 1)
     (early_part,) = kernel_call(add_kernel, [((4 * HEAD + 8 * share, LANES), BF16)], quarters * "v", megas=24)(
         *head_parts
     )

time: 134 us -> 133 us (level)
  Pallas kernels: 76.1 us -> 73.5 us
    pallas_call x13, Pallas kernels: 76.1 us -> 73.5 us  [call(): pl.pallas_call(outer, out_shape=[jax.ShapeDtypeStruct(out[0], out[1]) for...]
  transfers between devices with their start and end apart: 25 -> 25, of which waited for: 11 -> 11; matrix products, arithmetic and copies ran while one was open for 1% -> 1% of each run, Pallas kernels for 29% -> 30%
where the time goes in v1:
time: 133 us; the launch traced here: 132 us
  Pallas kernels  73.5 us (55%)
  starting transfers between devices  36.3 us (27%)
  waiting for transfers between devices  14.1 us (11%)
  local copies, waits for them, and re-layouts  3.67 us (3%)
  other arithmetic  3.07 us (2%)
    pallas_call x13, Pallas kernels, call(): pl.pallas_call(outer, out_shape=[jax.ShapeDtypeStruct(out[0], out[1]) for...  73.5 us
    ppermute x22, starting transfers between devices, moved(): lax.ppermute(block, axis, [(index, index ^ bits) for index in range(count)])  23.6 us
    ppermute x22, waiting for transfers between devices, moved(): lax.ppermute(block, axis, [(index, index ^ bits) for index in range(count)])  14.1 us
    all_to_all x1, starting transfers between devices, head_device(): late_moved = lax.all_to_all(late_pack, 'stream', 0, 0, tiled=True)  5.02 us
    all_to_all x1, starting transfers between devices, head_device(): joined_all = lax.all_to_all(joined, 'tm', 0, 0, tiled=True)  3.89 us
    all_to_all x1, starting transfers between devices, head_device(): mixed_own = lax.all_to_all(mixed, 'tm', 0, 0, tiled=True)  3.77 us
    unnamed x44, local copies, waits for them, and re-layouts  3.67 us
  transfers between devices with their start and end apart: 25, of which 11 were waited for; matrix products, arithmetic and copies ran while one was open for 1% of the time, Pallas kernels for 30%

profile of v1, /device:TPU:0, one launch (start us, length us, event | category | flops | bytes accessed | tf_op | source)
XLA Modules:
  0.0 131.9 jit_solution(7401761129393319053)
XLA Ops:
  1.7 4.0 %collective-permute-start.2 = (bf16[128,1024]{1,0:T(8,128)(2,1)S(1)}, bf16[128,1024]{1,0:T(8,128)(2,1)S(1)}, u32[]{:S(2)}, u32[]{:S(2)}) collective-permute-start(bf16[128,1024]{1,0:T(8,128)(2,1)S(1)} %pad_maximum_fusion.2.refs_1_.refs_5_.refs_0_.refs_4_), channel_id=1, source_target_pairs={{0,6},{1,7},{2,4},{3,5},{4,2},{5,3},{6,0},{7,1},{8,14},{9,15},{10,... | collective-permute-start | bytes 786440 | tf_op jit(solution)/shard_map/ppermute | solution.py:1797
  6.3 5.5 %shard_map.373 = (bf16[512,384]{1,0:T(8,128)(2,1)}, f32[2,40,128]{2,1,0:T(8,128)}, bf16[512,384]{1,0:T(8,128)(2,1)}, bf16[512,128]{1,0:T(8,128)(2,1)}, f32[8,128]{1,0:T(8,128)}) custom-call(bf16[512,3072]{1,0:T(8,128)(2,1)} %refs_18_.1, bf16[3072]{0:T(1024)(128)(2,1)} %refs_19_.1, bf16[1536]{0:T(1024)(128)(2,1)} %refs_2_.2, bf16[1536]{0:T(1024)(128)(2,1)} %refs_3_.2, ...), custom_call_target="tpu_custom_call" | custom-call | tf_op jit(solution)/shard_map/pallas_call | solution.py:740
  12.8 4.7 %collective-permute-done.1.refs_5_.refs_9_.refs_4_.refs_8_ = bf16[128,1024]{1,0:T(8,128)(2,1)S(1)} collective-permute-done((bf16[128,1024]{1,0:T(8,128)(2,1)S(1)}, bf16[128,1024]{1,0:T(8,128)(2,1)S(1)}, u32[]{:S(2)}, u32[]{:S(2)}) %collective-permute-start.1) | collective-permute-done | bytes 262176 | tf_op jit(solution)/shard_map/ppermute | solution.py:1797
  21.3 12.8 %shard_map.374 = (bf16[1024,512]{1,0:T(8,128)(2,1)}, bf16[1024,512]{1,0:T(8,128)(2,1)}, bf16[1024,512]{1,0:T(8,128)(2,1)}, bf16[1024,128]{1,0:T(8,128)(2,1)}, bf...) custom-call(s32[1,5]{1,0:T(1,128)} %refs_0_.5, ...), custom_call_target="tpu_custom_call" | custom-call | tf_op jit(solution)/shard_map/pallas_call | solution.py:740
  34.2 15.6 %shard_map.375 = (bf16[8,144,256]{2,1,0:T(8,128)(2,1)}, bf16[1536,128]{1,0:T(8,128)(2,1)}, bf16[1536,128]{1,0:T(8,128)(2,1)}, bf16[1536,128]{1,0:T(8,128)(2,1)},...) custom-call(s32[1,5]{1,0:T(1,128)} %refs_0_.5, ...), custom_call_target="tpu_custom_call" | custom-call | tf_op jit(solution)/shard_map/pallas_call | solution.py:740
  49.8 3.8 %all-to-all-start = ((bf16[8,144,256]{2,1,0:T(8,128)(2,1)}), bf16[8,144,256]{2,1,0:T(8,128)(2,1)S(1)}, u32[]{:S(2)}, u32[]{:S(2)}) async-start(bf16[8,144,256]{2,1,0:T(8,128)(2,1)} %get-tuple-element.124), calls=%async_computation | async-start | bytes 1179648 | tf_op jit(solution)/shard_map/all_to_all | solution.py:1979
  53.6 12.6 %shard_map.376 = (bf16[1024,512]{1,0:T(8,128)(2,1)}, bf16[1024,512]{1,0:T(8,128)(2,1)}, bf16[640,128]{1,0:T(8,128)(2,1)}, bf16[640,128]{1,0:T(8,128)(2,1)}, bf16...) custom-call(bf16[128,1024]{1,0:T(8,128)(2,1)} %copy-done.11, bf16[128,1024]{1,0:T(8,128)(2,1)} %copy-done.15, ...), custom_call_target="tpu_custom_call" | custom-call | tf_op jit(solution)/shard_map/pallas_call | solution.py:740
  67.5 2.5 %shard_map.377 = (bf16[128,512]{1,0:T(8,128)(2,1)}, bf16[8,256,128]{2,1,0:T(8,128)(2,1)S(1)}) custom-call(bf16[128,512]{1,0:T(8,128)(2,1)S(1)} %bitcast.13, bf16[8,144,256]{2,1,0:T(8,128)(2,1)S(1)} %all-to-all-done.refs_1_.refs_0_, bf16[512,512]{1,0:T(8,128)(2,1)S(1)} %copy-done.3, bf16[1536,512]{1,0:T(8,128)(2,1)S(1)} %copy-done.1, ...), custom_call_target="tpu_custom_call" | custom-call | tf_op jit(solution)/shard_map/pallas_call | solution.py:740
  70.8 3.9 %all-to-all-start.1 = ((bf16[8,256,128]{2,1,0:T(8,128)(2,1)}), bf16[8,256,128]{2,1,0:T(8,128)(2,1)S(1)}, u32[]{:S(2)}, u32[]{:S(2)}) async-start(bf16[8,256,128]{2,1,0:T(8,128)(2,1)} %copy-done.6), calls=%async_computation.1 | async-start | bytes 1048576 | tf_op jit(solution)/shard_map/all_to_all | solution.py:2046
  74.7 1.6 %collective-permute-start.7 = (bf16[640,128]{1,0:T(8,128)(2,1)}, bf16[640,128]{1,0:T(8,128)(2,1)S(1)}, u32[]{:S(2)}, u32[]{:S(2)}) collective-permute-start(bf16[640,128]{1,0:T(8,128)(2,1)} %get-tuple-element.152), channel_id=1, source_target_pairs={{0,8},{8,0},{16,24},{24,16},{1,9},{9,1},{17,25},{25,17},{2,10},{10... | collective-permute-start | bytes 491528 | tf_op jit(solution)/shard_map/ppermute | solution.py:1797
  76.3 2.6 %collective-permute-start.8 = (bf16[640,128]{1,0:T(8,128)(2,1)}, bf16[640,128]{1,0:T(8,128)(2,1)S(1)}, u32[]{:S(2)}, u32[]{:S(2)}) collective-permute-start(bf16[640,128]{1,0:T(8,128)(2,1)} %get-tuple-element.153), channel_id=1, source_target_pairs={{0,16},{8,24},{16,0},{24,8},{1,17},{9,25},{17,1},{25,9},{2,18},{10... | collective-permute-start | bytes 491528 | tf_op jit(solution)/shard_map/ppermute | solution.py:1797
  79.1 8.1 %shard_map.378 = (bf16[1024,384]{1,0:T(8,128)(2,1)}, bf16[4,128,512]{2,1,0:T(8,128)(2,1)}, bf16[4,128,512]{2,1,0:T(8,128)(2,1)}, f32[8,512]{1,0:T(8,128)}, f32[192,128]{1,0:T(8,128)}) custom-call(bf16[8,144,256]{2,1,0:T(8,128)(2,1)} %copy-done.2, bf16[1536,128]{1,0:T(8,128)(2,1)} %get-tuple-element.138.refs_1_, ...), custom_call_target="tpu_custom_call" | custom-call | tf_op jit(solution)/shard_map/pallas_call | solution.py:740
  88.0 5.4 %shard_map.379 = bf16[4,448,128]{2,1,0:T(8,128)(2,1)} custom-call(bf16[1024,384]{1,0:T(8,128)(2,1)} %get-tuple-element.144.refs_0_, bf16[1024,512]{1,0:T(8,128)(2,1)} %get-tuple-element.119.refs_1_, bf16[8,256,128]{2,1,0:T(8,128)(2,1)} %copy-done.19, bf16[1024,512]{1,0:T(8,128)(2,1)} %get-tuple-element.146.refs_3_, bf16[128,1024]{1,0:T(8,128)(2,1)} %copy-done.11, ...), custom_call_target="tpu_custom_call" | custom-call | tf_op jit(solution)/shard_map/pallas_call | solution.py:740
  93.4 5.0 %all-to-all-start.2 = ((bf16[4,448,128]{2,1,0:T(8,128)(2,1)}), bf16[4,448,128]{2,1,0:T(8,128)(2,1)S(1)}, u32[]{:S(2)}, u32[]{:S(2)}) async-start(bf16[4,448,128]{2,1,0:T(8,128)(2,1)} %shard_map.379), calls=%async_computation.2 | async-start | bytes 917504 | tf_op jit(solution)/shard_map/all_to_all | solution.py:2089
  99.4 3.0 %collective-permute-start.12 = (bf16[640,128]{1,0:T(8,128)(2,1)S(1)}, bf16[640,128]{1,0:T(8,128)(2,1)S(1)}, u32[]{:S(2)}, u32[]{:S(2)}) collective-permute-start(bf16[640,128]{1,0:T(8,128)(2,1)S(1)} %shard_map.380), channel_id=1, source_target_pairs={{0,6},{1,7},{2,4},{3,5},{4,2},{5,3},{6,0},{7,1},{8,14},{9,15},{10,... | collective-permute-start | bytes 491528 | tf_op jit(solution)/shard_map/ppermute | solution.py:1797
  104.0 2.0 %collective-permute-start.14 = (bf16[128,512]{1,0:T(8,128)(2,1)S(1)}, bf16[128,512]{1,0:T(8,128)(2,1)S(1)}, u32[]{:S(2)}, u32[]{:S(2)}) collective-permute-start(bf16[128,512]{1,0:T(8,128)(2,1)S(1)} %get-tuple-element.163), channel_id=1, source_target_pairs={{0,2},{1,3},{2,0},{3,1},{4,6},{5,7},{6,4},{7,5},{8,10},{9,11},{10,... | collective-permute-start | bytes 393224 | tf_op jit(solution)/shard_map/ppermute | solution.py:1797
  107.5 2.8 %collective-permute-start.16 = (bf16[128,512]{1,0:T(8,128)(2,1)S(1)}, bf16[128,512]{1,0:T(8,128)(2,1)S(1)}, u32[]{:S(2)}, u32[]{:S(2)}) collective-permute-start(bf16[128,512]{1,0:T(8,128)(2,1)S(1)} %get-tuple-element.165), channel_id=1, source_target_pairs={{0,6},{1,7},{2,4},{3,5},{4,2},{5,3},{6,0},{7,1},{8,14},{9,15},{10,... | collective-permute-start | bytes 393224 | tf_op jit(solution)/shard_map/ppermute | solution.py:1797
  111.5 2.8 %collective-permute-done.14.refs_3_ = bf16[128,512]{1,0:T(8,128)(2,1)S(1)} collective-permute-done((bf16[128,512]{1,0:T(8,128)(2,1)S(1)}, bf16[128,512]{1,0:T(8,128)(2,1)S(1)}, u32[]{:S(2)}, u32[]{:S(2)}) %collective-permute-start.14) | collective-permute-done | bytes 131104 | tf_op jit(solution)/shard_map/ppermute | solution.py:1797
  114.3 2.1 %collective-permute-done.16.refs_5_ = bf16[128,512]{1,0:T(8,128)(2,1)S(1)} collective-permute-done((bf16[128,512]{1,0:T(8,128)(2,1)S(1)}, bf16[128,512]{1,0:T(8,128)(2,1)S(1)}, u32[]{:S(2)}, u32[]{:S(2)}) %collective-permute-start.16) | collective-permute-done | bytes 131104 | tf_op jit(solution)/shard_map/ppermute | solution.py:1797
  117.5 2.7 %collective-permute-start.19 = (bf16[448,128]{1,0:T(8,128)(2,1)S(1)}, bf16[448,128]{1,0:T(8,128)(2,1)S(1)}, u32[]{:S(2)}, u32[]{:S(2)}) collective-permute-start(bf16[448,128]{1,0:T(8,128)(2,1)S(1)} %shard_map.382), channel_id=1, source_target_pairs={{0,6},{1,7},{2,4},{3,5},{4,2},{5,3},{6,0},{7,1},{8,14},{9,15},{10,... | collective-permute-start | bytes 344072 | tf_op jit(solution)/shard_map/ppermute | solution.py:1797
  121.1 1.9 %shard_map.383 = f32[128,512]{1,0:T(8,128)} custom-call(bf16[128,512]{1,0:T(8,128)(2,1)S(1)} %bitcast.14, bf16[128,512]{1,0:T(8,128)(2,1)S(1)} %bitcast.17, bf16[128,512]{1,0:T(8,128)(2,1)S(1)} %get-tuple-element.167.refs_2_, bf16[128,512]{1,0:T(8,128)(2,1)S(1)} %collective-permute-done.14.refs_3_, bf16[128,512]{1,0:T(8,128)(2,1)S(1)} %collective-permute-done.15.refs_4_, ...), custom_call_target="tpu_custom_call" | custom-call | tf_op jit(solution)/shard_map/pallas_call | solution.py:740
  123.0 3.4 %shard_map.384 = (f32[128,1536]{1,0:T(8,128)}, f32[128,512]{1,0:T(8,128)}, f32[384,512]{1,0:T(8,128)}, f32[128,3072]{1,0:T(8,128)}) custom-call(bf16[4,640,128]{2,1,0:T(8,128)(2,1)S(1)} %pad_maximum_fusion.refs_0_, bf16[4,640,128]{2,1,0:T(8,128)(2,1)S(1)} %collective-permute-done.20.refs_1_), custom_call_target="tpu_custom_call" | custom-call | tf_op jit(solution)/shard_map/pallas_call | solution.py:740
  127.0 1.8 %collective-permute-done.21.refs_2_ = bf16[4,448,128]{2,1,0:T(8,128)(2,1)S(1)} collective-permute-done((bf16[4,448,128]{2,1,0:T(8,128)(2,1)S(1)}, bf16[4,448,128]{2,1,0:T(8,128)(2,1)S(1)}, u32[]{:S(2)}, u32[]{:S(2)}) %collective-permute-start.21) | collective-permute-done | bytes 458784 | tf_op jit(solution)/shard_map/ppermute | solution.py:1797
  128.8 2.9 %shard_map.385 = (f32[128]{0:T(128)}, f32[128]{0:T(128)}, f32[128]{0:T(128)}, f32[128]{0:T(128)}, f32[128]{0:T(128)}, /*index=5*/f32[128]{0:T(128)}, f32[128,512...) custom-call(f32[128,3072]{1,0:T(8,128)} %get-tuple-element.177.refs_, ...), custom_call_target="tpu_custom_call", output_to_operand_aliasing={{7}: (0, {})} | custom-call | tf_op jit(solution)/shard_map/pallas_call | solution.py:740
  (92 shorter events, 17.1 us)
Async XLA Ops:
  1.7 11.1 %collective-permute-start.2 = (bf16[128,1024]{1,0:T(8,128)(2,1)S(1)}, bf16[128,1024]{1,0:T(8,128)(2,1)S(1)}, u32[]{:S(2)}, u32[]{:S(2)}) collective-permute-start(bf16[128,1024]{1,0:T(8,128)(2,1)S(1)} %pad_maximum_fusion.2.refs_1_.refs_5_.refs_0_.refs_4_), channel_id=1, source_target_pairs={{0,6},{1,7},{2,4},{3,5},{4,2},{5,3},{6,0},{7,1},{8,14},{9,15},{10,... | collective-permute-start | bytes 786440 | tf_op jit(solution)/shard_map/ppermute | solution.py:1797
  5.6 11.9 %collective-permute-start.1 = (bf16[128,1024]{1,0:T(8,128)(2,1)S(1)}, bf16[128,1024]{1,0:T(8,128)(2,1)S(1)}, u32[]{:S(2)}, u32[]{:S(2)}) collective-permute-start(bf16[128,1024]{1,0:T(8,128)(2,1)S(1)} %pad_maximum_fusion.2.refs_1_.refs_5_.refs_0_.refs_4_), channel_id=1, source_target_pairs={{0,4},{1,5},{2,6},{3,7},{4,0},{5,1},{6,2},{7,3},{8,12},{9,13},{10,... | collective-permute-start | bytes 786440 | tf_op jit(solution)/shard_map/ppermute | solution.py:1797
  6.1 11.7 %collective-permute-start = (bf16[128,1024]{1,0:T(8,128)(2,1)S(1)}, bf16[128,1024]{1,0:T(8,128)(2,1)S(1)}, u32[]{:S(2)}, u32[]{:S(2)}) collective-permute-start(bf16[128,1024]{1,0:T(8,128)(2,1)S(1)} %pad_maximum_fusion.2.refs_1_.refs_5_.refs_0_.refs_4_), channel_id=1, source_target_pairs={{0,2},{1,3},{2,0},{3,1},{4,6},{5,7},{6,4},{7,5},{8,10},{9,11},{10,... | collective-permute-start | bytes 786440 | tf_op jit(solution)/shard_map/ppermute | solution.py:1797
  17.8 2.5 %collective-permute-start.3 = (bf16[128,1024]{1,0:T(8,128)(2,1)S(1)}, bf16[128,1024]{1,0:T(8,128)(2,1)S(1)}, u32[]{:S(2)}, u32[]{:S(2)}) collective-permute-start(bf16[128,1024]{1,0:T(8,128)(2,1)S(1)} %pad_maximum_fusion.2.refs_1_.refs_5_.refs_0_.refs_4_), channel_id=1, source_target_pairs={{0,1},{1,0},{2,3},{3,2},{4,5},{5,4},{6,7},{7,6},{8,9},{9,8},{10,11... | collective-permute-start | bytes 786440 | tf_op jit(solution)/shard_map/ppermute | solution.py:1797
  17.9 2.5 %collective-permute-start.4 = (bf16[128,1024]{1,0:T(8,128)(2,1)S(1)}, bf16[128,1024]{1,0:T(8,128)(2,1)S(1)}, u32[]{:S(2)}, u32[]{:S(2)}) collective-permute-start(bf16[128,1024]{1,0:T(8,128)(2,1)S(1)} %collective-permute-done.refs_3_.refs_7_.refs_2_.refs_6_), channel_id=1, source_target_pairs={{0,1},{1,0},{2,3},{3,2},{4,5},{5,4},{6,7},{7,6},{8,9},{9,8},{10,11... | collective-permute-start | bytes 786440 | tf_op jit(solution)/shard_map/ppermute | solution.py:1797
  18.4 2.0 %collective-permute-start.5 = (bf16[128,1024]{1,0:T(8,128)(2,1)S(1)}, bf16[128,1024]{1,0:T(8,128)(2,1)S(1)}, u32[]{:S(2)}, u32[]{:S(2)}) collective-permute-start(bf16[128,1024]{1,0:T(8,128)(2,1)S(1)} %collective-permute-done.1.refs_5_.refs_9_.refs_4_.refs_8_), channel_id=1, source_target_pairs={{0,1},{1,0},{2,3},{3,2},{4,5},{5,4},{6,7},{7,6},{8,9},{9,8},{10,11... | collective-permute-start | bytes 786440 | tf_op jit(solution)/shard_map/ppermute | solution.py:1797
  18.4 2.1 %collective-permute-start.6 = (bf16[128,1024]{1,0:T(8,128)(2,1)S(1)}, bf16[128,1024]{1,0:T(8,128)(2,1)S(1)}, u32[]{:S(2)}, u32[]{:S(2)}) collective-permute-start(bf16[128,1024]{1,0:T(8,128)(2,1)S(1)} %collective-permute-done.2.refs_7_.refs_11_.refs_6_.refs_10_), channel_id=1, source_target_pairs={{0,1},{1,0},{2,3},{3,2},{4,5},{5,4},{6,7},{7,6},{8,9},{9,8},{10,11... | collective-permute-start | bytes 786440 | tf_op jit(solution)/shard_map/ppermute | solution.py:1797
  49.8 16.4 %all-to-all-start = ((bf16[8,144,256]{2,1,0:T(8,128)(2,1)}), bf16[8,144,256]{2,1,0:T(8,128)(2,1)S(1)}, u32[]{:S(2)}, u32[]{:S(2)}) async-start(bf16[8,144,256]{2,1,0:T(8,128)(2,1)} %get-tuple-element.124), calls=%async_computation | async-start | bytes 1179648 | tf_op jit(solution)/shard_map/all_to_all | solution.py:1979
  70.8 16.4 %all-to-all-start.1 = ((bf16[8,256,128]{2,1,0:T(8,128)(2,1)}), bf16[8,256,128]{2,1,0:T(8,128)(2,1)S(1)}, u32[]{:S(2)}, u32[]{:S(2)}) async-start(bf16[8,256,128]{2,1,0:T(8,128)(2,1)} %copy-done.6), calls=%async_computation.1 | async-start | bytes 1048576 | tf_op jit(solution)/shard_map/all_to_all | solution.py:2046
  74.7 18.7 %collective-permute-start.7 = (bf16[640,128]{1,0:T(8,128)(2,1)}, bf16[640,128]{1,0:T(8,128)(2,1)S(1)}, u32[]{:S(2)}, u32[]{:S(2)}) collective-permute-start(bf16[640,128]{1,0:T(8,128)(2,1)} %get-tuple-element.152), channel_id=1, source_target_pairs={{0,8},{8,0},{16,24},{24,16},{1,9},{9,1},{17,25},{25,17},{2,10},{10... | collective-permute-start | bytes 491528 | tf_op jit(solution)/shard_map/ppermute | solution.py:1797
  76.3 17.1 %collective-permute-start.8 = (bf16[640,128]{1,0:T(8,128)(2,1)}, bf16[640,128]{1,0:T(8,128)(2,1)S(1)}, u32[]{:S(2)}, u32[]{:S(2)}) collective-permute-start(bf16[640,128]{1,0:T(8,128)(2,1)} %get-tuple-element.153), channel_id=1, source_target_pairs={{0,16},{8,24},{16,0},{24,8},{1,17},{9,25},{17,1},{25,9},{2,18},{10... | collective-permute-start | bytes 491528 | tf_op jit(solution)/shard_map/ppermute | solution.py:1797
  78.9 14.5 %collective-permute-start.9 = (bf16[640,128]{1,0:T(8,128)(2,1)S(1)}, bf16[640,128]{1,0:T(8,128)(2,1)S(1)}, u32[]{:S(2)}, u32[]{:S(2)}) collective-permute-start(bf16[640,128]{1,0:T(8,128)(2,1)S(1)} %copy-done.21), channel_id=1, source_target_pairs={{0,24},{8,16},{16,8},{24,0},{1,25},{9,17},{17,9},{25,1},{2,26},{10... | collective-permute-start | bytes 491528 | tf_op jit(solution)/shard_map/ppermute | solution.py:1797
  93.4 23.0 %all-to-all-start.2 = ((bf16[4,448,128]{2,1,0:T(8,128)(2,1)}), bf16[4,448,128]{2,1,0:T(8,128)(2,1)S(1)}, u32[]{:S(2)}, u32[]{:S(2)}) async-start(bf16[4,448,128]{2,1,0:T(8,128)(2,1)} %shard_map.379), calls=%async_computation.2 | async-start | bytes 917504 | tf_op jit(solution)/shard_map/all_to_all | solution.py:2089
  98.4 4.6 %collective-permute-start.13 = (bf16[4,128,512]{2,1,0:T(8,128)(2,1)S(1)}, bf16[4,128,512]{2,1,0:T(8,128)(2,1)S(1)}, u32[]{:S(2)}, u32[]{:S(2)}) collective-permute-start(bf16[4,128,512]{2,1,0:T(8,128)(2,1)S(1)} %copy-done.20), channel_id=1, source_target_pairs={{0,1},{1,0},{2,3},{3,2},{4,5},{5,4},{6,7},{7,6},{8,9},{9,8},{10,11... | collective-permute-start | bytes 1572872 | tf_op jit(solution)/shard_map/ppermute | solution.py:1797
  99.4 8.1 %collective-permute-start.12 = (bf16[640,128]{1,0:T(8,128)(2,1)S(1)}, bf16[640,128]{1,0:T(8,128)(2,1)S(1)}, u32[]{:S(2)}, u32[]{:S(2)}) collective-permute-start(bf16[640,128]{1,0:T(8,128)(2,1)S(1)} %shard_map.380), channel_id=1, source_target_pairs={{0,6},{1,7},{2,4},{3,5},{4,2},{5,3},{6,0},{7,1},{8,14},{9,15},{10,... | collective-permute-start | bytes 491528 | tf_op jit(solution)/shard_map/ppermute | solution.py:1797
  102.4 8.4 %collective-permute-start.11 = (bf16[640,128]{1,0:T(8,128)(2,1)S(1)}, bf16[640,128]{1,0:T(8,128)(2,1)S(1)}, u32[]{:S(2)}, u32[]{:S(2)}) collective-permute-start(bf16[640,128]{1,0:T(8,128)(2,1)S(1)} %shard_map.380), channel_id=1, source_target_pairs={{0,4},{1,5},{2,6},{3,7},{4,0},{5,1},{6,2},{7,3},{8,12},{9,13},{10,... | collective-permute-start | bytes 491528 | tf_op jit(solution)/shard_map/ppermute | solution.py:1797
  103.0 8.5 %collective-permute-start.10 = (bf16[640,128]{1,0:T(8,128)(2,1)S(1)}, bf16[640,128]{1,0:T(8,128)(2,1)S(1)}, u32[]{:S(2)}, u32[]{:S(2)}) collective-permute-start(bf16[640,128]{1,0:T(8,128)(2,1)S(1)} %shard_map.380), channel_id=1, source_target_pairs={{0,2},{1,3},{2,0},{3,1},{4,6},{5,7},{6,4},{7,5},{8,10},{9,11},{10,... | collective-permute-start | bytes 491528 | tf_op jit(solution)/shard_map/ppermute | solution.py:1797
  104.0 10.3 %collective-permute-start.14 = (bf16[128,512]{1,0:T(8,128)(2,1)S(1)}, bf16[128,512]{1,0:T(8,128)(2,1)S(1)}, u32[]{:S(2)}, u32[]{:S(2)}) collective-permute-start(bf16[128,512]{1,0:T(8,128)(2,1)S(1)} %get-tuple-element.163), channel_id=1, source_target_pairs={{0,2},{1,3},{2,0},{3,1},{4,6},{5,7},{6,4},{7,5},{8,10},{9,11},{10,... | collective-permute-start | bytes 393224 | tf_op jit(solution)/shard_map/ppermute | solution.py:1797
  106.1 8.2 %collective-permute-start.15 = (bf16[128,512]{1,0:T(8,128)(2,1)S(1)}, bf16[128,512]{1,0:T(8,128)(2,1)S(1)}, u32[]{:S(2)}, u32[]{:S(2)}) collective-permute-start(bf16[128,512]{1,0:T(8,128)(2,1)S(1)} %get-tuple-element.164), channel_id=1, source_target_pairs={{0,4},{1,5},{2,6},{3,7},{4,0},{5,1},{6,2},{7,3},{8,12},{9,13},{10,... | collective-permute-start | bytes 393224 | tf_op jit(solution)/shard_map/ppermute | solution.py:1797
  107.5 8.9 %collective-permute-start.16 = (bf16[128,512]{1,0:T(8,128)(2,1)S(1)}, bf16[128,512]{1,0:T(8,128)(2,1)S(1)}, u32[]{:S(2)}, u32[]{:S(2)}) collective-permute-start(bf16[128,512]{1,0:T(8,128)(2,1)S(1)} %get-tuple-element.165), channel_id=1, source_target_pairs={{0,6},{1,7},{2,4},{3,5},{4,2},{5,3},{6,0},{7,1},{8,14},{9,15},{10,... | collective-permute-start | bytes 393224 | tf_op jit(solution)/shard_map/ppermute | solution.py:1797
  116.5 6.4 %collective-permute-start.20 = (bf16[4,640,128]{2,1,0:T(8,128)(2,1)S(1)}, bf16[4,640,128]{2,1,0:T(8,128)(2,1)S(1)}, u32[]{:S(2)}, u32[]{:S(2)}) collective-permute-start(bf16[4,640,128]{2,1,0:T(8,128)(2,1)S(1)} %pad_maximum_fusion.refs_0_), channel_id=1, source_target_pairs={{0,1},{1,0},{2,3},{3,2},{4,5},{5,4},{6,7},{7,6},{8,9},{9,8},{10,11... | collective-permute-start | bytes 1966088 | tf_op jit(solution)/shard_map/ppermute | solution.py:1797
  117.5 8.8 %collective-permute-start.19 = (bf16[448,128]{1,0:T(8,128)(2,1)S(1)}, bf16[448,128]{1,0:T(8,128)(2,1)S(1)}, u32[]{:S(2)}, u32[]{:S(2)}) collective-permute-start(bf16[448,128]{1,0:T(8,128)(2,1)S(1)} %shard_map.382), channel_id=1, source_target_pairs={{0,6},{1,7},{2,4},{3,5},{4,2},{5,3},{6,0},{7,1},{8,14},{9,15},{10,... | collective-permute-start | bytes 344072 | tf_op jit(solution)/shard_map/ppermute | solution.py:1797
  120.2 6.3 %collective-permute-start.18 = (bf16[448,128]{1,0:T(8,128)(2,1)S(1)}, bf16[448,128]{1,0:T(8,128)(2,1)S(1)}, u32[]{:S(2)}, u32[]{:S(2)}) collective-permute-start(bf16[448,128]{1,0:T(8,128)(2,1)S(1)} %shard_map.382), channel_id=1, source_target_pairs={{0,4},{1,5},{2,6},{3,7},{4,0},{5,1},{6,2},{7,3},{8,12},{9,13},{10,... | collective-permute-start | bytes 344072 | tf_op jit(solution)/shard_map/ppermute | solution.py:1797
  120.8 6.0 %collective-permute-start.17 = (bf16[448,128]{1,0:T(8,128)(2,1)S(1)}, bf16[448,128]{1,0:T(8,128)(2,1)S(1)}, u32[]{:S(2)}, u32[]{:S(2)}) collective-permute-start(bf16[448,128]{1,0:T(8,128)(2,1)S(1)} %shard_map.382), channel_id=1, source_target_pairs={{0,2},{1,3},{2,0},{3,1},{4,6},{5,7},{6,4},{7,5},{8,10},{9,11},{10,... | collective-permute-start | bytes 344072 | tf_op jit(solution)/shard_map/ppermute | solution.py:1797
  (23 other events, 168.1 us)

commit v2 on v1

--- a/solution.py
+++ b/solution.py
@@ -877,7 +877,8 @@
     value_out,
     prob_out,
     attn_out,
-    stats_out,
+    mean_out,
+    rate_out,
     bounds_s,
 ):
     frames = n_attn_out.buffer.shape[0]
@@ -923,8 +924,6 @@
         out.go()
     up_ref = up_ref()
     up_bias = line_of(up_bias_ref)[:, HALF:]
-    lane = lax.broadcasted_iota(jnp.int32, (16, LANES), 1)
-
     @pl.loop(0, frames // TALL, unroll=2)
     def _(block):
         values = dot_nn(n_mlp_out.buffer[rows_of(block, TALL)], up_ref[...])
@@ -935,9 +934,11 @@
             centred = hidden - mean
             rate = lax.rsqrt(jnp.mean(centred * centred, axis=-1, keepdims=True) + EPS)
             at = pl.ds(pl.multiple_of(block * TALL + part * 16, 16), 16)
-            stats_out.buffer[at] = jnp.where(lane == 0, mean, rate)
-
-    stats_out.go()
+            mean_out.buffer[at] = jnp.broadcast_to(mean, (16, LANES))
+            rate_out.buffer[at] = jnp.broadcast_to(rate, (16, LANES))
+
+    mean_out.go()
+    rate_out.go()
     key_code = item_codes(bounds_s, lax.broadcasted_iota(jnp.int32, (1, frames), 1))
 
     low = low_lanes(32)
@@ -1047,7 +1048,8 @@
     n_ref,
     up_ref,
     table_ref,
-    stats_ref,
+    mean_ref,
+    rate_ref,
     cot_ref,
     merge_ref,
     down_ref,
@@ -1098,12 +1100,11 @@
     low = low_lanes(64)
     gate_pre_ref = gate_pre_out.buffer
     n_ref = n_ref()
-    stats_ref = stats_ref()
+    mean_ref, rate_ref = mean_ref(), rate_ref()
     begin(cot_ref, merge_ref, down_ref, attn_ref)
 
     def stat_rows(rows):
-        stats = stats_ref[rows]
-        return stats[:, 0:1], stats[:, 1:2]
+        return mean_ref[rows], rate_ref[rows]
 
     def chunk(start, base=0):
         return pl.ds(pl.multiple_of(start, 64) + base, 64)
@@ -1472,12 +1473,14 @@
         both = mixed_ref[source].astype(F32)
         totals = totals + (both[:, :LANES] + both[:, LANES:])
     totals = totals * (1.0 / HALF)
-    columns = jnp.transpose(jnp.concatenate([totals, jnp.zeros((LANES - 2 * blocks, LANES), F32)], axis=0))
-    lane = lax.broadcasted_iota(jnp.int32, (BLOCK, LANES), 1)
+    high = totals.astype(BF16)
+    low_part = (totals - high.astype(F32)).astype(BF16)
+    both = jnp.concatenate([high, low_part], axis=0)
+    lane = lax.broadcasted_iota(jnp.int32, (4 * blocks, 2 * LANES), 1) // LANES
+    line = lax.broadcasted_iota(jnp.int32, (4 * blocks, 2 * LANES), 0)
     for block in range(blocks):
-        columns_s[block * BLOCK : (block + 1) * BLOCK] = jnp.where(
-            lane == 0, columns[:, 2 * block : 2 * block + 1], columns[:, 2 * block + 1 : 2 * block + 2]
-        )
+        chosen = (lax.rem(line, 2 * blocks) == 2 * block + lane).astype(F32).astype(BF16)
+        columns_s[block * BLOCK : (block + 1) * BLOCK] = dot_tn(both, chosen)
     gate_pre_ref, grad_ref, rate_ref, hat_ref = gate_pre_ref(), grad_ref(), rate_ref(), hat_ref()
     begin(up_ref, norm_hat_ref, other_ref)
     low = low_lanes(64)
@@ -1499,8 +1502,7 @@
             tables = []
             for base in (0, half):
                 rows = chunk(start, base)
-                values = columns_s[rows]
-                table = [values[:, item : item + 1] for item in range(2)]
+                table = [columns_s[rows, item * LANES : (item + 1) * LANES] for item in range(2)]
                 tables.append(table)
                 pre, main_up = pre_part(rows, table, main_up)
                 pre_s[rows, :LANES] = gate_pre_ref[rows]
@@ -1875,15 +1877,15 @@
         content_bias,
         position_bias,
     )
-    near, up_own = lax.optimization_barrier((near, up_own))
-    blocks = far_blocks(near)
     frequency = jnp.exp(jnp.arange(D // 2, dtype=F32) * (-2.0 * math.log(10000.0) / D))
     coarse = jnp.arange(0, total, BLOCK, dtype=F32)[:, None] * frequency[None]
     fine = jnp.arange(BLOCK, dtype=F32)[:, None] * frequency[None]
     coarse_table = jnp.concatenate([jnp.sin(coarse), jnp.cos(coarse)], axis=1)
     fine_table = jnp.concatenate([jnp.sin(fine), jnp.cos(fine)], axis=1)
-
-    n_attn, n_mlp, hat, q_position, query, key, value, prob, attn, stats = kernel_call(
+    near, up_own, coarse_table, fine_table = lax.optimization_barrier((near, up_own, coarse_table, fine_table))
+    blocks = far_blocks(near)
+
+    n_attn, n_mlp, hat, q_position, query, key, value, prob, attn, mean, rate = kernel_call(
         attend_kernel,
         [
             ((total, D), BF16, 1),
@@ -1894,6 +1896,7 @@
             ((total, LANES + D), BF16, 1),
             ((total, LANES), BF16, 1),
             ((total, total), BF16, 1),
+            ((total, LANES), F32, 1),
             ((total, LANES), F32, 1),
             ((total, LANES), F32, 1),
         ],
@@ -1949,6 +1952,7 @@
             whole,
             "v",
             "v",
+            whole,
             whole,
             blocks_part(1, late=True),
             rows_part(D, D, late=True),
@@ -1975,7 +1979,7 @@
             ((3, WINDOW + 2 * MARGIN, LANES), F32),
         ],
         bounds=True,
-    )(lengths, n_mlp, up_own, table, stats, *blocks, merge_weight, down_weight, attn)
+    )(lengths, n_mlp, up_own, table, mean, rate, *blocks, merge_weight, down_weight, attn)
     mixed_own = lax.all_to_all(mixed, "tm", 0, 0, tiled=True)
 
     def own_head(refs, buffer):
@@ -2066,7 +2070,7 @@
             "v",
             late,
         ],
-        [((total, LANES), F32)],
+        [((total, 2 * LANES), F32)],
     )(mixed_own, gate_pre, grad_y, slope, gate_hat, up_own, hat, ln_mlp_gain, from_attn)
     sibling = moved(apart, "tm", 1)
     pre, joined_all = lax.optimization_barrier((pre, joined_all))
@@ -2092,14 +2096,11 @@
     )
     early_near = near_blocks(early_part)
     pairs = kernel_call(pair_kernel, [((own, D), BF16)] * (count // 2), "vv", megas=24)(same, sibling)
+    late_moved, early_near, pairs = lax.optimization_barrier((late_moved, early_near, pairs))
     sums = [pairs[0]] + [moved(pairs[slot], "tm", 2 * slot) for slot in range(1, count // 2)]
-    late_moved, early_near, sums = lax.optimization_barrier((late_moved, early_near, sums))
     (late_part,) = kernel_call(add_streams_kernel, [((late_rows, LANES), BF16)], "v", megas=24)(late_moved)
     late_near = near_blocks(late_part)
     early_all = far_stack(early_near)
-    (grad_frames,) = kernel_call(frames_kernel, [((own, D), F32)], (2 + count // 2) * "v", megas=24)(
-        own_frames, own_cotangent, *sums
-    )
     grad_qkv, grad_pos, grad_down, half_up = kernel_call(
         early_kernel,
         [
@@ -2112,8 +2113,12 @@
         [((count, 4 * HEAD + 8 * share, LANES), BF16)],
         megas=24,
     )(*early_all)
-    late_near, grad_frames, grad_pos = lax.optimization_barrier((late_near, grad_frames, grad_pos))
+    late_near, grad_pos, sums = lax.optimization_barrier((late_near, grad_pos, sums))
     late_parts = far_stack(late_near)
+    (grad_frames,) = kernel_call(frames_kernel, [((own, D), F32)], (2 + count // 2) * "v", megas=24)(
+        own_frames, own_cotangent, *sums
+    )
+    late_parts, grad_frames = lax.optimization_barrier((late_parts, grad_frames))
     late = kernel_call(
         late_kernel,
         [((quarter,), F32)] * 6

time: 133 us -> 134 us (level)
  transfers between devices with their start and end apart: 25 -> 25, of which waited for: 11 -> 13; matrix products, arithmetic and copies ran while one was open for 1% -> 1% of each run, Pallas kernels for 30% -> 30%
where the time goes in v2:
time: 134 us; the launch traced here: 133 us
  Pallas kernels  73.9 us (55%)
  starting transfers between devices  35.7 us (27%)
  waiting for transfers between devices  15.3 us (11%)
  local copies, waits for them, and re-layouts  3.57 us (3%)
  other arithmetic  3.08 us (2%)
    pallas_call x13, Pallas kernels, call(): pl.pallas_call(outer, out_shape=[jax.ShapeDtypeStruct(out[0], out[1]) for...  73.9 us
    ppermute x22, starting transfers between devices, moved(): lax.ppermute(block, axis, [(index, index ^ bits) for index in range(count)])  23.6 us
    ppermute x22, waiting for transfers between devices, moved(): lax.ppermute(block, axis, [(index, index ^ bits) for index in range(count)])  15 us
    all_to_all x1, starting transfers between devices, head_device(): late_moved = lax.all_to_all(late_pack, 'stream', 0, 0, tiled=True)  4.48 us
    all_to_all x1, starting transfers between devices, head_device(): joined_all = lax.all_to_all(joined, 'tm', 0, 0, tiled=True)  3.89 us
    all_to_all x1, starting transfers between devices, head_device(): mixed_own = lax.all_to_all(mixed, 'tm', 0, 0, tiled=True)  3.77 us
    unnamed x44, local copies, waits for them, and re-layouts  3.57 us
  transfers between devices with their start and end apart: 25, of which 13 were waited for; matrix products, arithmetic and copies ran while one was open for 1% of the time, Pallas kernels for 30%

profile of v2, /device:TPU:0, one launch (start us, length us, event | category | flops | bytes accessed | tf_op | source)
XLA Modules:
  0.0 132.9 jit_solution(11019015200473953723)
XLA Ops:
  1.7 4.0 %collective-permute-start.2 = (bf16[128,1024]{1,0:T(8,128)(2,1)S(1)}, bf16[128,1024]{1,0:T(8,128)(2,1)S(1)}, u32[]{:S(2)}, u32[]{:S(2)}) collective-permute-start(bf16[128,1024]{1,0:T(8,128)(2,1)S(1)} %pad_maximum_fusion.2.refs_1_.refs_6_.refs_0_.refs_4_), channel_id=1, source_target_pairs={{0,6},{1,7},{2,4},{3,5},{4,2},{5,3},{6,0},{7,1},{8,14},{9,15},{10,... | collective-permute-start | bytes 786440 | tf_op jit(solution)/shard_map/ppermute | solution.py:1799
  6.9 5.5 %shard_map.373 = (bf16[512,384]{1,0:T(8,128)(2,1)}, f32[2,40,128]{2,1,0:T(8,128)}, bf16[512,384]{1,0:T(8,128)(2,1)}, bf16[512,128]{1,0:T(8,128)(2,1)}, f32[8,128]{1,0:T(8,128)}) custom-call(bf16[512,3072]{1,0:T(8,128)(2,1)} %refs_18_.1, bf16[3072]{0:T(1024)(128)(2,1)} %refs_19_.1, bf16[1536]{0:T(1024)(128)(2,1)} %refs_2_.2, bf16[1536]{0:T(1024)(128)(2,1)} %refs_3_.2, ...), custom_call_target="tpu_custom_call" | custom-call | tf_op jit(solution)/shard_map/pallas_call | solution.py:740
  13.7 3.8 %collective-permute-done.1.refs_5_.refs_10_.refs_4_.refs_8_ = bf16[128,1024]{1,0:T(8,128)(2,1)S(1)} collective-permute-done((bf16[128,1024]{1,0:T(8,128)(2,1)S(1)}, bf16[128,1024]{1,0:T(8,128)(2,1)S(1)}, u32[]{:S(2)}, u32[]{:S(2)}) %collective-permute-start.1) | collective-permute-done | bytes 262176 | tf_op jit(solution)/shard_map/ppermute | solution.py:1799
  21.2 12.8 %shard_map.374 = (bf16[1024,512]{1,0:T(8,128)(2,1)}, bf16[1024,512]{1,0:T(8,128)(2,1)}, bf16[1024,512]{1,0:T(8,128)(2,1)}, bf16[1024,128]{1,0:T(8,128)(2,1)}, bf...) custom-call(s32[1,5]{1,0:T(1,128)} %refs_0_.5, ...), custom_call_target="tpu_custom_call" | custom-call | tf_op jit(solution)/shard_map/pallas_call | solution.py:740
  34.1 15.7 %shard_map.375 = (bf16[8,144,256]{2,1,0:T(8,128)(2,1)}, bf16[1536,128]{1,0:T(8,128)(2,1)}, bf16[1536,128]{1,0:T(8,128)(2,1)}, bf16[1536,128]{1,0:T(8,128)(2,1)},...) custom-call(s32[1,5]{1,0:T(1,128)} %refs_0_.5, ...), custom_call_target="tpu_custom_call" | custom-call | tf_op jit(solution)/shard_map/pallas_call | solution.py:740
  49.8 3.8 %all-to-all-start = ((bf16[8,144,256]{2,1,0:T(8,128)(2,1)}), bf16[8,144,256]{2,1,0:T(8,128)(2,1)S(1)}, u32[]{:S(2)}, u32[]{:S(2)}) async-start(bf16[8,144,256]{2,1,0:T(8,128)(2,1)} %get-tuple-element.136), calls=%async_computation | async-start | bytes 1179648 | tf_op jit(solution)/shard_map/all_to_all | solution.py:1983
  53.6 12.6 %shard_map.376 = (bf16[1024,512]{1,0:T(8,128)(2,1)}, bf16[1024,512]{1,0:T(8,128)(2,1)}, bf16[640,128]{1,0:T(8,128)(2,1)}, bf16[640,128]{1,0:T(8,128)(2,1)}, bf16...) custom-call(bf16[128,1024]{1,0:T(8,128)(2,1)} %copy-done.11, bf16[128,1024]{1,0:T(8,128)(2,1)} %copy-done.15, ...), custom_call_target="tpu_custom_call" | custom-call | tf_op jit(solution)/shard_map/pallas_call | solution.py:740
  67.6 2.5 %shard_map.377 = (bf16[128,512]{1,0:T(8,128)(2,1)}, bf16[8,256,128]{2,1,0:T(8,128)(2,1)S(1)}) custom-call(bf16[128,512]{1,0:T(8,128)(2,1)S(1)} %bitcast.13, bf16[8,144,256]{2,1,0:T(8,128)(2,1)S(1)} %all-to-all-done.refs_1_.refs_0_, bf16[512,512]{1,0:T(8,128)(2,1)S(1)} %copy-done.3, bf16[1536,512]{1,0:T(8,128)(2,1)S(1)} %copy-done.1, ...), custom_call_target="tpu_custom_call" | custom-call | tf_op jit(solution)/shard_map/pallas_call | solution.py:740
  70.9 3.9 %all-to-all-start.1 = ((bf16[8,256,128]{2,1,0:T(8,128)(2,1)}), bf16[8,256,128]{2,1,0:T(8,128)(2,1)S(1)}, u32[]{:S(2)}, u32[]{:S(2)}) async-start(bf16[8,256,128]{2,1,0:T(8,128)(2,1)} %copy-done.6), calls=%async_computation.1 | async-start | bytes 1048576 | tf_op jit(solution)/shard_map/all_to_all | solution.py:2050
  74.8 1.6 %collective-permute-start.7 = (bf16[640,128]{1,0:T(8,128)(2,1)}, bf16[640,128]{1,0:T(8,128)(2,1)S(1)}, u32[]{:S(2)}, u32[]{:S(2)}) collective-permute-start(bf16[640,128]{1,0:T(8,128)(2,1)} %get-tuple-element.164), channel_id=1, source_target_pairs={{0,8},{8,0},{16,24},{24,16},{1,9},{9,1},{17,25},{25,17},{2,10},{10... | collective-permute-start | bytes 491528 | tf_op jit(solution)/shard_map/ppermute | solution.py:1799
  76.3 2.6 %collective-permute-start.8 = (bf16[640,128]{1,0:T(8,128)(2,1)}, bf16[640,128]{1,0:T(8,128)(2,1)S(1)}, u32[]{:S(2)}, u32[]{:S(2)}) collective-permute-start(bf16[640,128]{1,0:T(8,128)(2,1)} %get-tuple-element.165), channel_id=1, source_target_pairs={{0,16},{8,24},{16,0},{24,8},{1,17},{9,25},{17,1},{25,9},{2,18},{10... | collective-permute-start | bytes 491528 | tf_op jit(solution)/shard_map/ppermute | solution.py:1799
  79.7 8.4 %shard_map.378 = (bf16[1024,384]{1,0:T(8,128)(2,1)}, bf16[4,128,512]{2,1,0:T(8,128)(2,1)}, bf16[4,128,512]{2,1,0:T(8,128)(2,1)}, f32[8,512]{1,0:T(8,128)}, f32[192,128]{1,0:T(8,128)}) custom-call(bf16[8,144,256]{2,1,0:T(8,128)(2,1)} %copy-done.2, bf16[1536,128]{1,0:T(8,128)(2,1)} %get-tuple-element.150.refs_1_, ...), custom_call_target="tpu_custom_call" | custom-call | tf_op jit(solution)/shard_map/pallas_call | solution.py:740
  88.9 5.3 %shard_map.379 = bf16[4,448,128]{2,1,0:T(8,128)(2,1)} custom-call(bf16[1024,384]{1,0:T(8,128)(2,1)} %get-tuple-element.156.refs_0_, bf16[1024,512]{1,0:T(8,128)(2,1)} %get-tuple-element.130.refs_1_, bf16[8,256,128]{2,1,0:T(8,128)(2,1)} %copy-done.19, bf16[1024,512]{1,0:T(8,128)(2,1)} %get-tuple-element.158.refs_3_, bf16[128,1024]{1,0:T(8,128)(2,1)} %copy-done.11, ...), custom_call_target="tpu_custom_call" | custom-call | tf_op jit(solution)/shard_map/pallas_call | solution.py:740
  94.3 4.5 %all-to-all-start.2 = ((bf16[4,448,128]{2,1,0:T(8,128)(2,1)}), bf16[4,448,128]{2,1,0:T(8,128)(2,1)S(1)}, u32[]{:S(2)}, u32[]{:S(2)}) async-start(bf16[4,448,128]{2,1,0:T(8,128)(2,1)} %shard_map.379), calls=%async_computation.2 | async-start | bytes 917504 | tf_op jit(solution)/shard_map/all_to_all | solution.py:2093
  99.8 3.0 %collective-permute-start.12 = (bf16[640,128]{1,0:T(8,128)(2,1)S(1)}, bf16[640,128]{1,0:T(8,128)(2,1)S(1)}, u32[]{:S(2)}, u32[]{:S(2)}) collective-permute-start(bf16[640,128]{1,0:T(8,128)(2,1)S(1)} %shard_map.380), channel_id=1, source_target_pairs={{0,6},{1,7},{2,4},{3,5},{4,2},{5,3},{6,0},{7,1},{8,14},{9,15},{10,... | collective-permute-start | bytes 491528 | tf_op jit(solution)/shard_map/ppermute | solution.py:1799
  104.4 3.5 %collective-permute-done.12 = bf16[640,128]{1,0:T(8,128)(2,1)S(1)} collective-permute-done((bf16[640,128]{1,0:T(8,128)(2,1)S(1)}, bf16[640,128]{1,0:T(8,128)(2,1)S(1)}, u32[]{:S(2)}, u32[]{:S(2)}) %collective-permute-start.12) | collective-permute-done | bytes 163872 | tf_op jit(solution)/shard_map/ppermute | solution.py:1799
  107.8 3.3 %collective-permute-done.11 = bf16[640,128]{1,0:T(8,128)(2,1)S(1)} collective-permute-done((bf16[640,128]{1,0:T(8,128)(2,1)S(1)}, bf16[640,128]{1,0:T(8,128)(2,1)S(1)}, u32[]{:S(2)}, u32[]{:S(2)}) %collective-permute-start.11) | collective-permute-done | bytes 163872 | tf_op jit(solution)/shard_map/ppermute | solution.py:1799
  112.8 2.6 %collective-permute-start.16 = (bf16[448,128]{1,0:T(8,128)(2,1)S(1)}, bf16[448,128]{1,0:T(8,128)(2,1)S(1)}, u32[]{:S(2)}, u32[]{:S(2)}) collective-permute-start(bf16[448,128]{1,0:T(8,128)(2,1)S(1)} %shard_map.382), channel_id=1, source_target_pairs={{0,6},{1,7},{2,4},{3,5},{4,2},{5,3},{6,0},{7,1},{8,14},{9,15},{10,... | collective-permute-start | bytes 344072 | tf_op jit(solution)/shard_map/ppermute | solution.py:1799
  116.4 2.6 %collective-permute-start.20 = (bf16[128,512]{1,0:T(8,128)(2,1)S(1)}, bf16[128,512]{1,0:T(8,128)(2,1)S(1)}, u32[]{:S(2)}, u32[]{:S(2)}) collective-permute-start(bf16[128,512]{1,0:T(8,128)(2,1)S(1)} %get-tuple-element.187), channel_id=1, source_target_pairs={{0,6},{1,7},{2,4},{3,5},{4,2},{5,3},{6,0},{7,1},{8,14},{9,15},{10,... | collective-permute-start | bytes 393224 | tf_op jit(solution)/shard_map/ppermute | solution.py:1799
  119.7 1.7 %collective-permute-start.15 = (bf16[448,128]{1,0:T(8,128)(2,1)S(1)}, bf16[448,128]{1,0:T(8,128)(2,1)S(1)}, u32[]{:S(2)}, u32[]{:S(2)}) collective-permute-start(bf16[448,128]{1,0:T(8,128)(2,1)S(1)} %shard_map.382), channel_id=1, source_target_pairs={{0,4},{1,5},{2,6},{3,7},{4,0},{5,1},{6,2},{7,3},{8,12},{9,13},{10,... | collective-permute-start | bytes 344072 | tf_op jit(solution)/shard_map/ppermute | solution.py:1799
  121.4 1.4 %collective-permute-start.14 = (bf16[448,128]{1,0:T(8,128)(2,1)S(1)}, bf16[448,128]{1,0:T(8,128)(2,1)S(1)}, u32[]{:S(2)}, u32[]{:S(2)}) collective-permute-start(bf16[448,128]{1,0:T(8,128)(2,1)S(1)} %shard_map.382), channel_id=1, source_target_pairs={{0,2},{1,3},{2,0},{3,1},{4,6},{5,7},{6,4},{7,5},{8,10},{9,11},{10,... | collective-permute-start | bytes 344072 | tf_op jit(solution)/shard_map/ppermute | solution.py:1799
  122.8 3.4 %shard_map.383 = (f32[128,1536]{1,0:T(8,128)}, f32[128,512]{1,0:T(8,128)}, f32[384,512]{1,0:T(8,128)}, f32[128,3072]{1,0:T(8,128)}) custom-call(bf16[4,640,128]{2,1,0:T(8,128)(2,1)S(1)} %pad_maximum_fusion.refs_0_, bf16[4,640,128]{2,1,0:T(8,128)(2,1)S(1)} %collective-permute-done.17.refs_1_), custom_call_target="tpu_custom_call" | custom-call | tf_op jit(solution)/shard_map/pallas_call | solution.py:740
  127.8 1.9 %shard_map.384 = f32[128,512]{1,0:T(8,128)} custom-call(bf16[128,512]{1,0:T(8,128)(2,1)S(1)} %bitcast.14, bf16[128,512]{1,0:T(8,128)(2,1)S(1)} %bitcast.17, bf16[128,512]{1,0:T(8,128)(2,1)S(1)} %get-tuple-element.192.refs_2_, bf16[128,512]{1,0:T(8,128)(2,1)S(1)} %collective-permute-done.18.refs_3_, bf16[128,512]{1,0:T(8,128)(2,1)S(1)} %collective-permute-done.19.refs_4_, ...), custom_call_target="tpu_custom_call" | custom-call | tf_op jit(solution)/shard_map/pallas_call | solution.py:740
  129.7 2.9 %shard_map.385 = (f32[128]{0:T(128)}, f32[128]{0:T(128)}, f32[128]{0:T(128)}, f32[128]{0:T(128)}, f32[128]{0:T(128)}, /*index=5*/f32[128]{0:T(128)}, f32[128,512...) custom-call(f32[128,3072]{1,0:T(8,128)} %get-tuple-element.197.refs_, ...), custom_call_target="tpu_custom_call", output_to_operand_aliasing={{7}: (0, {})} | custom-call | tf_op jit(solution)/shard_map/pallas_call | solution.py:740
  (92 shorter events, 18.4 us)
Async XLA Ops:
  1.7 12.1 %collective-permute-start.2 = (bf16[128,1024]{1,0:T(8,128)(2,1)S(1)}, bf16[128,1024]{1,0:T(8,128)(2,1)S(1)}, u32[]{:S(2)}, u32[]{:S(2)}) collective-permute-start(bf16[128,1024]{1,0:T(8,128)(2,1)S(1)} %pad_maximum_fusion.2.refs_1_.refs_6_.refs_0_.refs_4_), channel_id=1, source_target_pairs={{0,6},{1,7},{2,4},{3,5},{4,2},{5,3},{6,0},{7,1},{8,14},{9,15},{10,... | collective-permute-start | bytes 786440 | tf_op jit(solution)/shard_map/ppermute | solution.py:1799
  5.6 11.9 %collective-permute-start.1 = (bf16[128,1024]{1,0:T(8,128)(2,1)S(1)}, bf16[128,1024]{1,0:T(8,128)(2,1)S(1)}, u32[]{:S(2)}, u32[]{:S(2)}) collective-permute-start(bf16[128,1024]{1,0:T(8,128)(2,1)S(1)} %pad_maximum_fusion.2.refs_1_.refs_6_.refs_0_.refs_4_), channel_id=1, source_target_pairs={{0,4},{1,5},{2,6},{3,7},{4,0},{5,1},{6,2},{7,3},{8,12},{9,13},{10,... | collective-permute-start | bytes 786440 | tf_op jit(solution)/shard_map/ppermute | solution.py:1799
  6.1 11.7 %collective-permute-start = (bf16[128,1024]{1,0:T(8,128)(2,1)S(1)}, bf16[128,1024]{1,0:T(8,128)(2,1)S(1)}, u32[]{:S(2)}, u32[]{:S(2)}) collective-permute-start(bf16[128,1024]{1,0:T(8,128)(2,1)S(1)} %pad_maximum_fusion.2.refs_1_.refs_6_.refs_0_.refs_4_), channel_id=1, source_target_pairs={{0,2},{1,3},{2,0},{3,1},{4,6},{5,7},{6,4},{7,5},{8,10},{9,11},{10,... | collective-permute-start | bytes 786440 | tf_op jit(solution)/shard_map/ppermute | solution.py:1799
  17.9 1.9 %collective-permute-start.4 = (bf16[128,1024]{1,0:T(8,128)(2,1)S(1)}, bf16[128,1024]{1,0:T(8,128)(2,1)S(1)}, u32[]{:S(2)}, u32[]{:S(2)}) collective-permute-start(bf16[128,1024]{1,0:T(8,128)(2,1)S(1)} %collective-permute-done.refs_3_.refs_8_.refs_2_.refs_6_), channel_id=1, source_target_pairs={{0,1},{1,0},{2,3},{3,2},{4,5},{5,4},{6,7},{7,6},{8,9},{9,8},{10,11... | collective-permute-start | bytes 786440 | tf_op jit(solution)/shard_map/ppermute | solution.py:1799
  18.4 1.8 %collective-permute-start.5 = (bf16[128,1024]{1,0:T(8,128)(2,1)S(1)}, bf16[128,1024]{1,0:T(8,128)(2,1)S(1)}, u32[]{:S(2)}, u32[]{:S(2)}) collective-permute-start(bf16[128,1024]{1,0:T(8,128)(2,1)S(1)} %collective-permute-done.1.refs_5_.refs_10_.refs_4_.refs_8_), channel_id=1, source_target_pairs={{0,1},{1,0},{2,3},{3,2},{4,5},{5,4},{6,7},{7,6},{8,9},{9,8},{10,11... | collective-permute-start | bytes 786440 | tf_op jit(solution)/shard_map/ppermute | solution.py:1799
  18.4 2.1 %collective-permute-start.6 = (bf16[128,1024]{1,0:T(8,128)(2,1)S(1)}, bf16[128,1024]{1,0:T(8,128)(2,1)S(1)}, u32[]{:S(2)}, u32[]{:S(2)}) collective-permute-start(bf16[128,1024]{1,0:T(8,128)(2,1)S(1)} %collective-permute-done.2.refs_7_.refs_12_.refs_6_.refs_10_), channel_id=1, source_target_pairs={{0,1},{1,0},{2,3},{3,2},{4,5},{5,4},{6,7},{7,6},{8,9},{9,8},{10,11... | collective-permute-start | bytes 786440 | tf_op jit(solution)/shard_map/ppermute | solution.py:1799
  49.8 16.5 %all-to-all-start = ((bf16[8,144,256]{2,1,0:T(8,128)(2,1)}), bf16[8,144,256]{2,1,0:T(8,128)(2,1)S(1)}, u32[]{:S(2)}, u32[]{:S(2)}) async-start(bf16[8,144,256]{2,1,0:T(8,128)(2,1)} %get-tuple-element.136), calls=%async_computation | async-start | bytes 1179648 | tf_op jit(solution)/shard_map/all_to_all | solution.py:1983
  70.9 17.2 %all-to-all-start.1 = ((bf16[8,256,128]{2,1,0:T(8,128)(2,1)}), bf16[8,256,128]{2,1,0:T(8,128)(2,1)S(1)}, u32[]{:S(2)}, u32[]{:S(2)}) async-start(bf16[8,256,128]{2,1,0:T(8,128)(2,1)} %copy-done.6), calls=%async_computation.1 | async-start | bytes 1048576 | tf_op jit(solution)/shard_map/all_to_all | solution.py:2050
  74.8 19.5 %collective-permute-start.7 = (bf16[640,128]{1,0:T(8,128)(2,1)}, bf16[640,128]{1,0:T(8,128)(2,1)S(1)}, u32[]{:S(2)}, u32[]{:S(2)}) collective-permute-start(bf16[640,128]{1,0:T(8,128)(2,1)} %get-tuple-element.164), channel_id=1, source_target_pairs={{0,8},{8,0},{16,24},{24,16},{1,9},{9,1},{17,25},{25,17},{2,10},{10... | collective-permute-start | bytes 491528 | tf_op jit(solution)/shard_map/ppermute | solution.py:1799
  76.3 17.9 %collective-permute-start.8 = (bf16[640,128]{1,0:T(8,128)(2,1)}, bf16[640,128]{1,0:T(8,128)(2,1)S(1)}, u32[]{:S(2)}, u32[]{:S(2)}) collective-permute-start(bf16[640,128]{1,0:T(8,128)(2,1)} %get-tuple-element.165), channel_id=1, source_target_pairs={{0,16},{8,24},{16,0},{24,8},{1,17},{9,25},{17,1},{25,9},{2,18},{10... | collective-permute-start | bytes 491528 | tf_op jit(solution)/shard_map/ppermute | solution.py:1799
  78.9 15.4 %collective-permute-start.9 = (bf16[640,128]{1,0:T(8,128)(2,1)S(1)}, bf16[640,128]{1,0:T(8,128)(2,1)S(1)}, u32[]{:S(2)}, u32[]{:S(2)}) collective-permute-start(bf16[640,128]{1,0:T(8,128)(2,1)S(1)} %copy-done.21), channel_id=1, source_target_pairs={{0,24},{8,16},{16,8},{24,0},{1,25},{9,17},{17,9},{25,1},{2,26},{10... | collective-permute-start | bytes 491528 | tf_op jit(solution)/shard_map/ppermute | solution.py:1799
  94.3 17.4 %all-to-all-start.2 = ((bf16[4,448,128]{2,1,0:T(8,128)(2,1)}), bf16[4,448,128]{2,1,0:T(8,128)(2,1)S(1)}, u32[]{:S(2)}, u32[]{:S(2)}) async-start(bf16[4,448,128]{2,1,0:T(8,128)(2,1)} %shard_map.379), calls=%async_computation.2 | async-start | bytes 917504 | tf_op jit(solution)/shard_map/all_to_all | solution.py:2093
  98.8 4.6 %collective-permute-start.13 = (bf16[4,128,512]{2,1,0:T(8,128)(2,1)S(1)}, bf16[4,128,512]{2,1,0:T(8,128)(2,1)S(1)}, u32[]{:S(2)}, u32[]{:S(2)}) collective-permute-start(bf16[4,128,512]{2,1,0:T(8,128)(2,1)S(1)} %copy-done.20), channel_id=1, source_target_pairs={{0,1},{1,0},{2,3},{3,2},{4,5},{5,4},{6,7},{7,6},{8,9},{9,8},{10,11... | collective-permute-start | bytes 1572872 | tf_op jit(solution)/shard_map/ppermute | solution.py:1799
  99.8 8.1 %collective-permute-start.12 = (bf16[640,128]{1,0:T(8,128)(2,1)S(1)}, bf16[640,128]{1,0:T(8,128)(2,1)S(1)}, u32[]{:S(2)}, u32[]{:S(2)}) collective-permute-start(bf16[640,128]{1,0:T(8,128)(2,1)S(1)} %shard_map.380), channel_id=1, source_target_pairs={{0,6},{1,7},{2,4},{3,5},{4,2},{5,3},{6,0},{7,1},{8,14},{9,15},{10,... | collective-permute-start | bytes 491528 | tf_op jit(solution)/shard_map/ppermute | solution.py:1799
  102.7 8.4 %collective-permute-start.11 = (bf16[640,128]{1,0:T(8,128)(2,1)S(1)}, bf16[640,128]{1,0:T(8,128)(2,1)S(1)}, u32[]{:S(2)}, u32[]{:S(2)}) collective-permute-start(bf16[640,128]{1,0:T(8,128)(2,1)S(1)} %shard_map.380), channel_id=1, source_target_pairs={{0,4},{1,5},{2,6},{3,7},{4,0},{5,1},{6,2},{7,3},{8,12},{9,13},{10,... | collective-permute-start | bytes 491528 | tf_op jit(solution)/shard_map/ppermute | solution.py:1799
  103.3 8.1 %collective-permute-start.10 = (bf16[640,128]{1,0:T(8,128)(2,1)S(1)}, bf16[640,128]{1,0:T(8,128)(2,1)S(1)}, u32[]{:S(2)}, u32[]{:S(2)}) collective-permute-start(bf16[640,128]{1,0:T(8,128)(2,1)S(1)} %shard_map.380), channel_id=1, source_target_pairs={{0,2},{1,3},{2,0},{3,1},{4,6},{5,7},{6,4},{7,5},{8,10},{9,11},{10,... | collective-permute-start | bytes 491528 | tf_op jit(solution)/shard_map/ppermute | solution.py:1799
  111.8 9.6 %collective-permute-start.17 = (bf16[4,640,128]{2,1,0:T(8,128)(2,1)S(1)}, bf16[4,640,128]{2,1,0:T(8,128)(2,1)S(1)}, u32[]{:S(2)}, u32[]{:S(2)}) collective-permute-start(bf16[4,640,128]{2,1,0:T(8,128)(2,1)S(1)} %pad_maximum_fusion.refs_0_), channel_id=1, source_target_pairs={{0,1},{1,0},{2,3},{3,2},{4,5},{5,4},{6,7},{7,6},{8,9},{9,8},{10,11... | collective-permute-start | bytes 1966088 | tf_op jit(solution)/shard_map/ppermute | solution.py:1799
  112.8 6.9 %collective-permute-start.16 = (bf16[448,128]{1,0:T(8,128)(2,1)S(1)}, bf16[448,128]{1,0:T(8,128)(2,1)S(1)}, u32[]{:S(2)}, u32[]{:S(2)}) collective-permute-start(bf16[448,128]{1,0:T(8,128)(2,1)S(1)} %shard_map.382), channel_id=1, source_target_pairs={{0,6},{1,7},{2,4},{3,5},{4,2},{5,3},{6,0},{7,1},{8,14},{9,15},{10,... | collective-permute-start | bytes 344072 | tf_op jit(solution)/shard_map/ppermute | solution.py:1799
  115.4 12.2 %collective-permute-start.18 = (bf16[128,512]{1,0:T(8,128)(2,1)S(1)}, bf16[128,512]{1,0:T(8,128)(2,1)S(1)}, u32[]{:S(2)}, u32[]{:S(2)}) collective-permute-start(bf16[128,512]{1,0:T(8,128)(2,1)S(1)} %get-tuple-element.185), channel_id=1, source_target_pairs={{0,2},{1,3},{2,0},{3,1},{4,6},{5,7},{6,4},{7,5},{8,10},{9,11},{10,... | collective-permute-start | bytes 393224 | tf_op jit(solution)/shard_map/ppermute | solution.py:1799
  116.0 11.7 %collective-permute-start.19 = (bf16[128,512]{1,0:T(8,128)(2,1)S(1)}, bf16[128,512]{1,0:T(8,128)(2,1)S(1)}, u32[]{:S(2)}, u32[]{:S(2)}) collective-permute-start(bf16[128,512]{1,0:T(8,128)(2,1)S(1)} %get-tuple-element.186), channel_id=1, source_target_pairs={{0,4},{1,5},{2,6},{3,7},{4,0},{5,1},{6,2},{7,3},{8,12},{9,13},{10,... | collective-permute-start | bytes 393224 | tf_op jit(solution)/shard_map/ppermute | solution.py:1799
  116.4 11.3 %collective-permute-start.20 = (bf16[128,512]{1,0:T(8,128)(2,1)S(1)}, bf16[128,512]{1,0:T(8,128)(2,1)S(1)}, u32[]{:S(2)}, u32[]{:S(2)}) collective-permute-start(bf16[128,512]{1,0:T(8,128)(2,1)S(1)} %get-tuple-element.187), channel_id=1, source_target_pairs={{0,6},{1,7},{2,4},{3,5},{4,2},{5,3},{6,0},{7,1},{8,14},{9,15},{10,... | collective-permute-start | bytes 393224 | tf_op jit(solution)/shard_map/ppermute | solution.py:1799
  119.7 7.7 %collective-permute-start.15 = (bf16[448,128]{1,0:T(8,128)(2,1)S(1)}, bf16[448,128]{1,0:T(8,128)(2,1)S(1)}, u32[]{:S(2)}, u32[]{:S(2)}) collective-permute-start(bf16[448,128]{1,0:T(8,128)(2,1)S(1)} %shard_map.382), channel_id=1, source_target_pairs={{0,4},{1,5},{2,6},{3,7},{4,0},{5,1},{6,2},{7,3},{8,12},{9,13},{10,... | collective-permute-start | bytes 344072 | tf_op jit(solution)/shard_map/ppermute | solution.py:1799
  121.4 6.3 %collective-permute-start.14 = (bf16[448,128]{1,0:T(8,128)(2,1)S(1)}, bf16[448,128]{1,0:T(8,128)(2,1)S(1)}, u32[]{:S(2)}, u32[]{:S(2)}) collective-permute-start(bf16[448,128]{1,0:T(8,128)(2,1)S(1)} %shard_map.382), channel_id=1, source_target_pairs={{0,2},{1,3},{2,0},{3,1},{4,6},{5,7},{6,4},{7,5},{8,10},{9,11},{10,... | collective-permute-start | bytes 344072 | tf_op jit(solution)/shard_map/ppermute | solution.py:1799
  127.7 2.0 %collective-permute-start.21 = (bf16[4,448,128]{2,1,0:T(8,128)(2,1)S(1)}, bf16[4,448,128]{2,1,0:T(8,128)(2,1)S(1)}, u32[]{:S(2)}, u32[]{:S(2)}) collective-permute-start(bf16[4,448,128]{2,1,0:T(8,128)(2,1)S(1)} %pad_maximum_fusion.1.refs_1_), channel_id=1, source_target_pairs={{0,1},{1,0},{2,3},{3,2},{4,5},{5,4},{6,7},{7,6},{8,9},{9,8},{10,11... | collective-permute-start | bytes 1376264 | tf_op jit(solution)/shard_map/ppermute | solution.py:1799
  (23 other events, 160.0 us)

commit v3 on v2

--- a/solution.py
+++ b/solution.py
@@ -889,6 +889,8 @@
     content, position = bias_ref[0:1], bias_ref[1:2]
     x_ref = x_ref()
     begin(up_ref)
+    lane = lax.broadcasted_iota(jnp.int32, (1, LANES), 1)
+    spare = ((lane == HEAD) | (lane == HEAD + 1)).astype(F32)
 
     @pl.loop(0, frames // TALL, unroll=4)
     def _(block):
@@ -905,7 +907,7 @@
         q_position = (query + position).astype(BF16)
         q_position_out.buffer[rows] = q_position
         key_out.buffer[rows, :LANES] = parts[:, LANES : 2 * LANES].astype(BF16)
-        value_out.buffer[rows] = parts[:, 2 * LANES :].astype(BF16)
+        value_out.buffer[rows] = (parts[:, 2 * LANES :] + spare).astype(BF16)
         projected = dot_nt(q_position, pos_ref[...])
         for part in range(TALL // 32):
             at = pl.ds(pl.multiple_of(block * TALL + part * 32, 32), 32)
@@ -945,7 +947,6 @@
     for block in range(frames // TALL):
         rows = pl.ds(block * TALL, TALL)
         raw = dot_nt(query_out.buffer[rows], key_out.buffer[...])
-        shares = []
         for part in range(TALL // 32):
             start = block * TALL + part * 32
             index = start + lax.broadcasted_iota(jnp.int32, (32, 1), 0)
@@ -954,14 +955,12 @@
             )
             weight = jnp.exp(scaled - jnp.max(scaled, axis=1, keepdims=True))
             prob_out.buffer[pl.ds(start, 32)] = weight.astype(BF16)
-            shares.append(1.0 / jnp.sum(weight, axis=1, keepdims=True))
         prob_out.go(rows)
         attn = dot_nn(prob_out.buffer[rows], value_out.buffer[...])
         for part in range(TALL // 32):
-            share = shares[part]
-            attn_out.buffer[pl.ds(block * TALL + part * 32, 32)] = jnp.where(
-                low, attn[part * 32 : part * 32 + 32] * share, share
-            )
+            own = attn[part * 32 : part * 32 + 32]
+            share = 1.0 / own[:, HEAD : HEAD + 1]
+            attn_out.buffer[pl.ds(block * TALL + part * 32, 32)] = jnp.where(low, own * share, share)
 
 
 def fill_margins(wide_s, frames):
@@ -1354,7 +1353,12 @@
         rows = rows_of(block, TALL)
         branch = dot_nt(cot_ref[rows], merge_ref[...]).astype(BF16)
         branch_out.buffer[rows] = branch
-        grad_s[rows] = (dot_nt(branch, head_ref[...]) * attn_ref[rows, HEAD : HEAD + 1]).astype(BF16)
+        grad = (dot_nt(branch, head_ref[...]) * attn_ref[rows, HEAD : HEAD + 1]).astype(BF16).astype(F32)
+        delta = jnp.sum(grad * attn_ref[rows], axis=1, keepdims=True)
+        high = delta.astype(BF16).astype(F32)
+        lane = lax.broadcasted_iota(jnp.int32, (TALL, LANES), 1)
+        grad = jnp.where(lane == HEAD, -high, jnp.where(lane == HEAD + 1, high - delta, grad))
+        grad_s[rows] = grad.astype(BF16)
 
     branch_out.go()
     value_ref, prob_ref = value_ref(), prob_ref()
@@ -1369,8 +1373,7 @@
         for part in range(TALL // 32):
             at = pl.ds(pl.multiple_of(block * TALL + part * 32, 32), 32)
             inner = slice(part * 32, part * 32 + 32)
-            delta = jnp.sum(grad[inner].astype(F32) * attn_ref[at], axis=1, keepdims=True)
-            raw_s[at] = (prob_ref[at].astype(F32) * (score[inner] - delta)).astype(BF16)
+            raw_s[at] = (prob_ref[at].astype(F32) * score[inner]).astype(BF16)
         query = dot_nn(raw_s[rows], key_ref[...]) * 0.125
         for part in range(TALL // 32):
             at = pl.ds(pl.multiple_of(block * TALL + part * 32, 32), 32)
@@ -2096,8 +2099,8 @@
     )
     early_near = near_blocks(early_part)
     pairs = kernel_call(pair_kernel, [((own, D), BF16)] * (count // 2), "vv", megas=24)(same, sibling)
-    late_moved, early_near, pairs = lax.optimization_barrier((late_moved, early_near, pairs))
     sums = [pairs[0]] + [moved(pairs[slot], "tm", 2 * slot) for slot in range(1, count // 2)]
+    late_moved, early_near, sums[1], sums[2] = lax.optimization_barrier((late_moved, early_near, sums[1], sums[2]))
     (late_part,) = kernel_call(add_streams_kernel, [((late_rows, LANES), BF16)], "v", megas=24)(late_moved)
     late_near = near_blocks(late_part)
     early_all = far_stack(early_near)

time: 134 us -> 132 us (0.985)
  transfers between devices with their start and end apart: 25 -> 25, of which waited for: 13 -> 11; matrix products, arithmetic and copies ran while one was open for 1% -> 1% of each run, Pallas kernels for 30% -> 30%
where the time goes in v3:
time: 132 us
  Pallas kernels  74.8 us (57%)
  starting transfers between devices  35.1 us (27%)
  waiting for transfers between devices  14.4 us (11%)
  local copies, waits for them, and re-layouts  3.57 us (3%)
  other arithmetic  3.08 us (2%)
    pallas_call x13, Pallas kernels, call(): pl.pallas_call(outer, out_shape=[jax.ShapeDtypeStruct(out[0], out[1]) for...  74.8 us
    ppermute x22, starting transfers between devices, moved(): lax.ppermute(block, axis, [(index, index ^ bits) for index in range(count)])  22.9 us
    ppermute x22, waiting for transfers between devices, moved(): lax.ppermute(block, axis, [(index, index ^ bits) for index in range(count)])  14.4 us
    all_to_all x1, starting transfers between devices, head_device(): late_moved = lax.all_to_all(late_pack, 'stream', 0, 0, tiled=True)  4.48 us
    all_to_all x1, starting transfers between devices, head_device(): joined_all = lax.all_to_all(joined, 'tm', 0, 0, tiled=True)  3.89 us
    all_to_all x1, starting transfers between devices, head_device(): mixed_own = lax.all_to_all(mixed, 'tm', 0, 0, tiled=True)  3.77 us
    unnamed x44, local copies, waits for them, and re-layouts  3.57 us
  transfers between devices with their start and end apart: 25, of which 11 were waited for; matrix products, arithmetic and copies ran while one was open for 1% of the time, Pallas kernels for 30%

profile of v3, /device:TPU:0, one launch (start us, length us, event | category | flops | bytes accessed | tf_op | source)
XLA Modules:
  0.0 132.2 jit_solution(8149079973456811821)
XLA Ops:
  1.7 4.0 %collective-permute-start.2 = (bf16[128,1024]{1,0:T(8,128)(2,1)S(1)}, bf16[128,1024]{1,0:T(8,128)(2,1)S(1)}, u32[]{:S(2)}, u32[]{:S(2)}) collective-permute-start(bf16[128,1024]{1,0:T(8,128)(2,1)S(1)} %pad_maximum_fusion.2.refs_1_.refs_6_.refs_0_.refs_4_), channel_id=1, source_target_pairs={{0,6},{1,7},{2,4},{3,5},{4,2},{5,3},{6,0},{7,1},{8,14},{9,15},{10,... | collective-permute-start | bytes 786440 | tf_op jit(solution)/shard_map/ppermute | solution.py:1802
  6.9 5.5 %shard_map.373 = (bf16[512,384]{1,0:T(8,128)(2,1)}, f32[2,40,128]{2,1,0:T(8,128)}, bf16[512,384]{1,0:T(8,128)(2,1)}, bf16[512,128]{1,0:T(8,128)(2,1)}, f32[8,128]{1,0:T(8,128)}) custom-call(bf16[512,3072]{1,0:T(8,128)(2,1)} %refs_18_.1, bf16[3072]{0:T(1024)(128)(2,1)} %refs_19_.1, bf16[1536]{0:T(1024)(128)(2,1)} %refs_2_.2, bf16[1536]{0:T(1024)(128)(2,1)} %refs_3_.2, ...), custom_call_target="tpu_custom_call" | custom-call | tf_op jit(solution)/shard_map/pallas_call | solution.py:740
  13.7 3.8 %collective-permute-done.1.refs_5_.refs_10_.refs_4_.refs_8_ = bf16[128,1024]{1,0:T(8,128)(2,1)S(1)} collective-permute-done((bf16[128,1024]{1,0:T(8,128)(2,1)S(1)}, bf16[128,1024]{1,0:T(8,128)(2,1)S(1)}, u32[]{:S(2)}, u32[]{:S(2)}) %collective-permute-start.1) | collective-permute-done | bytes 262176 | tf_op jit(solution)/shard_map/ppermute | solution.py:1802
  21.2 12.8 %shard_map.374 = (bf16[1024,512]{1,0:T(8,128)(2,1)}, bf16[1024,512]{1,0:T(8,128)(2,1)}, bf16[1024,512]{1,0:T(8,128)(2,1)}, bf16[1024,128]{1,0:T(8,128)(2,1)}, bf...) custom-call(s32[1,5]{1,0:T(1,128)} %refs_0_.5, ...), custom_call_target="tpu_custom_call" | custom-call | tf_op jit(solution)/shard_map/pallas_call | solution.py:740
  34.0 16.6 %shard_map.375 = (bf16[8,144,256]{2,1,0:T(8,128)(2,1)}, bf16[1536,128]{1,0:T(8,128)(2,1)}, bf16[1536,128]{1,0:T(8,128)(2,1)}, bf16[1536,128]{1,0:T(8,128)(2,1)},...) custom-call(s32[1,5]{1,0:T(1,128)} %refs_0_.5, ...), custom_call_target="tpu_custom_call" | custom-call | tf_op jit(solution)/shard_map/pallas_call | solution.py:740
  50.6 3.8 %all-to-all-start = ((bf16[8,144,256]{2,1,0:T(8,128)(2,1)}), bf16[8,144,256]{2,1,0:T(8,128)(2,1)S(1)}, u32[]{:S(2)}, u32[]{:S(2)}) async-start(bf16[8,144,256]{2,1,0:T(8,128)(2,1)} %get-tuple-element.134), calls=%async_computation | async-start | bytes 1179648 | tf_op jit(solution)/shard_map/all_to_all | solution.py:1986
  54.5 12.6 %shard_map.376 = (bf16[1024,512]{1,0:T(8,128)(2,1)}, bf16[1024,512]{1,0:T(8,128)(2,1)}, bf16[640,128]{1,0:T(8,128)(2,1)}, bf16[640,128]{1,0:T(8,128)(2,1)}, bf16...) custom-call(bf16[128,1024]{1,0:T(8,128)(2,1)} %copy-done.11, bf16[128,1024]{1,0:T(8,128)(2,1)} %copy-done.15, ...), custom_call_target="tpu_custom_call" | custom-call | tf_op jit(solution)/shard_map/pallas_call | solution.py:740
  68.4 2.5 %shard_map.377 = (bf16[128,512]{1,0:T(8,128)(2,1)}, bf16[8,256,128]{2,1,0:T(8,128)(2,1)S(1)}) custom-call(bf16[128,512]{1,0:T(8,128)(2,1)S(1)} %bitcast.13, bf16[8,144,256]{2,1,0:T(8,128)(2,1)S(1)} %all-to-all-done.refs_1_.refs_0_, bf16[512,512]{1,0:T(8,128)(2,1)S(1)} %copy-done.3, bf16[1536,512]{1,0:T(8,128)(2,1)S(1)} %copy-done.1, ...), custom_call_target="tpu_custom_call" | custom-call | tf_op jit(solution)/shard_map/pallas_call | solution.py:740
  71.7 3.9 %all-to-all-start.1 = ((bf16[8,256,128]{2,1,0:T(8,128)(2,1)}), bf16[8,256,128]{2,1,0:T(8,128)(2,1)S(1)}, u32[]{:S(2)}, u32[]{:S(2)}) async-start(bf16[8,256,128]{2,1,0:T(8,128)(2,1)} %copy-done.6), calls=%async_computation.1 | async-start | bytes 1048576 | tf_op jit(solution)/shard_map/all_to_all | solution.py:2053
  75.6 1.6 %collective-permute-start.7 = (bf16[640,128]{1,0:T(8,128)(2,1)}, bf16[640,128]{1,0:T(8,128)(2,1)S(1)}, u32[]{:S(2)}, u32[]{:S(2)}) collective-permute-start(bf16[640,128]{1,0:T(8,128)(2,1)} %get-tuple-element.162), channel_id=1, source_target_pairs={{0,8},{8,0},{16,24},{24,16},{1,9},{9,1},{17,25},{25,17},{2,10},{10... | collective-permute-start | bytes 491528 | tf_op jit(solution)/shard_map/ppermute | solution.py:1802
  77.2 2.6 %collective-permute-start.8 = (bf16[640,128]{1,0:T(8,128)(2,1)}, bf16[640,128]{1,0:T(8,128)(2,1)S(1)}, u32[]{:S(2)}, u32[]{:S(2)}) collective-permute-start(bf16[640,128]{1,0:T(8,128)(2,1)} %get-tuple-element.163), channel_id=1, source_target_pairs={{0,16},{8,24},{16,0},{24,8},{1,17},{9,25},{17,1},{25,9},{2,18},{10... | collective-permute-start | bytes 491528 | tf_op jit(solution)/shard_map/ppermute | solution.py:1802
  80.5 8.4 %shard_map.378 = (bf16[1024,384]{1,0:T(8,128)(2,1)}, bf16[4,128,512]{2,1,0:T(8,128)(2,1)}, bf16[4,128,512]{2,1,0:T(8,128)(2,1)}, f32[8,512]{1,0:T(8,128)}, f32[192,128]{1,0:T(8,128)}) custom-call(bf16[8,144,256]{2,1,0:T(8,128)(2,1)} %copy-done.2, bf16[1536,128]{1,0:T(8,128)(2,1)} %get-tuple-element.148.refs_1_, ...), custom_call_target="tpu_custom_call" | custom-call | tf_op jit(solution)/shard_map/pallas_call | solution.py:740
  89.7 5.3 %shard_map.379 = bf16[4,448,128]{2,1,0:T(8,128)(2,1)} custom-call(bf16[1024,384]{1,0:T(8,128)(2,1)} %get-tuple-element.154.refs_0_, bf16[1024,512]{1,0:T(8,128)(2,1)} %get-tuple-element.128.refs_1_, bf16[8,256,128]{2,1,0:T(8,128)(2,1)} %copy-done.19, bf16[1024,512]{1,0:T(8,128)(2,1)} %get-tuple-element.156.refs_3_, bf16[128,1024]{1,0:T(8,128)(2,1)} %copy-done.11, ...), custom_call_target="tpu_custom_call" | custom-call | tf_op jit(solution)/shard_map/pallas_call | solution.py:740
  95.1 4.5 %all-to-all-start.2 = ((bf16[4,448,128]{2,1,0:T(8,128)(2,1)}), bf16[4,448,128]{2,1,0:T(8,128)(2,1)S(1)}, u32[]{:S(2)}, u32[]{:S(2)}) async-start(bf16[4,448,128]{2,1,0:T(8,128)(2,1)} %shard_map.379), calls=%async_computation.2 | async-start | bytes 917504 | tf_op jit(solution)/shard_map/all_to_all | solution.py:2096
  100.6 3.0 %collective-permute-start.12 = (bf16[640,128]{1,0:T(8,128)(2,1)S(1)}, bf16[640,128]{1,0:T(8,128)(2,1)S(1)}, u32[]{:S(2)}, u32[]{:S(2)}) collective-permute-start(bf16[640,128]{1,0:T(8,128)(2,1)S(1)} %shard_map.380), channel_id=1, source_target_pairs={{0,6},{1,7},{2,4},{3,5},{4,2},{5,3},{6,0},{7,1},{8,14},{9,15},{10,... | collective-permute-start | bytes 491528 | tf_op jit(solution)/shard_map/ppermute | solution.py:1802
  105.2 2.0 %collective-permute-start.14 = (bf16[128,512]{1,0:T(8,128)(2,1)S(1)}, bf16[128,512]{1,0:T(8,128)(2,1)S(1)}, u32[]{:S(2)}, u32[]{:S(2)}) collective-permute-start(bf16[128,512]{1,0:T(8,128)(2,1)S(1)} %get-tuple-element.172), channel_id=1, source_target_pairs={{0,2},{1,3},{2,0},{3,1},{4,6},{5,7},{6,4},{7,5},{8,10},{9,11},{10,... | collective-permute-start | bytes 393224 | tf_op jit(solution)/shard_map/ppermute | solution.py:1802
  108.7 3.3 %collective-permute-done.11 = bf16[640,128]{1,0:T(8,128)(2,1)S(1)} collective-permute-done((bf16[640,128]{1,0:T(8,128)(2,1)S(1)}, bf16[640,128]{1,0:T(8,128)(2,1)S(1)}, u32[]{:S(2)}, u32[]{:S(2)}) %collective-permute-start.11) | collective-permute-done | bytes 163872 | tf_op jit(solution)/shard_map/ppermute | solution.py:1802
  112.7 2.4 %collective-permute-done.14.refs_3_ = bf16[128,512]{1,0:T(8,128)(2,1)S(1)} collective-permute-done((bf16[128,512]{1,0:T(8,128)(2,1)S(1)}, bf16[128,512]{1,0:T(8,128)(2,1)S(1)}, u32[]{:S(2)}, u32[]{:S(2)}) %collective-permute-start.14) | collective-permute-done | bytes 131104 | tf_op jit(solution)/shard_map/ppermute | solution.py:1802
  115.3 1.6 %collective-permute-start.20 = (bf16[128,512]{1,0:T(8,128)(2,1)S(1)}, bf16[128,512]{1,0:T(8,128)(2,1)S(1)}, u32[]{:S(2)}, u32[]{:S(2)}) collective-permute-start(bf16[128,512]{1,0:T(8,128)(2,1)S(1)} %get-tuple-element.183), channel_id=1, source_target_pairs={{0,6},{1,7},{2,4},{3,5},{4,2},{5,3},{6,0},{7,1},{8,14},{9,15},{10,... | collective-permute-start | bytes 393224 | tf_op jit(solution)/shard_map/ppermute | solution.py:1802
  117.7 1.5 %collective-permute-start.18 = (bf16[448,128]{1,0:T(8,128)(2,1)S(1)}, bf16[448,128]{1,0:T(8,128)(2,1)S(1)}, u32[]{:S(2)}, u32[]{:S(2)}) collective-permute-start(bf16[448,128]{1,0:T(8,128)(2,1)S(1)} %shard_map.382), channel_id=1, source_target_pairs={{0,6},{1,7},{2,4},{3,5},{4,2},{5,3},{6,0},{7,1},{8,14},{9,15},{10,... | collective-permute-start | bytes 344072 | tf_op jit(solution)/shard_map/ppermute | solution.py:1802
  121.3 3.4 %shard_map.383 = (f32[128,1536]{1,0:T(8,128)}, f32[128,512]{1,0:T(8,128)}, f32[384,512]{1,0:T(8,128)}, f32[128,3072]{1,0:T(8,128)}) custom-call(bf16[4,640,128]{2,1,0:T(8,128)(2,1)S(1)} %pad_maximum_fusion.refs_0_, bf16[4,640,128]{2,1,0:T(8,128)(2,1)S(1)} %collective-permute-done.19.refs_1_), custom_call_target="tpu_custom_call" | custom-call | tf_op jit(solution)/shard_map/pallas_call | solution.py:740
  125.0 2.0 %collective-permute-done.17 = bf16[448,128]{1,0:T(8,128)(2,1)S(1)} collective-permute-done((bf16[448,128]{1,0:T(8,128)(2,1)S(1)}, bf16[448,128]{1,0:T(8,128)(2,1)S(1)}, u32[]{:S(2)}, u32[]{:S(2)}) %collective-permute-start.17) | collective-permute-done | bytes 114720 | tf_op jit(solution)/shard_map/ppermute | solution.py:1802
  127.1 1.9 %shard_map.384 = f32[128,512]{1,0:T(8,128)} custom-call(bf16[128,512]{1,0:T(8,128)(2,1)S(1)} %bitcast.14, bf16[128,512]{1,0:T(8,128)(2,1)S(1)} %bitcast.17, bf16[128,512]{1,0:T(8,128)(2,1)S(1)} %get-tuple-element.188.refs_2_, bf16[128,512]{1,0:T(8,128)(2,1)S(1)} %collective-permute-done.14.refs_3_, bf16[128,512]{1,0:T(8,128)(2,1)S(1)} %collective-permute-done.15.refs_4_, ...), custom_call_target="tpu_custom_call" | custom-call | tf_op jit(solution)/shard_map/pallas_call | solution.py:740
  129.0 2.9 %shard_map.385 = (f32[128]{0:T(128)}, f32[128]{0:T(128)}, f32[128]{0:T(128)}, f32[128]{0:T(128)}, f32[128]{0:T(128)}, /*index=5*/f32[128]{0:T(128)}, f32[128,512...) custom-call(f32[128,3072]{1,0:T(8,128)} %get-tuple-element.193.refs_, ...), custom_call_target="tpu_custom_call", output_to_operand_aliasing={{7}: (0, {})} | custom-call | tf_op jit(solution)/shard_map/pallas_call | solution.py:740
  (92 shorter events, 19.2 us)
Async XLA Ops:
  1.7 12.1 %collective-permute-start.2 = (bf16[128,1024]{1,0:T(8,128)(2,1)S(1)}, bf16[128,1024]{1,0:T(8,128)(2,1)S(1)}, u32[]{:S(2)}, u32[]{:S(2)}) collective-permute-start(bf16[128,1024]{1,0:T(8,128)(2,1)S(1)} %pad_maximum_fusion.2.refs_1_.refs_6_.refs_0_.refs_4_), channel_id=1, source_target_pairs={{0,6},{1,7},{2,4},{3,5},{4,2},{5,3},{6,0},{7,1},{8,14},{9,15},{10,... | collective-permute-start | bytes 786440 | tf_op jit(solution)/shard_map/ppermute | solution.py:1802
  5.6 11.9 %collective-permute-start.1 = (bf16[128,1024]{1,0:T(8,128)(2,1)S(1)}, bf16[128,1024]{1,0:T(8,128)(2,1)S(1)}, u32[]{:S(2)}, u32[]{:S(2)}) collective-permute-start(bf16[128,1024]{1,0:T(8,128)(2,1)S(1)} %pad_maximum_fusion.2.refs_1_.refs_6_.refs_0_.refs_4_), channel_id=1, source_target_pairs={{0,4},{1,5},{2,6},{3,7},{4,0},{5,1},{6,2},{7,3},{8,12},{9,13},{10,... | collective-permute-start | bytes 786440 | tf_op jit(solution)/shard_map/ppermute | solution.py:1802
  6.1 11.7 %collective-permute-start = (bf16[128,1024]{1,0:T(8,128)(2,1)S(1)}, bf16[128,1024]{1,0:T(8,128)(2,1)S(1)}, u32[]{:S(2)}, u32[]{:S(2)}) collective-permute-start(bf16[128,1024]{1,0:T(8,128)(2,1)S(1)} %pad_maximum_fusion.2.refs_1_.refs_6_.refs_0_.refs_4_), channel_id=1, source_target_pairs={{0,2},{1,3},{2,0},{3,1},{4,6},{5,7},{6,4},{7,5},{8,10},{9,11},{10,... | collective-permute-start | bytes 786440 | tf_op jit(solution)/shard_map/ppermute | solution.py:1802
  17.9 1.9 %collective-permute-start.4 = (bf16[128,1024]{1,0:T(8,128)(2,1)S(1)}, bf16[128,1024]{1,0:T(8,128)(2,1)S(1)}, u32[]{:S(2)}, u32[]{:S(2)}) collective-permute-start(bf16[128,1024]{1,0:T(8,128)(2,1)S(1)} %collective-permute-done.refs_3_.refs_8_.refs_2_.refs_6_), channel_id=1, source_target_pairs={{0,1},{1,0},{2,3},{3,2},{4,5},{5,4},{6,7},{7,6},{8,9},{9,8},{10,11... | collective-permute-start | bytes 786440 | tf_op jit(solution)/shard_map/ppermute | solution.py:1802
  18.4 1.8 %collective-permute-start.5 = (bf16[128,1024]{1,0:T(8,128)(2,1)S(1)}, bf16[128,1024]{1,0:T(8,128)(2,1)S(1)}, u32[]{:S(2)}, u32[]{:S(2)}) collective-permute-start(bf16[128,1024]{1,0:T(8,128)(2,1)S(1)} %collective-permute-done.1.refs_5_.refs_10_.refs_4_.refs_8_), channel_id=1, source_target_pairs={{0,1},{1,0},{2,3},{3,2},{4,5},{5,4},{6,7},{7,6},{8,9},{9,8},{10,11... | collective-permute-start | bytes 786440 | tf_op jit(solution)/shard_map/ppermute | solution.py:1802
  18.4 2.1 %collective-permute-start.6 = (bf16[128,1024]{1,0:T(8,128)(2,1)S(1)}, bf16[128,1024]{1,0:T(8,128)(2,1)S(1)}, u32[]{:S(2)}, u32[]{:S(2)}) collective-permute-start(bf16[128,1024]{1,0:T(8,128)(2,1)S(1)} %collective-permute-done.2.refs_7_.refs_12_.refs_6_.refs_10_), channel_id=1, source_target_pairs={{0,1},{1,0},{2,3},{3,2},{4,5},{5,4},{6,7},{7,6},{8,9},{9,8},{10,11... | collective-permute-start | bytes 786440 | tf_op jit(solution)/shard_map/ppermute | solution.py:1802
  50.6 16.5 %all-to-all-start = ((bf16[8,144,256]{2,1,0:T(8,128)(2,1)}), bf16[8,144,256]{2,1,0:T(8,128)(2,1)S(1)}, u32[]{:S(2)}, u32[]{:S(2)}) async-start(bf16[8,144,256]{2,1,0:T(8,128)(2,1)} %get-tuple-element.134), calls=%async_computation | async-start | bytes 1179648 | tf_op jit(solution)/shard_map/all_to_all | solution.py:1986
  71.7 17.2 %all-to-all-start.1 = ((bf16[8,256,128]{2,1,0:T(8,128)(2,1)}), bf16[8,256,128]{2,1,0:T(8,128)(2,1)S(1)}, u32[]{:S(2)}, u32[]{:S(2)}) async-start(bf16[8,256,128]{2,1,0:T(8,128)(2,1)} %copy-done.6), calls=%async_computation.1 | async-start | bytes 1048576 | tf_op jit(solution)/shard_map/all_to_all | solution.py:2053
  75.6 19.5 %collective-permute-start.7 = (bf16[640,128]{1,0:T(8,128)(2,1)}, bf16[640,128]{1,0:T(8,128)(2,1)S(1)}, u32[]{:S(2)}, u32[]{:S(2)}) collective-permute-start(bf16[640,128]{1,0:T(8,128)(2,1)} %get-tuple-element.162), channel_id=1, source_target_pairs={{0,8},{8,0},{16,24},{24,16},{1,9},{9,1},{17,25},{25,17},{2,10},{10... | collective-permute-start | bytes 491528 | tf_op jit(solution)/shard_map/ppermute | solution.py:1802
  77.2 17.9 %collective-permute-start.8 = (bf16[640,128]{1,0:T(8,128)(2,1)}, bf16[640,128]{1,0:T(8,128)(2,1)S(1)}, u32[]{:S(2)}, u32[]{:S(2)}) collective-permute-start(bf16[640,128]{1,0:T(8,128)(2,1)} %get-tuple-element.163), channel_id=1, source_target_pairs={{0,16},{8,24},{16,0},{24,8},{1,17},{9,25},{17,1},{25,9},{2,18},{10... | collective-permute-start | bytes 491528 | tf_op jit(solution)/shard_map/ppermute | solution.py:1802
  79.8 15.4 %collective-permute-start.9 = (bf16[640,128]{1,0:T(8,128)(2,1)S(1)}, bf16[640,128]{1,0:T(8,128)(2,1)S(1)}, u32[]{:S(2)}, u32[]{:S(2)}) collective-permute-start(bf16[640,128]{1,0:T(8,128)(2,1)S(1)} %copy-done.21), channel_id=1, source_target_pairs={{0,24},{8,16},{16,8},{24,0},{1,25},{9,17},{17,9},{25,1},{2,26},{10... | collective-permute-start | bytes 491528 | tf_op jit(solution)/shard_map/ppermute | solution.py:1802
  95.1 19.9 %all-to-all-start.2 = ((bf16[4,448,128]{2,1,0:T(8,128)(2,1)}), bf16[4,448,128]{2,1,0:T(8,128)(2,1)S(1)}, u32[]{:S(2)}, u32[]{:S(2)}) async-start(bf16[4,448,128]{2,1,0:T(8,128)(2,1)} %shard_map.379), calls=%async_computation.2 | async-start | bytes 917504 | tf_op jit(solution)/shard_map/all_to_all | solution.py:2096
  99.6 4.6 %collective-permute-start.13 = (bf16[4,128,512]{2,1,0:T(8,128)(2,1)S(1)}, bf16[4,128,512]{2,1,0:T(8,128)(2,1)S(1)}, u32[]{:S(2)}, u32[]{:S(2)}) collective-permute-start(bf16[4,128,512]{2,1,0:T(8,128)(2,1)S(1)} %copy-done.20), channel_id=1, source_target_pairs={{0,1},{1,0},{2,3},{3,2},{4,5},{5,4},{6,7},{7,6},{8,9},{9,8},{10,11... | collective-permute-start | bytes 1572872 | tf_op jit(solution)/shard_map/ppermute | solution.py:1802
  100.6 8.1 %collective-permute-start.12 = (bf16[640,128]{1,0:T(8,128)(2,1)S(1)}, bf16[640,128]{1,0:T(8,128)(2,1)S(1)}, u32[]{:S(2)}, u32[]{:S(2)}) collective-permute-start(bf16[640,128]{1,0:T(8,128)(2,1)S(1)} %shard_map.380), channel_id=1, source_target_pairs={{0,6},{1,7},{2,4},{3,5},{4,2},{5,3},{6,0},{7,1},{8,14},{9,15},{10,... | collective-permute-start | bytes 491528 | tf_op jit(solution)/shard_map/ppermute | solution.py:1802
  103.6 8.4 %collective-permute-start.11 = (bf16[640,128]{1,0:T(8,128)(2,1)S(1)}, bf16[640,128]{1,0:T(8,128)(2,1)S(1)}, u32[]{:S(2)}, u32[]{:S(2)}) collective-permute-start(bf16[640,128]{1,0:T(8,128)(2,1)S(1)} %shard_map.380), channel_id=1, source_target_pairs={{0,4},{1,5},{2,6},{3,7},{4,0},{5,1},{6,2},{7,3},{8,12},{9,13},{10,... | collective-permute-start | bytes 491528 | tf_op jit(solution)/shard_map/ppermute | solution.py:1802
  104.1 8.5 %collective-permute-start.10 = (bf16[640,128]{1,0:T(8,128)(2,1)S(1)}, bf16[640,128]{1,0:T(8,128)(2,1)S(1)}, u32[]{:S(2)}, u32[]{:S(2)}) collective-permute-start(bf16[640,128]{1,0:T(8,128)(2,1)S(1)} %shard_map.380), channel_id=1, source_target_pairs={{0,2},{1,3},{2,0},{3,1},{4,6},{5,7},{6,4},{7,5},{8,10},{9,11},{10,... | collective-permute-start | bytes 491528 | tf_op jit(solution)/shard_map/ppermute | solution.py:1802
  105.2 9.9 %collective-permute-start.14 = (bf16[128,512]{1,0:T(8,128)(2,1)S(1)}, bf16[128,512]{1,0:T(8,128)(2,1)S(1)}, u32[]{:S(2)}, u32[]{:S(2)}) collective-permute-start(bf16[128,512]{1,0:T(8,128)(2,1)S(1)} %get-tuple-element.172), channel_id=1, source_target_pairs={{0,2},{1,3},{2,0},{3,1},{4,6},{5,7},{6,4},{7,5},{8,10},{9,11},{10,... | collective-permute-start | bytes 393224 | tf_op jit(solution)/shard_map/ppermute | solution.py:1802
  107.2 7.9 %collective-permute-start.15 = (bf16[128,512]{1,0:T(8,128)(2,1)S(1)}, bf16[128,512]{1,0:T(8,128)(2,1)S(1)}, u32[]{:S(2)}, u32[]{:S(2)}) collective-permute-start(bf16[128,512]{1,0:T(8,128)(2,1)S(1)} %get-tuple-element.173), channel_id=1, source_target_pairs={{0,4},{1,5},{2,6},{3,7},{4,0},{5,1},{6,2},{7,3},{8,12},{9,13},{10,... | collective-permute-start | bytes 393224 | tf_op jit(solution)/shard_map/ppermute | solution.py:1802
  115.2 6.1 %collective-permute-start.19 = (bf16[4,640,128]{2,1,0:T(8,128)(2,1)S(1)}, bf16[4,640,128]{2,1,0:T(8,128)(2,1)S(1)}, u32[]{:S(2)}, u32[]{:S(2)}) collective-permute-start(bf16[4,640,128]{2,1,0:T(8,128)(2,1)S(1)} %pad_maximum_fusion.refs_0_), channel_id=1, source_target_pairs={{0,1},{1,0},{2,3},{3,2},{4,5},{5,4},{6,7},{7,6},{8,9},{9,8},{10,11... | collective-permute-start | bytes 1966088 | tf_op jit(solution)/shard_map/ppermute | solution.py:1802
  115.3 9.4 %collective-permute-start.20 = (bf16[128,512]{1,0:T(8,128)(2,1)S(1)}, bf16[128,512]{1,0:T(8,128)(2,1)S(1)}, u32[]{:S(2)}, u32[]{:S(2)}) collective-permute-start(bf16[128,512]{1,0:T(8,128)(2,1)S(1)} %get-tuple-element.183), channel_id=1, source_target_pairs={{0,6},{1,7},{2,4},{3,5},{4,2},{5,3},{6,0},{7,1},{8,14},{9,15},{10,... | collective-permute-start | bytes 393224 | tf_op jit(solution)/shard_map/ppermute | solution.py:1802
  117.7 7.3 %collective-permute-start.18 = (bf16[448,128]{1,0:T(8,128)(2,1)S(1)}, bf16[448,128]{1,0:T(8,128)(2,1)S(1)}, u32[]{:S(2)}, u32[]{:S(2)}) collective-permute-start(bf16[448,128]{1,0:T(8,128)(2,1)S(1)} %shard_map.382), channel_id=1, source_target_pairs={{0,6},{1,7},{2,4},{3,5},{4,2},{5,3},{6,0},{7,1},{8,14},{9,15},{10,... | collective-permute-start | bytes 344072 | tf_op jit(solution)/shard_map/ppermute | solution.py:1802
  119.2 7.7 %collective-permute-start.17 = (bf16[448,128]{1,0:T(8,128)(2,1)S(1)}, bf16[448,128]{1,0:T(8,128)(2,1)S(1)}, u32[]{:S(2)}, u32[]{:S(2)}) collective-permute-start(bf16[448,128]{1,0:T(8,128)(2,1)S(1)} %shard_map.382), channel_id=1, source_target_pairs={{0,4},{1,5},{2,6},{3,7},{4,0},{5,1},{6,2},{7,3},{8,12},{9,13},{10,... | collective-permute-start | bytes 344072 | tf_op jit(solution)/shard_map/ppermute | solution.py:1802
  120.7 6.3 %collective-permute-start.16 = (bf16[448,128]{1,0:T(8,128)(2,1)S(1)}, bf16[448,128]{1,0:T(8,128)(2,1)S(1)}, u32[]{:S(2)}, u32[]{:S(2)}) collective-permute-start(bf16[448,128]{1,0:T(8,128)(2,1)S(1)} %shard_map.382), channel_id=1, source_target_pairs={{0,2},{1,3},{2,0},{3,1},{4,6},{5,7},{6,4},{7,5},{8,10},{9,11},{10,... | collective-permute-start | bytes 344072 | tf_op jit(solution)/shard_map/ppermute | solution.py:1802
  127.1 2.0 %collective-permute-start.21 = (bf16[4,448,128]{2,1,0:T(8,128)(2,1)S(1)}, bf16[4,448,128]{2,1,0:T(8,128)(2,1)S(1)}, u32[]{:S(2)}, u32[]{:S(2)}) collective-permute-start(bf16[4,448,128]{2,1,0:T(8,128)(2,1)S(1)} %pad_maximum_fusion.1.refs_1_), channel_id=1, source_target_pairs={{0,1},{1,0},{2,3},{3,2},{4,5},{5,4},{6,7},{7,6},{8,9},{9,8},{10,11... | collective-permute-start | bytes 1376264 | tf_op jit(solution)/shard_map/ppermute | solution.py:1802
  (23 other events, 155.9 us)
